TPU v7x, 32 devices: a whole 2x2x4 slice. The times are simulated.
32 devices in a mesh: dp: 8 (over y, x, core), tensor: 4 (over z).
Axes of the slice: x: 2, y: 2, z: 4, core: 2. Of those that a mesh axis runs over, the one named last changes fastest.
Arguments:
- x_tokens: bfloat16 [512, 8192], P('dp', 'tensor'), may hold values from -6 to 6
- sign_bits: int32 [8192], P('tensor'), may hold values from 0 to 1
- weight: bfloat16 [8192, 28672], P('tensor', 'dp'), may hold values from -0.0625 to 0.0625
- upstream: bfloat16 [512, 28672], P('tensor', 'dp'), may hold values from -0.25 to 0.25
Outputs:
- projected: bfloat16 [512, 28672], P('tensor', 'dp')
- weight_grad: float32 [8192, 28672], P('tensor', 'dp')
All inputs are finite; a program needn't handle non-finite values.
Results may differ from a plain program's by a relative error of at most 0.028.
Values may be sent and summed in bfloat16 or wider, within the bound.
No kernel may reach another device: no remote copies, remote signals or barrier semaphores. Data moves between devices by JAX's collectives and lax.ppermute only.
A program may use at most 128 MiB of HBM per device.

v0:
```python
import functools
import math

import jax
import jax.numpy as jnp
from jax import lax
from jax.experimental import pallas as pl
from jax.experimental.pallas import tpu as pltpu
from jax.sharding import PartitionSpec as P

MIB = 1 << 20
VMEM = pl.BlockSpec(memory_space=pltpu.VMEM)


def hadamard(order):
    row_ids = jnp.arange(order, dtype=jnp.int32)[:, None]
    col_ids = jnp.arange(order, dtype=jnp.int32)[None, :]
    common = row_ids & col_ids
    parity = jnp.zeros((order, order), jnp.int32)
    for section_bit in range(max(order.bit_length() - 1, 0)):
        parity = parity + (common >> section_bit & 1)
    return (1 - 2 * (parity % 2)).astype(jnp.bfloat16)


def swap(block, axis, mask):
    count = lax.axis_size(axis)
    return lax.ppermute(
        block, axis, [(i, i ^ mask) for i in range(count) if i ^ mask < count]
    )


def plain(x_tokens, sign_bits, weight, upstream):
    panel_width = x_tokens.shape[1]
    groups = lax.axis_size("tensor")
    factor = 1.0 / math.sqrt(panel_width * groups)
    column_sign = (1 - 2 * sign_bits).astype(jnp.bfloat16)
    current = jnp.dot(
        x_tokens * column_sign[None, :],
        hadamard(panel_width),
        preferred_element_type=jnp.float32,
    )
    position = lax.axis_index("tensor")
    for section_bit in range(groups.bit_length() - 1):
        partner = swap(current.astype(jnp.bfloat16), "tensor", 1 << section_bit).astype(
            current.dtype
        )
        upper_half = position >> section_bit & 1 == 1
        current = jnp.where(upper_half, partner - current, current + partner)
    quantized = (current * factor).astype(jnp.bfloat16)
    gathered = lax.all_gather(quantized, "dp", axis=0, tiled=True)
    projected = lax.psum_scatter(
        jnp.dot(gathered, weight, preferred_element_type=jnp.float32).astype(jnp.bfloat16),
        "tensor",
        scatter_dimension=0,
        tiled=True,
    )
    weight_grad = lax.dot_general(
        gathered,
        lax.all_gather(upstream, "tensor", axis=0, tiled=True),
        (((0,), (0,)), ((), ())),
        preferred_element_type=jnp.float32,
    )
    return (projected, weight_grad)


def parity_sign(bits):
    return (1 - 2 * ((bits ^ bits >> 1) & 1)).astype(jnp.float32)


def butterfly(parts):
    stride = 1
    parts = list(parts)
    while stride < len(parts):
        for low in range(len(parts)):
            if not low & stride:
                a, b = parts[low], parts[low | stride]
                parts[low], parts[low | stride] = a + b, a - b
        stride *= 2
    return parts


def whole(shape):
    return pl.BlockSpec(shape, lambda n: (0,) * len(shape))


def tile_of(width, first=0):
    return next((t for t in (512, 256, 128) if width % t == 0 and first % t == 0), width)


def after(arrays, *earlier):
    arrays = list(arrays)
    return list(lax.optimization_barrier(tuple(arrays) + tuple(earlier))[: len(arrays)])


def sign_kernel(x_ref, bits_ref, *outs):
    z = lax.axis_index("tensor")
    rows = outs[0].shape[0]
    sign = (1 - 2 * bits_ref[...]).astype(jnp.float32)
    for m, out in enumerate(outs):
        first = pl.multiple_of((z ^ m) * rows, rows)
        out[...] = (x_ref[pl.ds(first, rows), :].astype(jnp.float32) * sign).astype(out.dtype)


def signed_pieces(x, sign_bits, groups):
    rows, width = x.shape
    part = rows // groups
    return pl.pallas_call(
        sign_kernel,
        out_shape=[jax.ShapeDtypeStruct((part, width), jnp.bfloat16)] * groups,
        in_specs=[VMEM] * 2,
        out_specs=[VMEM] * groups,
        compiler_params=pltpu.CompilerParams(vmem_limit_bytes=8 * MIB),
        name="signed_pieces",
    )(x, sign_bits.reshape(1, width))


def rotate_kernel(groups, order, factor, h_ref, *refs):
    pieces, outs = refs[:groups], refs[groups:]
    z = lax.axis_index("tensor")
    rows, width = pieces[0].shape
    chunks = width // order
    stacked = jnp.concatenate(
        [piece[:, j * order : (j + 1) * order] for piece in pieces for j in range(chunks)], axis=0
    )
    product = jnp.dot(stacked, h_ref[...], preferred_element_type=jnp.float32)
    rotated = []
    for i in range(groups):
        sign = parity_sign(z & i)
        rotated.append(
            butterfly(
                [
                    product[(i * chunks + j) * rows : (i * chunks + j + 1) * rows] * sign
                    for j in range(chunks)
                ]
            )
        )
    for j in range(chunks):
        panel = butterfly([r[j] for r in rotated])
        for m in range(groups):
            scale = parity_sign((z ^ m) & z) * factor
            outs[m][:, j * order : (j + 1) * order] = (panel[m] * scale).astype(jnp.bfloat16)


def rotate(pieces):
    groups = len(pieces)
    rows, width = pieces[0].shape
    order = min(256, width)
    return pl.pallas_call(
        functools.partial(rotate_kernel, groups, order, 1.0 / math.sqrt(width * groups)),
        out_shape=[jax.ShapeDtypeStruct((rows, width), jnp.bfloat16)] * groups,
        in_specs=[VMEM] * (1 + groups),
        out_specs=[VMEM] * groups,
        compiler_params=pltpu.CompilerParams(vmem_limit_bytes=8 * MIB),
        name="rotate",
    )(hadamard(order), *pieces)


def gather_rows(own, d):
    x, y, core = swap(own, "dp", 2), swap(own, "dp", 4), swap(own, "dp", 1)
    x, y = after([x, y])
    through = jnp.where(d & 1 == 0, x, y)
    diagonal = lax.ppermute(
        through, "dp", [(i, i ^ (4 if i & 1 == 0 else 2)) for i in range(8)]
    )
    return [
        own,
        core,
        x,
        swap(x, "dp", 1),
        y,
        swap(y, "dp", 1),
        diagonal,
        swap(diagonal, "dp", 1),
    ]


def is_outer(z):
    return 1 - ((z ^ z >> 1) & 1)


def slot(m, z):
    return m ^ (m >> 1 & is_outer(z))


def first_kernel(*refs):
    pieces, (w_ref, q_ref, *out_refs, sems) = refs[:8], refs[8:]
    rows = pieces[0].shape[0]

    @pl.when(pl.program_id(0) == 0)
    def _():
        z, d = lax.axis_index("tensor"), lax.axis_index("dp")
        copies = []
        for mask, piece in enumerate(pieces):
            start = slot(((d ^ mask) >> 1) ^ z, z) * (2 * rows) + ((d ^ mask) & 1) * rows
            copies.append(
                pltpu.make_async_copy(
                    piece, q_ref.at[pl.ds(pl.multiple_of(start, rows), rows), :], sems.at[mask]
                )
            )
        for copy in copies:
            copy.start()
        for copy in copies:
            copy.wait()

    project_kernel(q_ref, w_ref, *out_refs)


def project_kernel(q_ref, w_ref, *out_refs):
    product = jnp.dot(q_ref[...], w_ref[...], preferred_element_type=jnp.float32)
    first = 0
    for out_ref in out_refs:
        rows = out_ref.shape[0]
        out_ref[...] = product[first : first + rows].astype(out_ref.dtype)
        first += rows


def project_first(pieces, weight, width, blocks):
    depth = weight.shape[0]
    tokens = sum(blocks)
    tile = tile_of(width)
    q, *products = pl.pallas_call(
        first_kernel,
        out_shape=[
            jax.ShapeDtypeStruct((tokens, depth), jnp.bfloat16),
            *[jax.ShapeDtypeStruct((block, width), jnp.bfloat16) for block in blocks],
        ],
        grid=(width // tile,),
        in_specs=[pl.BlockSpec(memory_space=pl.ANY)] * len(pieces)
        + [pl.BlockSpec((depth, tile), lambda n: (0, n))],
        out_specs=[whole((tokens, depth))]
        + [pl.BlockSpec((block, tile), lambda n: (0, n)) for block in blocks],
        scratch_shapes=[pltpu.SemaphoreType.DMA((len(pieces),))],
        compiler_params=pltpu.CompilerParams(vmem_limit_bytes=48 * MIB),
        cost_estimate=pl.CostEstimate(flops=1, bytes_accessed=1, transcendentals=0),
        name="project_first",
    )(*pieces, weight)
    return q, products


def project(q, weight, first, width, blocks):
    tile = tile_of(width, first)
    tokens, depth = q.shape
    return pl.pallas_call(
        project_kernel,
        out_shape=[jax.ShapeDtypeStruct((block, width), jnp.bfloat16) for block in blocks],
        grid=(width // tile,),
        in_specs=[
            whole((tokens, depth)),
            pl.BlockSpec((depth, tile), lambda n: (0, n + first // tile)),
        ],
        out_specs=[pl.BlockSpec((block, tile), lambda n: (0, n)) for block in blocks],
        compiler_params=pltpu.CompilerParams(vmem_limit_bytes=48 * MIB),
        cost_estimate=pl.CostEstimate(
            flops=2 * tokens * depth * width,
            bytes_accessed=2 * (tokens * depth + depth * width + tokens * width),
            transcendentals=0,
        ),
        name="project",
    )(q, weight)


def transpose_kernel(q_ref, out_ref):
    out_ref[...] = q_ref[...].T


def transposed(q):
    tokens, depth = q.shape
    return pl.pallas_call(
        transpose_kernel,
        out_shape=jax.ShapeDtypeStruct((depth, tokens), jnp.bfloat16),
        in_specs=[VMEM],
        out_specs=VMEM,
        compiler_params=pltpu.CompilerParams(vmem_limit_bytes=16 * MIB),
        name="transposed",
    )(q)


def grad_kernel(tile, start, q_t, own_ref, e1, o1, o2, e2, e3, *refs):
    out_ref, up_all, sems = refs[-3:]
    z = lax.axis_index("tensor")
    rows, width = own_ref.shape[0], up_all.shape[1]

    @pl.when(pl.program_id(0) == 0)
    def _():
        def copy(source, m):
            return pltpu.make_async_copy(
                source.at[:, start : start + width],
                up_all.at[m * rows : (m + 1) * rows, :],
                sems.at[m],
            )

        copy(own_ref, 0).start()
        copy(e1, 1).start()

        @pl.when(is_outer(z) == 0)
        def _():
            copy(o2, 2).start()
            copy(o1, 3).start()

        @pl.when(is_outer(z) == 1)
        def _():
            copy(e3, 2).start()
            copy(e2, 3).start()

        for m in range(4):
            copy(own_ref, m).wait()

    first = pl.multiple_of(pl.program_id(0) * tile, tile)
    out_ref[...] = jnp.dot(
        q_t[...], up_all[:, pl.ds(first, tile)], preferred_element_type=jnp.float32
    )


def weight_gradient(q_t, own, moved, start, width, done=None):
    depth, tokens = q_t.shape
    hidden = own.shape[1]
    tile = tile_of(width, start)
    before = [] if done is None else [done]
    anywhere = pl.BlockSpec(memory_space=pl.ANY)
    return pl.pallas_call(
        functools.partial(grad_kernel, tile, start),
        out_shape=jax.ShapeDtypeStruct((depth, hidden), jnp.float32),
        grid=(width // tile,),
        in_specs=[whole((depth, tokens))] + [anywhere] * (6 + len(before)),
        out_specs=pl.BlockSpec((depth, tile), lambda n: (0, n + start // tile)),
        input_output_aliases={7: 0} if before else {},
        scratch_shapes=[
            pltpu.VMEM((tokens, width), jnp.bfloat16),
            pltpu.SemaphoreType.DMA((4,)),
        ],
        compiler_params=pltpu.CompilerParams(vmem_limit_bytes=28 * MIB),
        cost_estimate=pl.CostEstimate(
            flops=5 * tokens * depth * width,
            bytes_accessed=2 * tokens * (depth + width) + 4 * depth * width,
            transcendentals=0,
        ),
        name="weight_gradient",
    )(q_t, own, *moved, *before)


def total(*blocks):
    return sum(b.astype(jnp.float32) for b in blocks).astype(jnp.bfloat16)


def move(block, *pairs):
    return lax.ppermute(block, "tensor", pairs)


INWARD = ((0, 1), (3, 2))
MIDDLE = ((1, 2), (2, 1))
OUTWARD = ((1, 0), (2, 3))


def lined(x_tokens, sign_bits, weight, upstream):
    groups = lax.axis_size("tensor")
    z = lax.axis_index("tensor")
    d = lax.axis_index("dp")
    rows = x_tokens.shape[0]
    hidden = weight.shape[1]

    pieces = list(signed_pieces(x_tokens, sign_bits, groups))
    for m in (3, 2, 1):
        pieces[m] = swap(pieces[m], "tensor", m)
    turned = list(rotate(pieces))
    (up,) = after([upstream], turned[0])
    for m in (3, 2, 1):
        turned[m] = swap(turned[m], "tensor", m)
    own = jnp.concatenate(
        [lax.select_n(z, *[turned[g ^ k] for k in range(groups)]) for g in range(groups)]
    )

    e1 = swap(up, "tensor", 1)
    o1 = move(up, *MIDDLE)

    gathered = gather_rows(own, d)
    cut = 3 * hidden // 7 // 512 * 512
    block = rows * len(gathered) // groups
    q, *first = project_first(gathered, weight, cut, (block, block, 2 * block))
    own_a, pair_a, beyond_a = first[0]
    q, e1, o1 = after([q, e1, o1])
    o2 = move(e1, *MIDDLE)
    e2 = move(o1, *OUTWARD)
    own_b, pair_b, far_b, near_b = project(q, weight, cut, hidden - cut, (block,) * 4)

    inward_a = move(beyond_a, *INWARD)
    inward_far = move(far_b, *INWARD)
    (inward_near,) = after([near_b], inward_a)
    inward_near = move(inward_near, *INWARD)
    across_a = move(total(beyond_a, inward_a), *MIDDLE)
    o2, e2 = after([o2, e2], inward_a)
    e3 = move(o2, *OUTWARD)
    inward_far, o2, e2 = after([inward_far, o2, e2])
    across_far = move(total(far_b, inward_far), *MIDDLE)
    across_a, e3 = after([across_a, e3])
    out_a = swap(total(pair_a, across_a[:block]), "tensor", 1)

    (late,) = after([q], inward_far)
    q_t = transposed(late)
    moved = (e1, o1, o2, e2, e3)
    some = hidden // 2 // 512 * 512
    (late,) = after([q_t], across_a, inward_near)
    grad = weight_gradient(late, upstream, moved, 0, some)

    across_near = move(total(near_b, inward_near), *MIDDLE)
    across_far, grad, out_a = after([across_far, grad, out_a])
    out_b = swap(total(pair_b, across_far), "tensor", 1)
    (late,) = after([q_t], across_far)
    weight_grad = weight_gradient(late, upstream, moved, some, hidden - some, grad)
    projected = jnp.concatenate(
        [total(own_a, out_a, across_a[block:]), total(own_b, out_b, across_near)], axis=1
    )
    return (projected, weight_grad)


def per_device(x_tokens, sign_bits, weight, upstream):
    rows, width = x_tokens.shape
    hidden = weight.shape[1]
    fits = rows % 64 == 0 and width % 256 == 0 and hidden % 512 == 0 and hidden >= 1536
    if (lax.axis_size("dp"), lax.axis_size("tensor")) == (8, 4) and fits:
        return lined(x_tokens, sign_bits, weight, upstream)
    return plain(x_tokens, sign_bits, weight, upstream)


def solution(mesh):
    in_specs = (P("dp", "tensor"), P("tensor"), P("tensor", "dp"), P("tensor", "dp"))
    out_specs = (P("tensor", "dp"), P("tensor", "dp"))
    return jax.shard_map(
        per_device, mesh=mesh, in_specs=in_specs, out_specs=out_specs, check_vma=False
    )
```

profile of v0, /device:TPU:0, one launch (start us, length us, event | category | flops | bytes accessed | tf_op | source)
XLA Modules:
  0.0 113.6 jit_solution(12215244647545891964)
XLA Ops:
  0.6 1.0 copy-done.1
  1.7 0.7 copy-done.2
  2.4 0.1 signed_pieces.1
  2.4 3.1 %collective-permute-start = (bf16[16,2048]{1,0:T(8,128)(2,1)S(1)}, bf16[16,2048]{1,0:T(8,128)(2,1)S(1)}, u32[]{:S(2)}, u32[]{:S(2)}) collective-permute-start(bf16[16,2048]{1,0:T(8,128)(2,1)S(1)} %get-tuple-element.39), channel_id=1, source_target_pairs={{0,1},{1,0},{2,3},{3,2},{4,5},{5,4},{6,7},{7,6},{8,9},{9,8},{10,11... | collective-permute-start | bytes 196616 | tf_op jit(solution)/shard_map/ppermute | solution.py:27
  5.5 2.6 %collective-permute-start.1 = (bf16[16,2048]{1,0:T(8,128)(2,1)S(1)}, bf16[16,2048]{1,0:T(8,128)(2,1)S(1)}, u32[]{:S(2)}, u32[]{:S(2)}) collective-permute-start(bf16[16,2048]{1,0:T(8,128)(2,1)S(1)} %get-tuple-element.40), channel_id=1, source_target_pairs={{0,2},{1,3},{2,0},{3,1},{4,6},{5,7},{6,4},{7,5},{8,10},{9,11},{10,... | collective-permute-start | bytes 196616 | tf_op jit(solution)/shard_map/ppermute | solution.py:27
  8.1 0.0 collective-permute-start.2
  8.1 0.3 fusion.3.h_ref
  8.4 0.0 collective-permute-done.refs_1_
  8.5 4.3 %collective-permute-done.1.refs_2_ = bf16[16,2048]{1,0:T(8,128)(2,1)S(1)} collective-permute-done((bf16[16,2048]{1,0:T(8,128)(2,1)S(1)}, bf16[16,2048]{1,0:T(8,128)(2,1)S(1)}, u32[]{:S(2)}, u32[]{:S(2)}) %collective-permute-start.1) | collective-permute-done | bytes 65568 | tf_op jit(solution)/shard_map/ppermute | solution.py:27
  12.8 1.4 %collective-permute-done.2.refs_3_ = bf16[16,2048]{1,0:T(8,128)(2,1)S(1)} collective-permute-done((bf16[16,2048]{1,0:T(8,128)(2,1)S(1)}, bf16[16,2048]{1,0:T(8,128)(2,1)S(1)}, u32[]{:S(2)}, u32[]{:S(2)}) %collective-permute-start.2) | collective-permute-done | bytes 65568 | tf_op jit(solution)/shard_map/ppermute | solution.py:27
  14.2 0.3 rotate.1
  14.5 1.6 %collective-permute-start.4 = (bf16[16,2048]{1,0:T(8,128)(2,1)S(1)}, bf16[16,2048]{1,0:T(8,128)(2,1)S(1)}, u32[]{:S(2)}, u32[]{:S(2)}) collective-permute-start(bf16[16,2048]{1,0:T(8,128)(2,1)S(1)} %get-tuple-element.44), channel_id=1, source_target_pairs={{0,2},{1,3},{2,0},{3,1},{4,6},{5,7},{6,4},{7,5},{8,10},{9,11},{10,... | collective-permute-start | bytes 196616 | tf_op jit(solution)/shard_map/ppermute | solution.py:27
  16.1 0.7 collective-permute-start.5
  16.8 1.2 %collective-permute-start.3 = (bf16[16,2048]{1,0:T(8,128)(2,1)S(1)}, bf16[16,2048]{1,0:T(8,128)(2,1)S(1)}, u32[]{:S(2)}, u32[]{:S(2)}) collective-permute-start(bf16[16,2048]{1,0:T(8,128)(2,1)S(1)} %get-tuple-element.43), channel_id=1, source_target_pairs={{0,1},{1,0},{2,3},{3,2},{4,5},{5,4},{6,7},{7,6},{8,9},{9,8},{10,11... | collective-permute-start | bytes 196616 | tf_op jit(solution)/shard_map/ppermute | solution.py:27
  18.0 2.4 %collective-permute-done.4 = bf16[16,2048]{1,0:T(8,128)(2,1)S(1)} collective-permute-done((bf16[16,2048]{1,0:T(8,128)(2,1)S(1)}, bf16[16,2048]{1,0:T(8,128)(2,1)S(1)}, u32[]{:S(2)}, u32[]{:S(2)}) %collective-permute-start.4) | collective-permute-done | bytes 65568 | tf_op jit(solution)/shard_map/ppermute | solution.py:27
  20.5 1.7 %collective-permute-done.5 = bf16[16,2048]{1,0:T(8,128)(2,1)S(1)} collective-permute-done((bf16[16,2048]{1,0:T(8,128)(2,1)S(1)}, bf16[16,2048]{1,0:T(8,128)(2,1)S(1)}, u32[]{:S(2)}, u32[]{:S(2)}) %collective-permute-start.5) | collective-permute-done | bytes 65568 | tf_op jit(solution)/shard_map/ppermute | solution.py:27
  22.2 0.0 collective-permute-done.3
  22.3 1.6 %collective-permute-start.7 = (bf16[64,2048]{1,0:T(8,128)(2,1)S(1)}, bf16[64,2048]{1,0:T(8,128)(2,1)S(1)}, u32[]{:S(2)}, u32[]{:S(2)}) collective-permute-start(bf16[64,2048]{1,0:T(8,128)(2,1)S(1)} %pad_maximum_fusion.1.refs_0_), channel_id=1, source_target_pairs={{0,8},{4,12},{8,0},{12,4},{16,24},{20,28},{24,16},{28,20},{1,9},{5... | collective-permute-start | bytes 786440 | tf_op jit(solution)/shard_map/ppermute | solution.py:27
  23.8 1.5 %collective-permute-start.8 = (bf16[64,2048]{1,0:T(8,128)(2,1)S(1)}, bf16[64,2048]{1,0:T(8,128)(2,1)S(1)}, u32[]{:S(2)}, u32[]{:S(2)}) collective-permute-start(bf16[64,2048]{1,0:T(8,128)(2,1)S(1)} %pad_maximum_fusion.1.refs_0_), channel_id=1, source_target_pairs={{0,16},{4,20},{8,24},{12,28},{16,0},{20,4},{24,8},{28,12},{1,17},{... | collective-permute-start | bytes 786440 | tf_op jit(solution)/shard_map/ppermute | solution.py:27
  25.4 0.1 collective-permute-start.13
  25.5 0.7 collective-permute-start.14
  26.2 0.1 collective-permute-start.6
  26.3 2.5 %collective-permute-done.7.refs_2_ = bf16[64,2048]{1,0:T(8,128)(2,1)S(1)} collective-permute-done((bf16[64,2048]{1,0:T(8,128)(2,1)S(1)}, bf16[64,2048]{1,0:T(8,128)(2,1)S(1)}, u32[]{:S(2)}, u32[]{:S(2)}) %collective-permute-start.7) | collective-permute-done | bytes 262176 | tf_op jit(solution)/shard_map/ppermute | solution.py:27
  28.7 1.5 %collective-permute-done.8.refs_4_ = bf16[64,2048]{1,0:T(8,128)(2,1)S(1)} collective-permute-done((bf16[64,2048]{1,0:T(8,128)(2,1)S(1)}, bf16[64,2048]{1,0:T(8,128)(2,1)S(1)}, u32[]{:S(2)}, u32[]{:S(2)}) %collective-permute-start.8) | collective-permute-done | bytes 262176 | tf_op jit(solution)/shard_map/ppermute | solution.py:27
  30.2 1.6 %collective-permute-start.11 = (bf16[64,2048]{1,0:T(8,128)(2,1)S(1)}, bf16[64,2048]{1,0:T(8,128)(2,1)S(1)}, u32[]{:S(2)}, u32[]{:S(2)}) collective-permute-start(bf16[64,2048]{1,0:T(8,128)(2,1)S(1)} %broadcast_select_fusion), channel_id=1, source_target_pairs={{0,16},{4,12},{8,24},{12,4},{16,0},{20,28},{24,8},{28,20},{1,17},{... | collective-permute-start | bytes 786440 | tf_op jit(solution)/shard_map/ppermute | solution.py:162
  31.8 0.0 collective-permute-start.9
  31.8 0.5 collective-permute-start.10
  32.3 4.3 %collective-permute-done.11.refs_6_ = bf16[64,2048]{1,0:T(8,128)(2,1)S(1)} collective-permute-done((bf16[64,2048]{1,0:T(8,128)(2,1)S(1)}, bf16[64,2048]{1,0:T(8,128)(2,1)S(1)}, u32[]{:S(2)}, u32[]{:S(2)}) %collective-permute-start.11) | collective-permute-done | bytes 262176 | tf_op jit(solution)/shard_map/ppermute | solution.py:162
  36.7 1.5 %collective-permute-done.12.refs_7_ = bf16[64,2048]{1,0:T(8,128)(2,1)S(1)} collective-permute-done((bf16[64,2048]{1,0:T(8,128)(2,1)S(1)}, bf16[64,2048]{1,0:T(8,128)(2,1)S(1)}, u32[]{:S(2)}, u32[]{:S(2)}) %collective-permute-start.12) | collective-permute-done | bytes 262176 | tf_op jit(solution)/shard_map/ppermute | solution.py:27
  38.2 6.0 %project_first.1 = (bf16[512,2048]{1,0:T(8,128)(2,1)S(1)}, bf16[128,1536]{1,0:T(8,128)(2,1)S(1)}, bf16[128,1536]{1,0:T(8,128)(2,1)S(1)}, bf16[256,1536]{1,0:T(8,128)(2,1)S(1)}) custom-call(bf16[64,2048]{1,0:T(8,128)(2,1)S(1)} %pad_maximum_fusion.1.refs_0_, bf16[64,2048]{1,0:T(8,128)(2,1)S(1)} %collective-permute-done.6.refs_1_, ...), custom_call_target="tpu_custom_call" | custom-call | flops 1 | bytes 1 | tf_op jit(solution)/shard_map/project_first/pallas_call | solution.py:221
  44.2 2.3 %collective-permute-start.18 = (bf16[256,1536]{1,0:T(8,128)(2,1)S(1)}, bf16[256,1536]{1,0:T(8,128)(2,1)S(1)}, u32[]{:S(2)}, u32[]{:S(2)}) collective-permute-start(bf16[256,1536]{1,0:T(8,128)(2,1)S(1)} %get-tuple-element.55), channel_id=1, source_target_pairs={{0,1},{3,2},{4,5},{7,6},{8,9},{11,10},{12,13},{15,14},{16,17},{19,... | collective-permute-start | bytes 2359304 | tf_op jit(solution)/shard_map/ppermute | solution.py:346
  46.5 0.0 collective-permute-done.13.e1
  46.5 0.0 collective-permute-done.14.o1
  46.5 0.7 collective-permute-start.16
  47.3 1.3 %collective-permute-start.17 = (bf16[128,3584]{1,0:T(8,128)(2,1)S(1)}, bf16[128,3584]{1,0:T(8,128)(2,1)S(1)}, u32[]{:S(2)}, u32[]{:S(2)}) collective-permute-start(bf16[128,3584]{1,0:T(8,128)(2,1)S(1)} %collective-permute-done.14.o1), channel_id=1, source_target_pairs={{1,0},{2,3},{5,4},{6,7},{9,8},{10,11},{13,12},{14,15},{17,16},{18,... | collective-permute-start | bytes 2752520 | tf_op jit(solution)/shard_map/ppermute | solution.py:346
  48.6 7.1 %project.1 = (bf16[128,2048]{1,0:T(8,128)(2,1)S(1)}, bf16[128,2048]{1,0:T(8,128)(2,1)S(1)}, bf16[128,2048]{1,0:T(8,128)(2,1)S(1)}, bf16[128,2048]{1,0:T(8,128)(2,1)S(1)}) custom-call(bf16[512,2048]{1,0:T(8,128)(2,1)S(1)} %get-tuple-element.59.q_ref, bf16[2048,3584]{1,0:T(8,128)(2,1)} %w_ref.1), custom_call_target="tpu_custom_call" | custom-call | flops 4294967296 | bytes 12582912 | tf_op jit(solution)/shard_map/project/pallas_call | solution.py:243
  55.7 6.3 %collective-permute-start.15 = (bf16[128,2048]{1,0:T(8,128)(2,1)S(1)}, bf16[128,2048]{1,0:T(8,128)(2,1)S(1)}, u32[]{:S(2)}, u32[]{:S(2)}) collective-permute-start(bf16[128,2048]{1,0:T(8,128)(2,1)S(1)} %get-tuple-element.52), channel_id=1, source_target_pairs={{0,1},{3,2},{4,5},{7,6},{8,9},{11,10},{12,13},{15,14},{16,17},{19,... | collective-permute-start | bytes 1572872 | tf_op jit(solution)/shard_map/ppermute | solution.py:346
  62.0 2.3 %collective-permute-done.18 = bf16[256,1536]{1,0:T(8,128)(2,1)S(1)} collective-permute-done((bf16[256,1536]{1,0:T(8,128)(2,1)S(1)}, bf16[256,1536]{1,0:T(8,128)(2,1)S(1)}, u32[]{:S(2)}, u32[]{:S(2)}) %collective-permute-start.18) | collective-permute-done | bytes 786464 | tf_op jit(solution)/shard_map/ppermute | solution.py:346
  64.4 4.4 %collective-permute-start.22 = (bf16[128,2048]{1,0:T(8,128)(2,1)S(1)}, bf16[128,2048]{1,0:T(8,128)(2,1)S(1)}, u32[]{:S(2)}, u32[]{:S(2)}) collective-permute-start(bf16[128,2048]{1,0:T(8,128)(2,1)S(1)} %get-tuple-element.62), channel_id=1, source_target_pairs={{0,1},{3,2},{4,5},{7,6},{8,9},{11,10},{12,13},{15,14},{16,17},{19,... | collective-permute-start | bytes 1572872 | tf_op jit(solution)/shard_map/ppermute | solution.py:346
  68.8 0.2 add_convert_fusion
  69.0 0.7 collective-permute-start.20
  69.7 0.0 collective-permute-done.16.o2
  69.7 1.6 %collective-permute-done.17.e2 = bf16[128,3584]{1,0:T(8,128)(2,1)S(1)} collective-permute-done((bf16[128,3584]{1,0:T(8,128)(2,1)S(1)}, bf16[128,3584]{1,0:T(8,128)(2,1)S(1)}, u32[]{:S(2)}, u32[]{:S(2)}) %collective-permute-start.17) | collective-permute-done | bytes 917536 | tf_op jit(solution)/shard_map/ppermute | solution.py:346
  71.3 1.3 %collective-permute-start.21 = (bf16[128,3584]{1,0:T(8,128)(2,1)S(1)}, bf16[128,3584]{1,0:T(8,128)(2,1)S(1)}, u32[]{:S(2)}, u32[]{:S(2)}) collective-permute-start(bf16[128,3584]{1,0:T(8,128)(2,1)S(1)} %collective-permute-done.16.o2), channel_id=1, source_target_pairs={{1,0},{2,3},{5,4},{6,7},{9,8},{10,11},{13,12},{14,15},{17,16},{18,... | collective-permute-start | bytes 2752520 | tf_op jit(solution)/shard_map/ppermute | solution.py:346
  72.6 3.0 %collective-permute-done.15 = bf16[128,2048]{1,0:T(8,128)(2,1)S(1)} collective-permute-done((bf16[128,2048]{1,0:T(8,128)(2,1)S(1)}, bf16[128,2048]{1,0:T(8,128)(2,1)S(1)}, u32[]{:S(2)}, u32[]{:S(2)}) %collective-permute-start.15) | collective-permute-done | bytes 524320 | tf_op jit(solution)/shard_map/ppermute | solution.py:346
  75.6 0.1 add_convert_fusion.4
  75.7 0.7 collective-permute-start.19
  76.4 0.6 transposed.1.q_t
  77.0 9.0 %collective-permute-done.22 = bf16[128,2048]{1,0:T(8,128)(2,1)S(1)} collective-permute-done((bf16[128,2048]{1,0:T(8,128)(2,1)S(1)}, bf16[128,2048]{1,0:T(8,128)(2,1)S(1)}, u32[]{:S(2)}, u32[]{:S(2)}) %collective-permute-start.22) | collective-permute-done | bytes 524320 | tf_op jit(solution)/shard_map/ppermute | solution.py:346
  86.0 0.1 add_convert_fusion.2
  86.2 0.7 collective-permute-start.25
  86.9 0.0 collective-permute-done.20
  86.9 6.3 %collective-permute-done.21.e3 = bf16[128,3584]{1,0:T(8,128)(2,1)S(1)} collective-permute-done((bf16[128,3584]{1,0:T(8,128)(2,1)S(1)}, bf16[128,3584]{1,0:T(8,128)(2,1)S(1)}, u32[]{:S(2)}, u32[]{:S(2)}) %collective-permute-start.21) | collective-permute-done | bytes 917536 | tf_op jit(solution)/shard_map/ppermute | solution.py:346
  93.2 0.1 add_convert_fusion.6
  93.3 0.1 collective-permute-start.23
  93.4 6.7 %weight_gradient.2.refs_0_ = f32[2048,3584]{1,0:T(8,128)} custom-call(bf16[2048,512]{1,0:T(8,128)(2,1)S(1)} %transposed.1.q_t, bf16[128,3584]{1,0:T(8,128)(2,1)S(1)} %copy-done, bf16[128,3584]{1,0:T(8,128)(2,1)S(1)} %collective-permute-done.13.e1, bf16[128,3584]{1,0:T(8,128)(2,1)S(1)} %collective-permute-done.14.o1, ...), custom_call_target="tpu_custom_call" | custom-call | flops 8053063680 | bytes 16252928 | tf_op jit(solution)/shard_map/weight_gradient/pallas_call | solution.py:320
  100.1 1.5 %collective-permute-done.23 = bf16[128,1536]{1,0:T(8,128)(2,1)S(1)} collective-permute-done((bf16[128,1536]{1,0:T(8,128)(2,1)S(1)}, bf16[128,1536]{1,0:T(8,128)(2,1)S(1)}, u32[]{:S(2)}, u32[]{:S(2)}) %collective-permute-start.23) | collective-permute-done | bytes 393248 | tf_op jit(solution)/shard_map/ppermute | solution.py:27
  101.7 0.1 add_convert_fusion.3
  101.8 0.8 collective-permute-start.24
  102.6 8.1 %weight_gradient.3 = f32[2048,3584]{1,0:T(8,128)} custom-call(bf16[2048,512]{1,0:T(8,128)(2,1)S(1)} %transposed.1.q_t, bf16[128,3584]{1,0:T(8,128)(2,1)S(1)} %copy-done, bf16[128,3584]{1,0:T(8,128)(2,1)S(1)} %collective-permute-done.13.e1, bf16[128,3584]{1,0:T(8,128)(2,1)S(1)} %collective-permute-done.14.o1, ...), custom_call_target="tpu_custom_call", output_to_operand_aliasing={{}: (7, {})} | custom-call | flops 10737418240 | bytes 20971520 | tf_op jit(solution)/shard_map/weight_gradient/pallas_call | solution.py:320
  110.8 0.1 add_convert_fusion.5
  110.9 1.4 %collective-permute-done.24 = bf16[128,2048]{1,0:T(8,128)(2,1)S(1)} collective-permute-done((bf16[128,2048]{1,0:T(8,128)(2,1)S(1)}, bf16[128,2048]{1,0:T(8,128)(2,1)S(1)}, u32[]{:S(2)}, u32[]{:S(2)}) %collective-permute-start.24) | collective-permute-done | bytes 524320 | tf_op jit(solution)/shard_map/ppermute | solution.py:27
  112.4 0.2 add_convert_fusion.1
  112.6 1.0 pad_maximum_fusion
  (13 shorter events, 0.1 us)
Async XLA Ops:
  0.6 24.7 %copy-start = (bf16[128,3584]{1,0:T(8,128)(2,1)S(1)}, bf16[128,3584]{1,0:T(8,128)(2,1)}, u32[]{:S(2)}) copy-start(bf16[128,3584]{1,0:T(8,128)(2,1)} %own_ref.3) | copy-start | bytes 2752516
  0.6 1.0 copy-start.1
  1.7 0.7 copy-start.2
  2.4 6.0 %collective-permute-start = (bf16[16,2048]{1,0:T(8,128)(2,1)S(1)}, bf16[16,2048]{1,0:T(8,128)(2,1)S(1)}, u32[]{:S(2)}, u32[]{:S(2)}) collective-permute-start(bf16[16,2048]{1,0:T(8,128)(2,1)S(1)} %get-tuple-element.39), channel_id=1, source_target_pairs={{0,1},{1,0},{2,3},{3,2},{4,5},{5,4},{6,7},{7,6},{8,9},{9,8},{10,11... | collective-permute-start | bytes 196616 | tf_op jit(solution)/shard_map/ppermute | solution.py:27
  5.5 7.3 %collective-permute-start.1 = (bf16[16,2048]{1,0:T(8,128)(2,1)S(1)}, bf16[16,2048]{1,0:T(8,128)(2,1)S(1)}, u32[]{:S(2)}, u32[]{:S(2)}) collective-permute-start(bf16[16,2048]{1,0:T(8,128)(2,1)S(1)} %get-tuple-element.40), channel_id=1, source_target_pairs={{0,2},{1,3},{2,0},{3,1},{4,6},{5,7},{6,4},{7,5},{8,10},{9,11},{10,... | collective-permute-start | bytes 196616 | tf_op jit(solution)/shard_map/ppermute | solution.py:27
  8.1 6.1 %collective-permute-start.2 = (bf16[16,2048]{1,0:T(8,128)(2,1)S(1)}, bf16[16,2048]{1,0:T(8,128)(2,1)S(1)}, u32[]{:S(2)}, u32[]{:S(2)}) collective-permute-start(bf16[16,2048]{1,0:T(8,128)(2,1)S(1)} %get-tuple-element.41), channel_id=1, source_target_pairs={{0,3},{1,2},{2,1},{3,0},{4,7},{5,6},{6,5},{7,4},{8,11},{9,10},{10,... | collective-permute-start | bytes 196616 | tf_op jit(solution)/shard_map/ppermute | solution.py:27
  14.5 6.0 %collective-permute-start.4 = (bf16[16,2048]{1,0:T(8,128)(2,1)S(1)}, bf16[16,2048]{1,0:T(8,128)(2,1)S(1)}, u32[]{:S(2)}, u32[]{:S(2)}) collective-permute-start(bf16[16,2048]{1,0:T(8,128)(2,1)S(1)} %get-tuple-element.44), channel_id=1, source_target_pairs={{0,2},{1,3},{2,0},{3,1},{4,6},{5,7},{6,4},{7,5},{8,10},{9,11},{10,... | collective-permute-start | bytes 196616 | tf_op jit(solution)/shard_map/ppermute | solution.py:27
  16.1 6.1 %collective-permute-start.5 = (bf16[16,2048]{1,0:T(8,128)(2,1)S(1)}, bf16[16,2048]{1,0:T(8,128)(2,1)S(1)}, u32[]{:S(2)}, u32[]{:S(2)}) collective-permute-start(bf16[16,2048]{1,0:T(8,128)(2,1)S(1)} %get-tuple-element.45), channel_id=1, source_target_pairs={{0,3},{1,2},{2,1},{3,0},{4,7},{5,6},{6,5},{7,4},{8,11},{9,10},{10,... | collective-permute-start | bytes 196616 | tf_op jit(solution)/shard_map/ppermute | solution.py:27
  16.8 5.4 %collective-permute-start.3 = (bf16[16,2048]{1,0:T(8,128)(2,1)S(1)}, bf16[16,2048]{1,0:T(8,128)(2,1)S(1)}, u32[]{:S(2)}, u32[]{:S(2)}) collective-permute-start(bf16[16,2048]{1,0:T(8,128)(2,1)S(1)} %get-tuple-element.43), channel_id=1, source_target_pairs={{0,1},{1,0},{2,3},{3,2},{4,5},{5,4},{6,7},{7,6},{8,9},{9,8},{10,11... | collective-permute-start | bytes 196616 | tf_op jit(solution)/shard_map/ppermute | solution.py:27
  22.3 6.4 %collective-permute-start.7 = (bf16[64,2048]{1,0:T(8,128)(2,1)S(1)}, bf16[64,2048]{1,0:T(8,128)(2,1)S(1)}, u32[]{:S(2)}, u32[]{:S(2)}) collective-permute-start(bf16[64,2048]{1,0:T(8,128)(2,1)S(1)} %pad_maximum_fusion.1.refs_0_), channel_id=1, source_target_pairs={{0,8},{4,12},{8,0},{12,4},{16,24},{20,28},{24,16},{28,20},{1,9},{5... | collective-permute-start | bytes 786440 | tf_op jit(solution)/shard_map/ppermute | solution.py:27
  23.8 6.4 %collective-permute-start.8 = (bf16[64,2048]{1,0:T(8,128)(2,1)S(1)}, bf16[64,2048]{1,0:T(8,128)(2,1)S(1)}, u32[]{:S(2)}, u32[]{:S(2)}) collective-permute-start(bf16[64,2048]{1,0:T(8,128)(2,1)S(1)} %pad_maximum_fusion.1.refs_0_), channel_id=1, source_target_pairs={{0,16},{4,20},{8,24},{12,28},{16,0},{20,4},{24,8},{28,12},{1,17},{... | collective-permute-start | bytes 786440 | tf_op jit(solution)/shard_map/ppermute | solution.py:27
  25.4 21.2 %collective-permute-start.13 = (bf16[128,3584]{1,0:T(8,128)(2,1)S(1)}, bf16[128,3584]{1,0:T(8,128)(2,1)S(1)}, u32[]{:S(2)}, u32[]{:S(2)}) collective-permute-start(bf16[128,3584]{1,0:T(8,128)(2,1)S(1)} %copy-done), channel_id=1, source_target_pairs={{0,1},{1,0},{2,3},{3,2},{4,5},{5,4},{6,7},{7,6},{8,9},{9,8},{10,11... | collective-permute-start | bytes 2752520 | tf_op jit(solution)/shard_map/ppermute | solution.py:27
  25.5 21.1 %collective-permute-start.14 = (bf16[128,3584]{1,0:T(8,128)(2,1)S(1)}, bf16[128,3584]{1,0:T(8,128)(2,1)S(1)}, u32[]{:S(2)}, u32[]{:S(2)}) collective-permute-start(bf16[128,3584]{1,0:T(8,128)(2,1)S(1)} %copy-done), channel_id=1, source_target_pairs={{1,2},{2,1},{5,6},{6,5},{9,10},{10,9},{13,14},{14,13},{17,18},{18,... | collective-permute-start | bytes 2752520 | tf_op jit(solution)/shard_map/ppermute | solution.py:346
  26.2 5.7 %collective-permute-start.6 = (bf16[64,2048]{1,0:T(8,128)(2,1)S(1)}, bf16[64,2048]{1,0:T(8,128)(2,1)S(1)}, u32[]{:S(2)}, u32[]{:S(2)}) collective-permute-start(bf16[64,2048]{1,0:T(8,128)(2,1)S(1)} %pad_maximum_fusion.1.refs_0_), channel_id=1, source_target_pairs={{0,4},{4,0},{8,12},{12,8},{16,20},{20,16},{24,28},{28,24},{1,5},{5... | collective-permute-start | bytes 786440 | tf_op jit(solution)/shard_map/ppermute | solution.py:27
  30.2 6.4 %collective-permute-start.11 = (bf16[64,2048]{1,0:T(8,128)(2,1)S(1)}, bf16[64,2048]{1,0:T(8,128)(2,1)S(1)}, u32[]{:S(2)}, u32[]{:S(2)}) collective-permute-start(bf16[64,2048]{1,0:T(8,128)(2,1)S(1)} %broadcast_select_fusion), channel_id=1, source_target_pairs={{0,16},{4,12},{8,24},{12,4},{16,0},{20,28},{24,8},{28,20},{1,17},{... | collective-permute-start | bytes 786440 | tf_op jit(solution)/shard_map/ppermute | solution.py:162
  31.8 4.9 %collective-permute-start.9 = (bf16[64,2048]{1,0:T(8,128)(2,1)S(1)}, bf16[64,2048]{1,0:T(8,128)(2,1)S(1)}, u32[]{:S(2)}, u32[]{:S(2)}) collective-permute-start(bf16[64,2048]{1,0:T(8,128)(2,1)S(1)} %collective-permute-done.7.refs_2_), channel_id=1, source_target_pairs={{0,4},{4,0},{8,12},{12,8},{16,20},{20,16},{24,28},{28,24},{1,5},{5... | collective-permute-start | bytes 786440 | tf_op jit(solution)/shard_map/ppermute | solution.py:27
  31.8 4.9 %collective-permute-start.10 = (bf16[64,2048]{1,0:T(8,128)(2,1)S(1)}, bf16[64,2048]{1,0:T(8,128)(2,1)S(1)}, u32[]{:S(2)}, u32[]{:S(2)}) collective-permute-start(bf16[64,2048]{1,0:T(8,128)(2,1)S(1)} %collective-permute-done.8.refs_4_), channel_id=1, source_target_pairs={{0,4},{4,0},{8,12},{12,8},{16,20},{20,16},{24,28},{28,24},{1,5},{5... | collective-permute-start | bytes 786440 | tf_op jit(solution)/shard_map/ppermute | solution.py:27
  36.7 1.5 %collective-permute-start.12 = (bf16[64,2048]{1,0:T(8,128)(2,1)S(1)}, bf16[64,2048]{1,0:T(8,128)(2,1)S(1)}, u32[]{:S(2)}, u32[]{:S(2)}) collective-permute-start(bf16[64,2048]{1,0:T(8,128)(2,1)S(1)} %collective-permute-done.11.refs_6_), channel_id=1, source_target_pairs={{0,4},{4,0},{8,12},{12,8},{16,20},{20,16},{24,28},{28,24},{1,5},{5... | collective-permute-start | bytes 786440 | tf_op jit(solution)/shard_map/ppermute | solution.py:27
  44.2 20.1 %collective-permute-start.18 = (bf16[256,1536]{1,0:T(8,128)(2,1)S(1)}, bf16[256,1536]{1,0:T(8,128)(2,1)S(1)}, u32[]{:S(2)}, u32[]{:S(2)}) collective-permute-start(bf16[256,1536]{1,0:T(8,128)(2,1)S(1)} %get-tuple-element.55), channel_id=1, source_target_pairs={{0,1},{3,2},{4,5},{7,6},{8,9},{11,10},{12,13},{15,14},{16,17},{19,... | collective-permute-start | bytes 2359304 | tf_op jit(solution)/shard_map/ppermute | solution.py:346
  46.5 23.1 %collective-permute-start.16 = (bf16[128,3584]{1,0:T(8,128)(2,1)S(1)}, bf16[128,3584]{1,0:T(8,128)(2,1)S(1)}, u32[]{:S(2)}, u32[]{:S(2)}) collective-permute-start(bf16[128,3584]{1,0:T(8,128)(2,1)S(1)} %collective-permute-done.13.e1), channel_id=1, source_target_pairs={{1,2},{2,1},{5,6},{6,5},{9,10},{10,9},{13,14},{14,13},{17,18},{18,... | collective-permute-start | bytes 2752520 | tf_op jit(solution)/shard_map/ppermute | solution.py:346
  47.3 24.0 %collective-permute-start.17 = (bf16[128,3584]{1,0:T(8,128)(2,1)S(1)}, bf16[128,3584]{1,0:T(8,128)(2,1)S(1)}, u32[]{:S(2)}, u32[]{:S(2)}) collective-permute-start(bf16[128,3584]{1,0:T(8,128)(2,1)S(1)} %collective-permute-done.14.o1), channel_id=1, source_target_pairs={{1,0},{2,3},{5,4},{6,7},{9,8},{10,11},{13,12},{14,15},{17,16},{18,... | collective-permute-start | bytes 2752520 | tf_op jit(solution)/shard_map/ppermute | solution.py:346
  55.7 19.9 %collective-permute-start.15 = (bf16[128,2048]{1,0:T(8,128)(2,1)S(1)}, bf16[128,2048]{1,0:T(8,128)(2,1)S(1)}, u32[]{:S(2)}, u32[]{:S(2)}) collective-permute-start(bf16[128,2048]{1,0:T(8,128)(2,1)S(1)} %get-tuple-element.52), channel_id=1, source_target_pairs={{0,1},{3,2},{4,5},{7,6},{8,9},{11,10},{12,13},{15,14},{16,17},{19,... | collective-permute-start | bytes 1572872 | tf_op jit(solution)/shard_map/ppermute | solution.py:346
  64.4 21.7 %collective-permute-start.22 = (bf16[128,2048]{1,0:T(8,128)(2,1)S(1)}, bf16[128,2048]{1,0:T(8,128)(2,1)S(1)}, u32[]{:S(2)}, u32[]{:S(2)}) collective-permute-start(bf16[128,2048]{1,0:T(8,128)(2,1)S(1)} %get-tuple-element.62), channel_id=1, source_target_pairs={{0,1},{3,2},{4,5},{7,6},{8,9},{11,10},{12,13},{15,14},{16,17},{19,... | collective-permute-start | bytes 1572872 | tf_op jit(solution)/shard_map/ppermute | solution.py:346
  69.0 17.9 %collective-permute-start.20 = (bf16[256,1536]{1,0:T(8,128)(2,1)S(1)}, bf16[256,1536]{1,0:T(8,128)(2,1)S(1)}, u32[]{:S(2)}, u32[]{:S(2)}) collective-permute-start(bf16[256,1536]{1,0:T(8,128)(2,1)S(1)} %add_convert_fusion), channel_id=1, source_target_pairs={{1,2},{2,1},{5,6},{6,5},{9,10},{10,9},{13,14},{14,13},{17,18},{18,... | collective-permute-start | bytes 2359304 | tf_op jit(solution)/shard_map/ppermute | solution.py:346
  71.3 21.9 %collective-permute-start.21 = (bf16[128,3584]{1,0:T(8,128)(2,1)S(1)}, bf16[128,3584]{1,0:T(8,128)(2,1)S(1)}, u32[]{:S(2)}, u32[]{:S(2)}) collective-permute-start(bf16[128,3584]{1,0:T(8,128)(2,1)S(1)} %collective-permute-done.16.o2), channel_id=1, source_target_pairs={{1,0},{2,3},{5,4},{6,7},{9,8},{10,11},{13,12},{14,15},{17,16},{18,... | collective-permute-start | bytes 2752520 | tf_op jit(solution)/shard_map/ppermute | solution.py:346
  75.7 24.4 %collective-permute-start.19 = (bf16[128,2048]{1,0:T(8,128)(2,1)S(1)}, bf16[128,2048]{1,0:T(8,128)(2,1)S(1)}, u32[]{:S(2)}, u32[]{:S(2)}) collective-permute-start(bf16[128,2048]{1,0:T(8,128)(2,1)S(1)} %add_convert_fusion.4), channel_id=1, source_target_pairs={{1,2},{2,1},{5,6},{6,5},{9,10},{10,9},{13,14},{14,13},{17,18},{18,... | collective-permute-start | bytes 1572872 | tf_op jit(solution)/shard_map/ppermute | solution.py:346
  86.2 24.8 %collective-permute-start.25 = (bf16[128,2048]{1,0:T(8,128)(2,1)S(1)}, bf16[128,2048]{1,0:T(8,128)(2,1)S(1)}, u32[]{:S(2)}, u32[]{:S(2)}) collective-permute-start(bf16[128,2048]{1,0:T(8,128)(2,1)S(1)} %add_convert_fusion.2), channel_id=1, source_target_pairs={{1,2},{2,1},{5,6},{6,5},{9,10},{10,9},{13,14},{14,13},{17,18},{18,... | collective-permute-start | bytes 1572872 | tf_op jit(solution)/shard_map/ppermute | solution.py:346
  93.3 8.4 %collective-permute-start.23 = (bf16[128,1536]{1,0:T(8,128)(2,1)S(1)}, bf16[128,1536]{1,0:T(8,128)(2,1)S(1)}, u32[]{:S(2)}, u32[]{:S(2)}) collective-permute-start(bf16[128,1536]{1,0:T(8,128)(2,1)S(1)} %add_convert_fusion.6), channel_id=1, source_target_pairs={{0,1},{1,0},{2,3},{3,2},{4,5},{5,4},{6,7},{7,6},{8,9},{9,8},{10,11... | collective-permute-start | bytes 1179656 | tf_op jit(solution)/shard_map/ppermute | solution.py:27
  101.8 10.6 %collective-permute-start.24 = (bf16[128,2048]{1,0:T(8,128)(2,1)S(1)}, bf16[128,2048]{1,0:T(8,128)(2,1)S(1)}, u32[]{:S(2)}, u32[]{:S(2)}) collective-permute-start(bf16[128,2048]{1,0:T(8,128)(2,1)S(1)} %add_convert_fusion.3), channel_id=1, source_target_pairs={{0,1},{1,0},{2,3},{3,2},{4,5},{5,4},{6,7},{7,6},{8,9},{9,8},{10,11... | collective-permute-start | bytes 1572872 | tf_op jit(solution)/shard_map/ppermute | solution.py:27
where the time goes:
time: 114 us
  waiting for transfers between devices  45 us (39%)
  starting transfers between devices  34.6 us (30%)
  Pallas kernels  29 us (25%)
  other arithmetic  2.44 us (2%)
  local copies, waits for them, and re-layouts  1.72 us (2%)
    ppermute x10, waiting for transfers between devices, move(): return lax.ppermute(block, 'tensor', pairs)  22.3 us
    ppermute x10, starting transfers between devices, move(): return lax.ppermute(block, 'tensor', pairs)  19 us
    ppermute x15, waiting for transfers between devices, swap(): lax.ppermute(block, axis, [(i, i ^ mask) for i in range(count) if i ^ mas...  18.3 us
    pallas_call x2, Pallas kernels, weight_gradient(): pl.pallas_call(functools.partial(grad_kernel, tile, start), out_shape=jax...  14.8 us
    ppermute x15, starting transfers between devices, swap(): lax.ppermute(block, axis, [(i, i ^ mask) for i in range(count) if i ^ mas...  13.9 us
    pallas_call x1, Pallas kernels, project(): pl.pallas_call(project_kernel, out_shape=[jax.ShapeDtypeStruct((block, wi...  7.14 us
    pallas_call x1, Pallas kernels, project_first(): pl.pallas_call(first_kernel, out_shape=[jax.ShapeDtypeStruct((tokens, dep...  6.03 us
    ppermute x1, waiting for transfers between devices, gather_rows(): lax.ppermute(through, 'dp', [(i, i ^ (4 if i & 1 == 0 else 2)) for i in r...  4.34 us
  transfers between devices with their start and end apart: 26, of which 15 were waited for; matrix products, arithmetic and copies ran while one was open for 1% of the time, Pallas kernels for 25%

commit v1 on v0

--- a/solution.py
+++ b/solution.py
@@ -338,6 +338,100 @@
     )(q_t, own, *moved, *before)
 
 
+def early_kernel(tile, q_t, own_ref, e1, o1, e2, out_ref, near, far, sems):
+    z = lax.axis_index("tensor")
+    rows, width = far.shape
+
+    def copy(source, place, n):
+        return pltpu.make_async_copy(source.at[:, :width], place, sems.at[n])
+
+    copy(own_ref, near.at[:rows, :], 0).start()
+    copy(e1, near.at[rows:, :], 1).start()
+
+    @pl.when(is_outer(z) == 0)
+    def _():
+        copy(o1, far, 2).start()
+
+    @pl.when(is_outer(z) == 1)
+    def _():
+        copy(e2, far, 2).start()
+
+    copy(own_ref, near.at[:rows, :], 0).wait()
+    copy(e1, near.at[rows:, :], 1).wait()
+    copy(o1, far, 2).wait()
+
+    @pl.loop(0, width // tile)
+    def _(n):
+        columns = pl.ds(pl.multiple_of(n * tile, tile), tile)
+        out_ref[:, columns] = jnp.dot(
+            q_t[:, : 2 * rows], near[:, columns], preferred_element_type=jnp.float32
+        ) + jnp.dot(q_t[:, 3 * rows :], far[:, columns], preferred_element_type=jnp.float32)
+
+
+def gradient_early(q_t, own, e1, o1, e2, width):
+    depth, tokens = q_t.shape
+    rows = own.shape[0]
+    anywhere = pl.BlockSpec(memory_space=pl.ANY)
+    return pl.pallas_call(
+        functools.partial(early_kernel, tile_of(width)),
+        out_shape=jax.ShapeDtypeStruct((depth, width), jnp.float32),
+        in_specs=[VMEM] + [anywhere] * 4,
+        out_specs=VMEM,
+        scratch_shapes=[
+            pltpu.VMEM((2 * rows, width), jnp.bfloat16),
+            pltpu.VMEM((rows, width), jnp.bfloat16),
+            pltpu.SemaphoreType.DMA((3,)),
+        ],
+        compiler_params=pltpu.CompilerParams(vmem_limit_bytes=20 * MIB),
+        cost_estimate=pl.CostEstimate(flops=1, bytes_accessed=1, transcendentals=0),
+        name="gradient_early",
+    )(q_t, own, e1, o1, e2)
+
+
+def late_kernel(tile, early, q_t, o2, e3, out_ref, third, sem):
+    z = lax.axis_index("tensor")
+    rows, width = third.shape
+
+    @pl.when(pl.program_id(0) == 0)
+    def _():
+        @pl.when(is_outer(z) == 0)
+        def _():
+            pltpu.make_async_copy(o2.at[:, :width], third, sem).start()
+
+        @pl.when(is_outer(z) == 1)
+        def _():
+            pltpu.make_async_copy(e3.at[:, :width], third, sem).start()
+
+        pltpu.make_async_copy(o2.at[:, :width], third, sem).wait()
+
+    columns = pl.ds(pl.multiple_of(pl.program_id(0) * tile, tile), tile)
+    out_ref[...] = early[:, columns] + jnp.dot(
+        q_t[:, 2 * rows : 3 * rows], third[:, columns], preferred_element_type=jnp.float32
+    )
+
+
+def gradient_late(early, q_t, o2, e3):
+    depth, width = early.shape
+    rows, hidden = o2.shape
+    tile = tile_of(width)
+    anywhere = pl.BlockSpec(memory_space=pl.ANY)
+    return pl.pallas_call(
+        functools.partial(late_kernel, tile),
+        out_shape=jax.ShapeDtypeStruct((depth, hidden), jnp.float32),
+        grid=(width // tile,),
+        in_specs=[VMEM, VMEM, anywhere, anywhere],
+        out_specs=pl.BlockSpec((depth, tile), lambda n: (0, n)),
+        scratch_shapes=[pltpu.VMEM((rows, width), jnp.bfloat16), pltpu.SemaphoreType.DMA],
+        compiler_params=pltpu.CompilerParams(vmem_limit_bytes=16 * MIB),
+        cost_estimate=pl.CostEstimate(
+            flops=12 * rows * depth * width,
+            bytes_accessed=4 * depth * width,
+            transcendentals=0,
+        ),
+        name="gradient_late",
+    )(early, q_t, o2, e3)
+
+
 def total(*blocks):
     return sum(b.astype(jnp.float32) for b in blocks).astype(jnp.bfloat16)
 
@@ -398,8 +492,10 @@
     q_t = transposed(late)
     moved = (e1, o1, o2, e2, e3)
     some = hidden // 2 // 512 * 512
+    early = gradient_early(q_t, upstream, e1, o1, e2, some)
+    inward_near, early = after([inward_near, early])
     (late,) = after([q_t], across_a, inward_near)
-    grad = weight_gradient(late, upstream, moved, 0, some)
+    grad = gradient_late(early, late, o2, e3)
 
     across_near = move(total(near_b, inward_near), *MIDDLE)
     across_far, grad, out_a = after([across_far, grad, out_a])

time: 114 us -> 114 us (level)
  waiting for transfers between devices: 45 us -> 41.2 us
  Pallas kernels: 29 us -> 31.6 us
    pallas_call x0 -> x2, Pallas kernels: none -> 9.34 us  [the longest x1 5.48 us: gradient_late(): pl.pallas_call(functools.partial(late_kernel, tile), out_shape=jax.ShapeD...]
    pallas_call x2 -> x1, Pallas kernels: 14.8 us -> 8.09 us  [weight_gradient(): pl.pallas_call(functools.partial(grad_kernel, tile, start), out_shape=jax...]
    ppermute x10, waiting for transfers between devices: 22.3 us -> 17.6 us  [move(): return lax.ppermute(block, 'tensor', pairs)]
  transfers between devices with their start and end apart: 26 -> 26, of which waited for: 15 -> 15; matrix products, arithmetic and copies ran while one was open for 1% -> 1% of each run, Pallas kernels for 25% -> 28%
where the time goes in v1:
time: 114 us; the launch traced here: 113 us
  waiting for transfers between devices  41.2 us (36%)
  starting transfers between devices  35.5 us (31%)
  Pallas kernels  31.6 us (28%)
  other arithmetic  2.45 us (2%)
  local copies, waits for them, and re-layouts  1.65 us (1%)
    ppermute x10, starting transfers between devices, move(): return lax.ppermute(block, 'tensor', pairs)  19.4 us
    ppermute x15, waiting for transfers between devices, swap(): lax.ppermute(block, axis, [(i, i ^ mask) for i in range(count) if i ^ mas...  19.2 us
    ppermute x10, waiting for transfers between devices, move(): return lax.ppermute(block, 'tensor', pairs)  17.6 us
    ppermute x15, starting transfers between devices, swap(): lax.ppermute(block, axis, [(i, i ^ mask) for i in range(count) if i ^ mas...  14.5 us
    pallas_call x1, Pallas kernels, weight_gradient(): pl.pallas_call(functools.partial(grad_kernel, tile, start), out_shape=jax...  8.09 us
    pallas_call x1, Pallas kernels, project(): pl.pallas_call(project_kernel, out_shape=[jax.ShapeDtypeStruct((block, wi...  7.14 us
    pallas_call x1, Pallas kernels, project_first(): pl.pallas_call(first_kernel, out_shape=[jax.ShapeDtypeStruct((tokens, dep...  6.03 us
    pallas_call x1, Pallas kernels, gradient_late(): pl.pallas_call(functools.partial(late_kernel, tile), out_shape=jax.ShapeD...  5.48 us
  transfers between devices with their start and end apart: 26, of which 15 were waited for; matrix products, arithmetic and copies ran while one was open for 1% of the time, Pallas kernels for 28%

profile of v1, /device:TPU:0, one launch (start us, length us, event | category | flops | bytes accessed | tf_op | source)
XLA Modules:
  0.0 113.3 jit_solution(1580663357740800543)
XLA Ops:
  0.6 0.9 copy-done.1
  1.6 0.7 copy-done.2
  2.3 0.1 signed_pieces.1
  2.3 3.1 %collective-permute-start = (bf16[16,2048]{1,0:T(8,128)(2,1)S(1)}, bf16[16,2048]{1,0:T(8,128)(2,1)S(1)}, u32[]{:S(2)}, u32[]{:S(2)}) collective-permute-start(bf16[16,2048]{1,0:T(8,128)(2,1)S(1)} %get-tuple-element.41), channel_id=1, source_target_pairs={{0,1},{1,0},{2,3},{3,2},{4,5},{5,4},{6,7},{7,6},{8,9},{9,8},{10,11... | collective-permute-start | bytes 196616 | tf_op jit(solution)/shard_map/ppermute | solution.py:27
  5.4 2.6 %collective-permute-start.1 = (bf16[16,2048]{1,0:T(8,128)(2,1)S(1)}, bf16[16,2048]{1,0:T(8,128)(2,1)S(1)}, u32[]{:S(2)}, u32[]{:S(2)}) collective-permute-start(bf16[16,2048]{1,0:T(8,128)(2,1)S(1)} %get-tuple-element.42), channel_id=1, source_target_pairs={{0,2},{1,3},{2,0},{3,1},{4,6},{5,7},{6,4},{7,5},{8,10},{9,11},{10,... | collective-permute-start | bytes 196616 | tf_op jit(solution)/shard_map/ppermute | solution.py:27
  8.0 0.0 collective-permute-start.2
  8.0 0.3 fusion.3.h_ref
  8.4 4.3 %collective-permute-done.1.refs_2_ = bf16[16,2048]{1,0:T(8,128)(2,1)S(1)} collective-permute-done((bf16[16,2048]{1,0:T(8,128)(2,1)S(1)}, bf16[16,2048]{1,0:T(8,128)(2,1)S(1)}, u32[]{:S(2)}, u32[]{:S(2)}) %collective-permute-start.1) | collective-permute-done | bytes 65568 | tf_op jit(solution)/shard_map/ppermute | solution.py:27
  12.7 1.4 %collective-permute-done.2.refs_3_ = bf16[16,2048]{1,0:T(8,128)(2,1)S(1)} collective-permute-done((bf16[16,2048]{1,0:T(8,128)(2,1)S(1)}, bf16[16,2048]{1,0:T(8,128)(2,1)S(1)}, u32[]{:S(2)}, u32[]{:S(2)}) %collective-permute-start.2) | collective-permute-done | bytes 65568 | tf_op jit(solution)/shard_map/ppermute | solution.py:27
  14.1 0.3 rotate.1
  14.4 1.6 %collective-permute-start.4 = (bf16[16,2048]{1,0:T(8,128)(2,1)S(1)}, bf16[16,2048]{1,0:T(8,128)(2,1)S(1)}, u32[]{:S(2)}, u32[]{:S(2)}) collective-permute-start(bf16[16,2048]{1,0:T(8,128)(2,1)S(1)} %get-tuple-element.46), channel_id=1, source_target_pairs={{0,2},{1,3},{2,0},{3,1},{4,6},{5,7},{6,4},{7,5},{8,10},{9,11},{10,... | collective-permute-start | bytes 196616 | tf_op jit(solution)/shard_map/ppermute | solution.py:27
  16.1 0.7 collective-permute-start.5
  16.7 1.2 %collective-permute-start.3 = (bf16[16,2048]{1,0:T(8,128)(2,1)S(1)}, bf16[16,2048]{1,0:T(8,128)(2,1)S(1)}, u32[]{:S(2)}, u32[]{:S(2)}) collective-permute-start(bf16[16,2048]{1,0:T(8,128)(2,1)S(1)} %get-tuple-element.45), channel_id=1, source_target_pairs={{0,1},{1,0},{2,3},{3,2},{4,5},{5,4},{6,7},{7,6},{8,9},{9,8},{10,11... | collective-permute-start | bytes 196616 | tf_op jit(solution)/shard_map/ppermute | solution.py:27
  18.0 2.4 %collective-permute-done.4 = bf16[16,2048]{1,0:T(8,128)(2,1)S(1)} collective-permute-done((bf16[16,2048]{1,0:T(8,128)(2,1)S(1)}, bf16[16,2048]{1,0:T(8,128)(2,1)S(1)}, u32[]{:S(2)}, u32[]{:S(2)}) %collective-permute-start.4) | collective-permute-done | bytes 65568 | tf_op jit(solution)/shard_map/ppermute | solution.py:27
  20.4 1.7 %collective-permute-done.5 = bf16[16,2048]{1,0:T(8,128)(2,1)S(1)} collective-permute-done((bf16[16,2048]{1,0:T(8,128)(2,1)S(1)}, bf16[16,2048]{1,0:T(8,128)(2,1)S(1)}, u32[]{:S(2)}, u32[]{:S(2)}) %collective-permute-start.5) | collective-permute-done | bytes 65568 | tf_op jit(solution)/shard_map/ppermute | solution.py:27
  22.1 0.0 collective-permute-done.3
  22.2 1.5 %collective-permute-start.7 = (bf16[64,2048]{1,0:T(8,128)(2,1)S(1)}, bf16[64,2048]{1,0:T(8,128)(2,1)S(1)}, u32[]{:S(2)}, u32[]{:S(2)}) collective-permute-start(bf16[64,2048]{1,0:T(8,128)(2,1)S(1)} %pad_maximum_fusion.1.refs_0_), channel_id=1, source_target_pairs={{0,8},{4,12},{8,0},{12,4},{16,24},{20,28},{24,16},{28,20},{1,9},{5... | collective-permute-start | bytes 786440 | tf_op jit(solution)/shard_map/ppermute | solution.py:27
  23.7 1.5 %collective-permute-start.8 = (bf16[64,2048]{1,0:T(8,128)(2,1)S(1)}, bf16[64,2048]{1,0:T(8,128)(2,1)S(1)}, u32[]{:S(2)}, u32[]{:S(2)}) collective-permute-start(bf16[64,2048]{1,0:T(8,128)(2,1)S(1)} %pad_maximum_fusion.1.refs_0_), channel_id=1, source_target_pairs={{0,16},{4,20},{8,24},{12,28},{16,0},{20,4},{24,8},{28,12},{1,17},{... | collective-permute-start | bytes 786440 | tf_op jit(solution)/shard_map/ppermute | solution.py:27
  25.3 0.1 collective-permute-start.13
  25.4 0.7 collective-permute-start.14
  26.1 0.1 collective-permute-start.6
  26.2 2.5 %collective-permute-done.7.refs_2_ = bf16[64,2048]{1,0:T(8,128)(2,1)S(1)} collective-permute-done((bf16[64,2048]{1,0:T(8,128)(2,1)S(1)}, bf16[64,2048]{1,0:T(8,128)(2,1)S(1)}, u32[]{:S(2)}, u32[]{:S(2)}) %collective-permute-start.7) | collective-permute-done | bytes 262176 | tf_op jit(solution)/shard_map/ppermute | solution.py:27
  28.6 1.5 %collective-permute-done.8.refs_4_ = bf16[64,2048]{1,0:T(8,128)(2,1)S(1)} collective-permute-done((bf16[64,2048]{1,0:T(8,128)(2,1)S(1)}, bf16[64,2048]{1,0:T(8,128)(2,1)S(1)}, u32[]{:S(2)}, u32[]{:S(2)}) %collective-permute-start.8) | collective-permute-done | bytes 262176 | tf_op jit(solution)/shard_map/ppermute | solution.py:27
  30.1 1.6 %collective-permute-start.11 = (bf16[64,2048]{1,0:T(8,128)(2,1)S(1)}, bf16[64,2048]{1,0:T(8,128)(2,1)S(1)}, u32[]{:S(2)}, u32[]{:S(2)}) collective-permute-start(bf16[64,2048]{1,0:T(8,128)(2,1)S(1)} %broadcast_select_fusion), channel_id=1, source_target_pairs={{0,16},{4,12},{8,24},{12,4},{16,0},{20,28},{24,8},{28,20},{1,17},{... | collective-permute-start | bytes 786440 | tf_op jit(solution)/shard_map/ppermute | solution.py:162
  31.7 0.5 collective-permute-start.10
  32.2 4.3 %collective-permute-done.11.refs_6_ = bf16[64,2048]{1,0:T(8,128)(2,1)S(1)} collective-permute-done((bf16[64,2048]{1,0:T(8,128)(2,1)S(1)}, bf16[64,2048]{1,0:T(8,128)(2,1)S(1)}, u32[]{:S(2)}, u32[]{:S(2)}) %collective-permute-start.11) | collective-permute-done | bytes 262176 | tf_op jit(solution)/shard_map/ppermute | solution.py:162
  36.6 0.0 collective-permute-start.12
  36.6 1.5 %collective-permute-done.12.refs_7_ = bf16[64,2048]{1,0:T(8,128)(2,1)S(1)} collective-permute-done((bf16[64,2048]{1,0:T(8,128)(2,1)S(1)}, bf16[64,2048]{1,0:T(8,128)(2,1)S(1)}, u32[]{:S(2)}, u32[]{:S(2)}) %collective-permute-start.12) | collective-permute-done | bytes 262176 | tf_op jit(solution)/shard_map/ppermute | solution.py:27
  38.1 6.0 %project_first.1 = (bf16[512,2048]{1,0:T(8,128)(2,1)S(1)}, bf16[128,1536]{1,0:T(8,128)(2,1)S(1)}, bf16[128,1536]{1,0:T(8,128)(2,1)S(1)}, bf16[256,1536]{1,0:T(8,128)(2,1)S(1)}) custom-call(bf16[64,2048]{1,0:T(8,128)(2,1)S(1)} %pad_maximum_fusion.1.refs_0_, bf16[64,2048]{1,0:T(8,128)(2,1)S(1)} %collective-permute-done.6.refs_1_, ...), custom_call_target="tpu_custom_call" | custom-call | flops 1 | bytes 1 | tf_op jit(solution)/shard_map/project_first/pallas_call | solution.py:221
  44.1 2.3 %collective-permute-start.18 = (bf16[256,1536]{1,0:T(8,128)(2,1)S(1)}, bf16[256,1536]{1,0:T(8,128)(2,1)S(1)}, u32[]{:S(2)}, u32[]{:S(2)}) collective-permute-start(bf16[256,1536]{1,0:T(8,128)(2,1)S(1)} %get-tuple-element.57), channel_id=1, source_target_pairs={{0,1},{3,2},{4,5},{7,6},{8,9},{11,10},{12,13},{15,14},{16,17},{19,... | collective-permute-start | bytes 2359304 | tf_op jit(solution)/shard_map/ppermute | solution.py:440
  46.4 0.7 collective-permute-start.16
  47.2 1.3 %collective-permute-start.17 = (bf16[128,3584]{1,0:T(8,128)(2,1)S(1)}, bf16[128,3584]{1,0:T(8,128)(2,1)S(1)}, u32[]{:S(2)}, u32[]{:S(2)}) collective-permute-start(bf16[128,3584]{1,0:T(8,128)(2,1)S(1)} %collective-permute-done.14.o1), channel_id=1, source_target_pairs={{1,0},{2,3},{5,4},{6,7},{9,8},{10,11},{13,12},{14,15},{17,16},{18,... | collective-permute-start | bytes 2752520 | tf_op jit(solution)/shard_map/ppermute | solution.py:440
  48.5 7.1 %project.1 = (bf16[128,2048]{1,0:T(8,128)(2,1)S(1)}, bf16[128,2048]{1,0:T(8,128)(2,1)S(1)}, bf16[128,2048]{1,0:T(8,128)(2,1)S(1)}, bf16[128,2048]{1,0:T(8,128)(2,1)S(1)}) custom-call(bf16[512,2048]{1,0:T(8,128)(2,1)S(1)} %get-tuple-element.63.q_ref, bf16[2048,3584]{1,0:T(8,128)(2,1)} %w_ref.1), custom_call_target="tpu_custom_call" | custom-call | flops 4294967296 | bytes 12582912 | tf_op jit(solution)/shard_map/project/pallas_call | solution.py:243
  55.6 6.5 %collective-permute-start.15 = (bf16[128,2048]{1,0:T(8,128)(2,1)S(1)}, bf16[128,2048]{1,0:T(8,128)(2,1)S(1)}, u32[]{:S(2)}, u32[]{:S(2)}) collective-permute-start(bf16[128,2048]{1,0:T(8,128)(2,1)S(1)} %get-tuple-element.54), channel_id=1, source_target_pairs={{0,1},{3,2},{4,5},{7,6},{8,9},{11,10},{12,13},{15,14},{16,17},{19,... | collective-permute-start | bytes 1572872 | tf_op jit(solution)/shard_map/ppermute | solution.py:440
  62.1 2.1 %collective-permute-done.18 = bf16[256,1536]{1,0:T(8,128)(2,1)S(1)} collective-permute-done((bf16[256,1536]{1,0:T(8,128)(2,1)S(1)}, bf16[256,1536]{1,0:T(8,128)(2,1)S(1)}, u32[]{:S(2)}, u32[]{:S(2)}) %collective-permute-start.18) | collective-permute-done | bytes 786464 | tf_op jit(solution)/shard_map/ppermute | solution.py:440
  64.3 4.4 %collective-permute-start.20 = (bf16[128,2048]{1,0:T(8,128)(2,1)S(1)}, bf16[128,2048]{1,0:T(8,128)(2,1)S(1)}, u32[]{:S(2)}, u32[]{:S(2)}) collective-permute-start(bf16[128,2048]{1,0:T(8,128)(2,1)S(1)} %get-tuple-element.62), channel_id=1, source_target_pairs={{0,1},{3,2},{4,5},{7,6},{8,9},{11,10},{12,13},{15,14},{16,17},{19,... | collective-permute-start | bytes 1572872 | tf_op jit(solution)/shard_map/ppermute | solution.py:440
  68.7 0.2 add_convert_fusion
  68.9 0.0 copy-start
  68.9 0.8 collective-permute-start.21
  69.7 1.4 %collective-permute-done.17.e2 = bf16[128,3584]{1,0:T(8,128)(2,1)S(1)} collective-permute-done((bf16[128,3584]{1,0:T(8,128)(2,1)S(1)}, bf16[128,3584]{1,0:T(8,128)(2,1)S(1)}, u32[]{:S(2)}, u32[]{:S(2)}) %collective-permute-start.17) | collective-permute-done | bytes 917536 | tf_op jit(solution)/shard_map/ppermute | solution.py:440
  71.2 1.3 %collective-permute-start.22 = (bf16[128,3584]{1,0:T(8,128)(2,1)S(1)}, bf16[128,3584]{1,0:T(8,128)(2,1)S(1)}, u32[]{:S(2)}, u32[]{:S(2)}) collective-permute-start(bf16[128,3584]{1,0:T(8,128)(2,1)S(1)} %collective-permute-done.16.o2), channel_id=1, source_target_pairs={{1,0},{2,3},{5,4},{6,7},{9,8},{10,11},{13,12},{14,15},{17,16},{18,... | collective-permute-start | bytes 2752520 | tf_op jit(solution)/shard_map/ppermute | solution.py:440
  72.5 3.0 %collective-permute-done.15 = bf16[128,2048]{1,0:T(8,128)(2,1)S(1)} collective-permute-done((bf16[128,2048]{1,0:T(8,128)(2,1)S(1)}, bf16[128,2048]{1,0:T(8,128)(2,1)S(1)}, u32[]{:S(2)}, u32[]{:S(2)}) %collective-permute-start.15) | collective-permute-done | bytes 524320 | tf_op jit(solution)/shard_map/ppermute | solution.py:440
  75.5 0.6 transposed.1.q_t
  76.1 0.1 add_convert_fusion.4
  76.2 0.7 collective-permute-start.19
  76.9 3.9 %gradient_early.1.early = f32[2048,1536]{1,0:T(8,128)S(1)} custom-call(bf16[2048,512]{1,0:T(8,128)(2,1)S(1)} %transposed.1.q_t, bf16[128,3584]{1,0:T(8,128)(2,1)S(1)} %copy-done, bf16[128,3584]{1,0:T(8,128)(2,1)S(1)} %collective-permute-done.13.e1, bf16[128,3584]{1,0:T(8,128)(2,1)S(1)} %collective-permute-done.14.o1, ...), custom_call_target="tpu_custom_call" | custom-call | flops 1 | bytes 1 | tf_op jit(solution)/shard_map/gradient_early/pallas_call | solution.py:375
  80.8 5.1 %collective-permute-done.20 = bf16[128,2048]{1,0:T(8,128)(2,1)S(1)} collective-permute-done((bf16[128,2048]{1,0:T(8,128)(2,1)S(1)}, bf16[128,2048]{1,0:T(8,128)(2,1)S(1)}, u32[]{:S(2)}, u32[]{:S(2)}) %collective-permute-start.20) | collective-permute-done | bytes 524320 | tf_op jit(solution)/shard_map/ppermute | solution.py:440
  85.9 0.1 add_convert_fusion.2
  86.1 0.7 collective-permute-start.25
  86.8 0.0 collective-permute-done.21
  86.8 5.9 %collective-permute-done.22.e3 = bf16[128,3584]{1,0:T(8,128)(2,1)S(1)} collective-permute-done((bf16[128,3584]{1,0:T(8,128)(2,1)S(1)}, bf16[128,3584]{1,0:T(8,128)(2,1)S(1)}, u32[]{:S(2)}, u32[]{:S(2)}) %collective-permute-start.22) | collective-permute-done | bytes 917536 | tf_op jit(solution)/shard_map/ppermute | solution.py:440
  92.6 0.1 add_convert_fusion.6
  92.7 0.1 collective-permute-start.23
  92.8 5.5 %gradient_late.1.refs_0_ = f32[2048,3584]{1,0:T(8,128)} custom-call(f32[2048,1536]{1,0:T(8,128)S(1)} %gradient_early.1.early, bf16[2048,512]{1,0:T(8,128)(2,1)S(1)} %transposed.1.q_t, bf16[128,3584]{1,0:T(8,128)(2,1)S(1)} %collective-permute-done.16.o2, bf16[128,3584]{1,0:T(8,128)(2,1)S(1)} %collective-permute-done.22.e3), custom_call_target="tpu_custom_call" | custom-call | flops 4831838208 | bytes 12582912 | tf_op jit(solution)/shard_map/gradient_late/pallas_call | solution.py:418
  98.3 0.0 collective-permute-done.19
  98.3 2.5 %collective-permute-done.23 = bf16[128,1536]{1,0:T(8,128)(2,1)S(1)} collective-permute-done((bf16[128,1536]{1,0:T(8,128)(2,1)S(1)}, bf16[128,1536]{1,0:T(8,128)(2,1)S(1)}, u32[]{:S(2)}, u32[]{:S(2)}) %collective-permute-start.23) | collective-permute-done | bytes 393248 | tf_op jit(solution)/shard_map/ppermute | solution.py:27
  100.8 0.1 add_convert_fusion.3
  101.0 1.5 %collective-permute-start.24 = (bf16[128,2048]{1,0:T(8,128)(2,1)S(1)}, bf16[128,2048]{1,0:T(8,128)(2,1)S(1)}, u32[]{:S(2)}, u32[]{:S(2)}) collective-permute-start(bf16[128,2048]{1,0:T(8,128)(2,1)S(1)} %add_convert_fusion.3), channel_id=1, source_target_pairs={{0,1},{1,0},{2,3},{3,2},{4,5},{5,4},{6,7},{7,6},{8,9},{9,8},{10,11... | collective-permute-start | bytes 1572872 | tf_op jit(solution)/shard_map/ppermute | solution.py:27
  102.4 8.1 %weight_gradient.1 = f32[2048,3584]{1,0:T(8,128)} custom-call(bf16[2048,512]{1,0:T(8,128)(2,1)S(1)} %transposed.1.q_t, bf16[128,3584]{1,0:T(8,128)(2,1)S(1)} %copy-done, bf16[128,3584]{1,0:T(8,128)(2,1)S(1)} %collective-permute-done.13.e1, bf16[128,3584]{1,0:T(8,128)(2,1)S(1)} %collective-permute-done.14.o1, ...), custom_call_target="tpu_custom_call", output_to_operand_aliasing={{}: (7, {})} | custom-call | flops 10737418240 | bytes 20971520 | tf_op jit(solution)/shard_map/weight_gradient/pallas_call | solution.py:320
  110.5 0.1 add_convert_fusion.5
  110.7 0.0 collective-permute-done.25
  110.7 1.4 %collective-permute-done.24 = bf16[128,2048]{1,0:T(8,128)(2,1)S(1)} collective-permute-done((bf16[128,2048]{1,0:T(8,128)(2,1)S(1)}, bf16[128,2048]{1,0:T(8,128)(2,1)S(1)}, u32[]{:S(2)}, u32[]{:S(2)}) %collective-permute-start.24) | collective-permute-done | bytes 524320 | tf_op jit(solution)/shard_map/ppermute | solution.py:27
  112.0 0.2 add_convert_fusion.1
  112.3 1.0 pad_maximum_fusion
  (14 shorter events, 0.1 us)
Async XLA Ops:
  0.6 1.0 copy-start.1
  1.6 0.7 copy-start.2
  2.3 6.0 %collective-permute-start = (bf16[16,2048]{1,0:T(8,128)(2,1)S(1)}, bf16[16,2048]{1,0:T(8,128)(2,1)S(1)}, u32[]{:S(2)}, u32[]{:S(2)}) collective-permute-start(bf16[16,2048]{1,0:T(8,128)(2,1)S(1)} %get-tuple-element.41), channel_id=1, source_target_pairs={{0,1},{1,0},{2,3},{3,2},{4,5},{5,4},{6,7},{7,6},{8,9},{9,8},{10,11... | collective-permute-start | bytes 196616 | tf_op jit(solution)/shard_map/ppermute | solution.py:27
  5.4 7.3 %collective-permute-start.1 = (bf16[16,2048]{1,0:T(8,128)(2,1)S(1)}, bf16[16,2048]{1,0:T(8,128)(2,1)S(1)}, u32[]{:S(2)}, u32[]{:S(2)}) collective-permute-start(bf16[16,2048]{1,0:T(8,128)(2,1)S(1)} %get-tuple-element.42), channel_id=1, source_target_pairs={{0,2},{1,3},{2,0},{3,1},{4,6},{5,7},{6,4},{7,5},{8,10},{9,11},{10,... | collective-permute-start | bytes 196616 | tf_op jit(solution)/shard_map/ppermute | solution.py:27
  8.0 6.1 %collective-permute-start.2 = (bf16[16,2048]{1,0:T(8,128)(2,1)S(1)}, bf16[16,2048]{1,0:T(8,128)(2,1)S(1)}, u32[]{:S(2)}, u32[]{:S(2)}) collective-permute-start(bf16[16,2048]{1,0:T(8,128)(2,1)S(1)} %get-tuple-element.43), channel_id=1, source_target_pairs={{0,3},{1,2},{2,1},{3,0},{4,7},{5,6},{6,5},{7,4},{8,11},{9,10},{10,... | collective-permute-start | bytes 196616 | tf_op jit(solution)/shard_map/ppermute | solution.py:27
  14.4 6.0 %collective-permute-start.4 = (bf16[16,2048]{1,0:T(8,128)(2,1)S(1)}, bf16[16,2048]{1,0:T(8,128)(2,1)S(1)}, u32[]{:S(2)}, u32[]{:S(2)}) collective-permute-start(bf16[16,2048]{1,0:T(8,128)(2,1)S(1)} %get-tuple-element.46), channel_id=1, source_target_pairs={{0,2},{1,3},{2,0},{3,1},{4,6},{5,7},{6,4},{7,5},{8,10},{9,11},{10,... | collective-permute-start | bytes 196616 | tf_op jit(solution)/shard_map/ppermute | solution.py:27
  16.1 6.1 %collective-permute-start.5 = (bf16[16,2048]{1,0:T(8,128)(2,1)S(1)}, bf16[16,2048]{1,0:T(8,128)(2,1)S(1)}, u32[]{:S(2)}, u32[]{:S(2)}) collective-permute-start(bf16[16,2048]{1,0:T(8,128)(2,1)S(1)} %get-tuple-element.47), channel_id=1, source_target_pairs={{0,3},{1,2},{2,1},{3,0},{4,7},{5,6},{6,5},{7,4},{8,11},{9,10},{10,... | collective-permute-start | bytes 196616 | tf_op jit(solution)/shard_map/ppermute | solution.py:27
  16.7 5.4 %collective-permute-start.3 = (bf16[16,2048]{1,0:T(8,128)(2,1)S(1)}, bf16[16,2048]{1,0:T(8,128)(2,1)S(1)}, u32[]{:S(2)}, u32[]{:S(2)}) collective-permute-start(bf16[16,2048]{1,0:T(8,128)(2,1)S(1)} %get-tuple-element.45), channel_id=1, source_target_pairs={{0,1},{1,0},{2,3},{3,2},{4,5},{5,4},{6,7},{7,6},{8,9},{9,8},{10,11... | collective-permute-start | bytes 196616 | tf_op jit(solution)/shard_map/ppermute | solution.py:27
  22.2 6.4 %collective-permute-start.7 = (bf16[64,2048]{1,0:T(8,128)(2,1)S(1)}, bf16[64,2048]{1,0:T(8,128)(2,1)S(1)}, u32[]{:S(2)}, u32[]{:S(2)}) collective-permute-start(bf16[64,2048]{1,0:T(8,128)(2,1)S(1)} %pad_maximum_fusion.1.refs_0_), channel_id=1, source_target_pairs={{0,8},{4,12},{8,0},{12,4},{16,24},{20,28},{24,16},{28,20},{1,9},{5... | collective-permute-start | bytes 786440 | tf_op jit(solution)/shard_map/ppermute | solution.py:27
  23.7 6.4 %collective-permute-start.8 = (bf16[64,2048]{1,0:T(8,128)(2,1)S(1)}, bf16[64,2048]{1,0:T(8,128)(2,1)S(1)}, u32[]{:S(2)}, u32[]{:S(2)}) collective-permute-start(bf16[64,2048]{1,0:T(8,128)(2,1)S(1)} %pad_maximum_fusion.1.refs_0_), channel_id=1, source_target_pairs={{0,16},{4,20},{8,24},{12,28},{16,0},{20,4},{24,8},{28,12},{1,17},{... | collective-permute-start | bytes 786440 | tf_op jit(solution)/shard_map/ppermute | solution.py:27
  25.3 21.2 %collective-permute-start.13 = (bf16[128,3584]{1,0:T(8,128)(2,1)}, bf16[128,3584]{1,0:T(8,128)(2,1)S(1)}, u32[]{:S(2)}, u32[]{:S(2)}) collective-permute-start(bf16[128,3584]{1,0:T(8,128)(2,1)} %own_ref.3), channel_id=1, source_target_pairs={{0,1},{1,0},{2,3},{3,2},{4,5},{5,4},{6,7},{7,6},{8,9},{9,8},{10,11... | collective-permute-start | bytes 2752520 | tf_op jit(solution)/shard_map/ppermute | solution.py:27
  25.4 21.1 %collective-permute-start.14 = (bf16[128,3584]{1,0:T(8,128)(2,1)}, bf16[128,3584]{1,0:T(8,128)(2,1)S(1)}, u32[]{:S(2)}, u32[]{:S(2)}) collective-permute-start(bf16[128,3584]{1,0:T(8,128)(2,1)} %own_ref.3), channel_id=1, source_target_pairs={{1,2},{2,1},{5,6},{6,5},{9,10},{10,9},{13,14},{14,13},{17,18},{18,... | collective-permute-start | bytes 2752520 | tf_op jit(solution)/shard_map/ppermute | solution.py:440
  26.1 5.6 %collective-permute-start.6 = (bf16[64,2048]{1,0:T(8,128)(2,1)S(1)}, bf16[64,2048]{1,0:T(8,128)(2,1)S(1)}, u32[]{:S(2)}, u32[]{:S(2)}) collective-permute-start(bf16[64,2048]{1,0:T(8,128)(2,1)S(1)} %pad_maximum_fusion.1.refs_0_), channel_id=1, source_target_pairs={{0,4},{4,0},{8,12},{12,8},{16,20},{20,16},{24,28},{28,24},{1,5},{5... | collective-permute-start | bytes 786440 | tf_op jit(solution)/shard_map/ppermute | solution.py:27
  30.1 6.4 %collective-permute-start.11 = (bf16[64,2048]{1,0:T(8,128)(2,1)S(1)}, bf16[64,2048]{1,0:T(8,128)(2,1)S(1)}, u32[]{:S(2)}, u32[]{:S(2)}) collective-permute-start(bf16[64,2048]{1,0:T(8,128)(2,1)S(1)} %broadcast_select_fusion), channel_id=1, source_target_pairs={{0,16},{4,12},{8,24},{12,4},{16,0},{20,28},{24,8},{28,20},{1,17},{... | collective-permute-start | bytes 786440 | tf_op jit(solution)/shard_map/ppermute | solution.py:162
  31.7 4.9 %collective-permute-start.9 = (bf16[64,2048]{1,0:T(8,128)(2,1)S(1)}, bf16[64,2048]{1,0:T(8,128)(2,1)S(1)}, u32[]{:S(2)}, u32[]{:S(2)}) collective-permute-start(bf16[64,2048]{1,0:T(8,128)(2,1)S(1)} %collective-permute-done.7.refs_2_), channel_id=1, source_target_pairs={{0,4},{4,0},{8,12},{12,8},{16,20},{20,16},{24,28},{28,24},{1,5},{5... | collective-permute-start | bytes 786440 | tf_op jit(solution)/shard_map/ppermute | solution.py:27
  31.7 4.9 %collective-permute-start.10 = (bf16[64,2048]{1,0:T(8,128)(2,1)S(1)}, bf16[64,2048]{1,0:T(8,128)(2,1)S(1)}, u32[]{:S(2)}, u32[]{:S(2)}) collective-permute-start(bf16[64,2048]{1,0:T(8,128)(2,1)S(1)} %collective-permute-done.8.refs_4_), channel_id=1, source_target_pairs={{0,4},{4,0},{8,12},{12,8},{16,20},{20,16},{24,28},{28,24},{1,5},{5... | collective-permute-start | bytes 786440 | tf_op jit(solution)/shard_map/ppermute | solution.py:27
  36.6 1.5 %collective-permute-start.12 = (bf16[64,2048]{1,0:T(8,128)(2,1)S(1)}, bf16[64,2048]{1,0:T(8,128)(2,1)S(1)}, u32[]{:S(2)}, u32[]{:S(2)}) collective-permute-start(bf16[64,2048]{1,0:T(8,128)(2,1)S(1)} %collective-permute-done.11.refs_6_), channel_id=1, source_target_pairs={{0,4},{4,0},{8,12},{12,8},{16,20},{20,16},{24,28},{28,24},{1,5},{5... | collective-permute-start | bytes 786440 | tf_op jit(solution)/shard_map/ppermute | solution.py:27
  44.1 20.1 %collective-permute-start.18 = (bf16[256,1536]{1,0:T(8,128)(2,1)S(1)}, bf16[256,1536]{1,0:T(8,128)(2,1)S(1)}, u32[]{:S(2)}, u32[]{:S(2)}) collective-permute-start(bf16[256,1536]{1,0:T(8,128)(2,1)S(1)} %get-tuple-element.57), channel_id=1, source_target_pairs={{0,1},{3,2},{4,5},{7,6},{8,9},{11,10},{12,13},{15,14},{16,17},{19,... | collective-permute-start | bytes 2359304 | tf_op jit(solution)/shard_map/ppermute | solution.py:440
  46.4 23.3 %collective-permute-start.16 = (bf16[128,3584]{1,0:T(8,128)(2,1)S(1)}, bf16[128,3584]{1,0:T(8,128)(2,1)S(1)}, u32[]{:S(2)}, u32[]{:S(2)}) collective-permute-start(bf16[128,3584]{1,0:T(8,128)(2,1)S(1)} %collective-permute-done.13.e1), channel_id=1, source_target_pairs={{1,2},{2,1},{5,6},{6,5},{9,10},{10,9},{13,14},{14,13},{17,18},{18,... | collective-permute-start | bytes 2752520 | tf_op jit(solution)/shard_map/ppermute | solution.py:440
  47.2 24.0 %collective-permute-start.17 = (bf16[128,3584]{1,0:T(8,128)(2,1)S(1)}, bf16[128,3584]{1,0:T(8,128)(2,1)S(1)}, u32[]{:S(2)}, u32[]{:S(2)}) collective-permute-start(bf16[128,3584]{1,0:T(8,128)(2,1)S(1)} %collective-permute-done.14.o1), channel_id=1, source_target_pairs={{1,0},{2,3},{5,4},{6,7},{9,8},{10,11},{13,12},{14,15},{17,16},{18,... | collective-permute-start | bytes 2752520 | tf_op jit(solution)/shard_map/ppermute | solution.py:440
  55.6 19.9 %collective-permute-start.15 = (bf16[128,2048]{1,0:T(8,128)(2,1)S(1)}, bf16[128,2048]{1,0:T(8,128)(2,1)S(1)}, u32[]{:S(2)}, u32[]{:S(2)}) collective-permute-start(bf16[128,2048]{1,0:T(8,128)(2,1)S(1)} %get-tuple-element.54), channel_id=1, source_target_pairs={{0,1},{3,2},{4,5},{7,6},{8,9},{11,10},{12,13},{15,14},{16,17},{19,... | collective-permute-start | bytes 1572872 | tf_op jit(solution)/shard_map/ppermute | solution.py:440
  64.3 21.7 %collective-permute-start.20 = (bf16[128,2048]{1,0:T(8,128)(2,1)S(1)}, bf16[128,2048]{1,0:T(8,128)(2,1)S(1)}, u32[]{:S(2)}, u32[]{:S(2)}) collective-permute-start(bf16[128,2048]{1,0:T(8,128)(2,1)S(1)} %get-tuple-element.62), channel_id=1, source_target_pairs={{0,1},{3,2},{4,5},{7,6},{8,9},{11,10},{12,13},{15,14},{16,17},{19,... | collective-permute-start | bytes 1572872 | tf_op jit(solution)/shard_map/ppermute | solution.py:440
  68.9 8.1 %copy-start = (bf16[128,3584]{1,0:T(8,128)(2,1)S(1)}, bf16[128,3584]{1,0:T(8,128)(2,1)}, u32[]{:S(2)}) copy-start(bf16[128,3584]{1,0:T(8,128)(2,1)} %own_ref.3) | copy-start | bytes 2752516
  68.9 17.9 %collective-permute-start.21 = (bf16[256,1536]{1,0:T(8,128)(2,1)S(1)}, bf16[256,1536]{1,0:T(8,128)(2,1)S(1)}, u32[]{:S(2)}, u32[]{:S(2)}) collective-permute-start(bf16[256,1536]{1,0:T(8,128)(2,1)S(1)} %add_convert_fusion), channel_id=1, source_target_pairs={{1,2},{2,1},{5,6},{6,5},{9,10},{10,9},{13,14},{14,13},{17,18},{18,... | collective-permute-start | bytes 2359304 | tf_op jit(solution)/shard_map/ppermute | solution.py:440
  71.2 21.5 %collective-permute-start.22 = (bf16[128,3584]{1,0:T(8,128)(2,1)S(1)}, bf16[128,3584]{1,0:T(8,128)(2,1)S(1)}, u32[]{:S(2)}, u32[]{:S(2)}) collective-permute-start(bf16[128,3584]{1,0:T(8,128)(2,1)S(1)} %collective-permute-done.16.o2), channel_id=1, source_target_pairs={{1,0},{2,3},{5,4},{6,7},{9,8},{10,11},{13,12},{14,15},{17,16},{18,... | collective-permute-start | bytes 2752520 | tf_op jit(solution)/shard_map/ppermute | solution.py:440
  76.2 22.1 %collective-permute-start.19 = (bf16[128,2048]{1,0:T(8,128)(2,1)S(1)}, bf16[128,2048]{1,0:T(8,128)(2,1)S(1)}, u32[]{:S(2)}, u32[]{:S(2)}) collective-permute-start(bf16[128,2048]{1,0:T(8,128)(2,1)S(1)} %add_convert_fusion.4), channel_id=1, source_target_pairs={{1,2},{2,1},{5,6},{6,5},{9,10},{10,9},{13,14},{14,13},{17,18},{18,... | collective-permute-start | bytes 1572872 | tf_op jit(solution)/shard_map/ppermute | solution.py:440
  86.1 24.6 %collective-permute-start.25 = (bf16[128,2048]{1,0:T(8,128)(2,1)S(1)}, bf16[128,2048]{1,0:T(8,128)(2,1)S(1)}, u32[]{:S(2)}, u32[]{:S(2)}) collective-permute-start(bf16[128,2048]{1,0:T(8,128)(2,1)S(1)} %add_convert_fusion.2), channel_id=1, source_target_pairs={{1,2},{2,1},{5,6},{6,5},{9,10},{10,9},{13,14},{14,13},{17,18},{18,... | collective-permute-start | bytes 1572872 | tf_op jit(solution)/shard_map/ppermute | solution.py:440
  92.7 8.1 %collective-permute-start.23 = (bf16[128,1536]{1,0:T(8,128)(2,1)S(1)}, bf16[128,1536]{1,0:T(8,128)(2,1)S(1)}, u32[]{:S(2)}, u32[]{:S(2)}) collective-permute-start(bf16[128,1536]{1,0:T(8,128)(2,1)S(1)} %add_convert_fusion.6), channel_id=1, source_target_pairs={{0,1},{1,0},{2,3},{3,2},{4,5},{5,4},{6,7},{7,6},{8,9},{9,8},{10,11... | collective-permute-start | bytes 1179656 | tf_op jit(solution)/shard_map/ppermute | solution.py:27
  101.0 11.1 %collective-permute-start.24 = (bf16[128,2048]{1,0:T(8,128)(2,1)S(1)}, bf16[128,2048]{1,0:T(8,128)(2,1)S(1)}, u32[]{:S(2)}, u32[]{:S(2)}) collective-permute-start(bf16[128,2048]{1,0:T(8,128)(2,1)S(1)} %add_convert_fusion.3), channel_id=1, source_target_pairs={{0,1},{1,0},{2,3},{3,2},{4,5},{5,4},{6,7},{7,6},{8,9},{9,8},{10,11... | collective-permute-start | bytes 1572872 | tf_op jit(solution)/shard_map/ppermute | solution.py:27

commit v2 on v1

--- a/solution.py
+++ b/solution.py
@@ -251,7 +251,7 @@
         out_specs=[pl.BlockSpec((block, tile), lambda n: (0, n)) for block in blocks],
         compiler_params=pltpu.CompilerParams(vmem_limit_bytes=48 * MIB),
         cost_estimate=pl.CostEstimate(
-            flops=2 * tokens * depth * width,
+            flops=20 * tokens * depth * width,
             bytes_accessed=2 * (tokens * depth + depth * width + tokens * width),
             transcendentals=0,
         ),
@@ -424,7 +424,7 @@
         scratch_shapes=[pltpu.VMEM((rows, width), jnp.bfloat16), pltpu.SemaphoreType.DMA],
         compiler_params=pltpu.CompilerParams(vmem_limit_bytes=16 * MIB),
         cost_estimate=pl.CostEstimate(
-            flops=12 * rows * depth * width,
+            flops=24 * rows * depth * width,
             bytes_accessed=4 * depth * width,
             transcendentals=0,
         ),
@@ -467,7 +467,7 @@
     o1 = move(up, *MIDDLE)
 
     gathered = gather_rows(own, d)
-    cut = 3 * hidden // 7 // 512 * 512
+    cut = (hidden // 512 + 1) // 2 * 512
     block = rows * len(gathered) // groups
     q, *first = project_first(gathered, weight, cut, (block, block, 2 * block))
     own_a, pair_a, beyond_a = first[0]
@@ -477,6 +477,7 @@
     own_b, pair_b, far_b, near_b = project(q, weight, cut, hidden - cut, (block,) * 4)
 
     inward_a = move(beyond_a, *INWARD)
+    inward_a, own_b = after([inward_a, own_b])
     inward_far = move(far_b, *INWARD)
     (inward_near,) = after([near_b], inward_a)
     inward_near = move(inward_near, *INWARD)

time: 114 us -> 124 us (1.088)
  waiting for transfers between devices: 41.2 us -> 49.7 us
  local copies, waits for them, and re-layouts: 1.65 us -> 3.23 us
    ppermute x10, waiting for transfers between devices: 17.6 us -> 23.8 us  [move(): return lax.ppermute(block, 'tensor', pairs)]
    ppermute x15, waiting for transfers between devices: 19.2 us -> 21.6 us  [swap(): lax.ppermute(block, axis, [(i, i ^ mask) for i in range(count) if i ^ mas...]
    unnamed x6 -> x8, local copies, waits for them, and re-layouts: 1.65 us -> 3.23 us
    pallas_call x1, Pallas kernels: 6.03 us -> 7.44 us  [project_first(): pl.pallas_call(first_kernel, out_shape=[jax.ShapeDtypeStruct((tokens, dep...]
    pallas_call x1, Pallas kernels: 7.14 us -> 5.76 us  [project(): pl.pallas_call(project_kernel, out_shape=[jax.ShapeDtypeStruct((block, wi...]
    ppermute x10, starting transfers between devices: 19.4 us -> 20.7 us  [move(): return lax.ppermute(block, 'tensor', pairs)]
  transfers between devices with their start and end apart: 26 -> 26, of which waited for: 15 -> 12; matrix products, arithmetic and copies ran while one was open for 1% -> 1% of each run, Pallas kernels for 28% -> 25%
where the time goes in v2:
time: 124 us
  waiting for transfers between devices  49.7 us (40%)
  starting transfers between devices  35.7 us (29%)
  Pallas kernels  31.6 us (25%)
  local copies, waits for them, and re-layouts  3.23 us (3%)
  other arithmetic  2.58 us (2%)
    ppermute x10, waiting for transfers between devices, move(): return lax.ppermute(block, 'tensor', pairs)  23.8 us
    ppermute x15, waiting for transfers between devices, swap(): lax.ppermute(block, axis, [(i, i ^ mask) for i in range(count) if i ^ mas...  21.6 us
    ppermute x10, starting transfers between devices, move(): return lax.ppermute(block, 'tensor', pairs)  20.7 us
    ppermute x15, starting transfers between devices, swap(): lax.ppermute(block, axis, [(i, i ^ mask) for i in range(count) if i ^ mas...  13.4 us
    pallas_call x1, Pallas kernels, weight_gradient(): pl.pallas_call(functools.partial(grad_kernel, tile, start), out_shape=jax...  8.15 us
    pallas_call x1, Pallas kernels, project_first(): pl.pallas_call(first_kernel, out_shape=[jax.ShapeDtypeStruct((tokens, dep...  7.44 us
    pallas_call x1, Pallas kernels, project(): pl.pallas_call(project_kernel, out_shape=[jax.ShapeDtypeStruct((block, wi...  5.76 us
    pallas_call x1, Pallas kernels, gradient_late(): pl.pallas_call(functools.partial(late_kernel, tile), out_shape=jax.ShapeD...  5.44 us
  transfers between devices with their start and end apart: 26, of which 12 were waited for; matrix products, arithmetic and copies ran while one was open for 1% of the time, Pallas kernels for 25%

profile of v2, /device:TPU:0, one launch (start us, length us, event | category | flops | bytes accessed | tf_op | source)
XLA Modules:
  0.0 123.8 jit_solution(3675700652744796703)
XLA Ops:
  0.6 0.9 copy-done.2
  1.6 0.7 copy-done.3
  2.3 0.1 signed_pieces.1
  2.3 3.1 %collective-permute-start = (bf16[16,2048]{1,0:T(8,128)(2,1)S(1)}, bf16[16,2048]{1,0:T(8,128)(2,1)S(1)}, u32[]{:S(2)}, u32[]{:S(2)}) collective-permute-start(bf16[16,2048]{1,0:T(8,128)(2,1)S(1)} %get-tuple-element.43), channel_id=1, source_target_pairs={{0,1},{1,0},{2,3},{3,2},{4,5},{5,4},{6,7},{7,6},{8,9},{9,8},{10,11... | collective-permute-start | bytes 196616 | tf_op jit(solution)/shard_map/ppermute | solution.py:27
  5.4 2.6 %collective-permute-start.1 = (bf16[16,2048]{1,0:T(8,128)(2,1)S(1)}, bf16[16,2048]{1,0:T(8,128)(2,1)S(1)}, u32[]{:S(2)}, u32[]{:S(2)}) collective-permute-start(bf16[16,2048]{1,0:T(8,128)(2,1)S(1)} %get-tuple-element.44), channel_id=1, source_target_pairs={{0,2},{1,3},{2,0},{3,1},{4,6},{5,7},{6,4},{7,5},{8,10},{9,11},{10,... | collective-permute-start | bytes 196616 | tf_op jit(solution)/shard_map/ppermute | solution.py:27
  8.0 0.3 fusion.3.h_ref
  8.4 0.0 collective-permute-done.refs_1_
  8.4 4.3 %collective-permute-done.1.refs_2_ = bf16[16,2048]{1,0:T(8,128)(2,1)S(1)} collective-permute-done((bf16[16,2048]{1,0:T(8,128)(2,1)S(1)}, bf16[16,2048]{1,0:T(8,128)(2,1)S(1)}, u32[]{:S(2)}, u32[]{:S(2)}) %collective-permute-start.1) | collective-permute-done | bytes 65568 | tf_op jit(solution)/shard_map/ppermute | solution.py:27
  12.7 1.4 %collective-permute-done.2.refs_3_ = bf16[16,2048]{1,0:T(8,128)(2,1)S(1)} collective-permute-done((bf16[16,2048]{1,0:T(8,128)(2,1)S(1)}, bf16[16,2048]{1,0:T(8,128)(2,1)S(1)}, u32[]{:S(2)}, u32[]{:S(2)}) %collective-permute-start.2) | collective-permute-done | bytes 65568 | tf_op jit(solution)/shard_map/ppermute | solution.py:27
  14.1 0.3 rotate.1
  14.4 1.6 %collective-permute-start.4 = (bf16[16,2048]{1,0:T(8,128)(2,1)S(1)}, bf16[16,2048]{1,0:T(8,128)(2,1)S(1)}, u32[]{:S(2)}, u32[]{:S(2)}) collective-permute-start(bf16[16,2048]{1,0:T(8,128)(2,1)S(1)} %get-tuple-element.48), channel_id=1, source_target_pairs={{0,2},{1,3},{2,0},{3,1},{4,6},{5,7},{6,4},{7,5},{8,10},{9,11},{10,... | collective-permute-start | bytes 196616 | tf_op jit(solution)/shard_map/ppermute | solution.py:27
  16.1 0.7 collective-permute-start.5
  16.7 1.2 %collective-permute-start.3 = (bf16[16,2048]{1,0:T(8,128)(2,1)S(1)}, bf16[16,2048]{1,0:T(8,128)(2,1)S(1)}, u32[]{:S(2)}, u32[]{:S(2)}) collective-permute-start(bf16[16,2048]{1,0:T(8,128)(2,1)S(1)} %get-tuple-element.47), channel_id=1, source_target_pairs={{0,1},{1,0},{2,3},{3,2},{4,5},{5,4},{6,7},{7,6},{8,9},{9,8},{10,11... | collective-permute-start | bytes 196616 | tf_op jit(solution)/shard_map/ppermute | solution.py:27
  18.0 2.4 %collective-permute-done.4 = bf16[16,2048]{1,0:T(8,128)(2,1)S(1)} collective-permute-done((bf16[16,2048]{1,0:T(8,128)(2,1)S(1)}, bf16[16,2048]{1,0:T(8,128)(2,1)S(1)}, u32[]{:S(2)}, u32[]{:S(2)}) %collective-permute-start.4) | collective-permute-done | bytes 65568 | tf_op jit(solution)/shard_map/ppermute | solution.py:27
  20.4 1.7 %collective-permute-done.5 = bf16[16,2048]{1,0:T(8,128)(2,1)S(1)} collective-permute-done((bf16[16,2048]{1,0:T(8,128)(2,1)S(1)}, bf16[16,2048]{1,0:T(8,128)(2,1)S(1)}, u32[]{:S(2)}, u32[]{:S(2)}) %collective-permute-start.5) | collective-permute-done | bytes 65568 | tf_op jit(solution)/shard_map/ppermute | solution.py:27
  22.1 0.0 collective-permute-done.3
  22.2 1.5 %collective-permute-start.7 = (bf16[64,2048]{1,0:T(8,128)(2,1)S(1)}, bf16[64,2048]{1,0:T(8,128)(2,1)S(1)}, u32[]{:S(2)}, u32[]{:S(2)}) collective-permute-start(bf16[64,2048]{1,0:T(8,128)(2,1)S(1)} %pad_maximum_fusion.1.refs_0_), channel_id=1, source_target_pairs={{0,8},{4,12},{8,0},{12,4},{16,24},{20,28},{24,16},{28,20},{1,9},{5... | collective-permute-start | bytes 786440 | tf_op jit(solution)/shard_map/ppermute | solution.py:27
  23.7 1.5 %collective-permute-start.8 = (bf16[64,2048]{1,0:T(8,128)(2,1)S(1)}, bf16[64,2048]{1,0:T(8,128)(2,1)S(1)}, u32[]{:S(2)}, u32[]{:S(2)}) collective-permute-start(bf16[64,2048]{1,0:T(8,128)(2,1)S(1)} %pad_maximum_fusion.1.refs_0_), channel_id=1, source_target_pairs={{0,16},{4,20},{8,24},{12,28},{16,0},{20,4},{24,8},{28,12},{1,17},{... | collective-permute-start | bytes 786440 | tf_op jit(solution)/shard_map/ppermute | solution.py:27
  25.3 0.1 collective-permute-start.13
  25.4 0.7 collective-permute-start.14
  26.1 0.1 collective-permute-start.6
  26.2 2.5 %collective-permute-done.7.refs_2_ = bf16[64,2048]{1,0:T(8,128)(2,1)S(1)} collective-permute-done((bf16[64,2048]{1,0:T(8,128)(2,1)S(1)}, bf16[64,2048]{1,0:T(8,128)(2,1)S(1)}, u32[]{:S(2)}, u32[]{:S(2)}) %collective-permute-start.7) | collective-permute-done | bytes 262176 | tf_op jit(solution)/shard_map/ppermute | solution.py:27
  28.6 1.5 %collective-permute-done.8.refs_4_ = bf16[64,2048]{1,0:T(8,128)(2,1)S(1)} collective-permute-done((bf16[64,2048]{1,0:T(8,128)(2,1)S(1)}, bf16[64,2048]{1,0:T(8,128)(2,1)S(1)}, u32[]{:S(2)}, u32[]{:S(2)}) %collective-permute-start.8) | collective-permute-done | bytes 262176 | tf_op jit(solution)/shard_map/ppermute | solution.py:27
  30.1 1.6 %collective-permute-start.11 = (bf16[64,2048]{1,0:T(8,128)(2,1)S(1)}, bf16[64,2048]{1,0:T(8,128)(2,1)S(1)}, u32[]{:S(2)}, u32[]{:S(2)}) collective-permute-start(bf16[64,2048]{1,0:T(8,128)(2,1)S(1)} %broadcast_select_fusion), channel_id=1, source_target_pairs={{0,16},{4,12},{8,24},{12,4},{16,0},{20,28},{24,8},{28,20},{1,17},{... | collective-permute-start | bytes 786440 | tf_op jit(solution)/shard_map/ppermute | solution.py:162
  31.7 0.0 collective-permute-start.9
  31.7 0.0 collective-permute-done.6.refs_1_
  31.7 0.5 collective-permute-start.10
  32.2 4.3 %collective-permute-done.11.refs_6_ = bf16[64,2048]{1,0:T(8,128)(2,1)S(1)} collective-permute-done((bf16[64,2048]{1,0:T(8,128)(2,1)S(1)}, bf16[64,2048]{1,0:T(8,128)(2,1)S(1)}, u32[]{:S(2)}, u32[]{:S(2)}) %collective-permute-start.11) | collective-permute-done | bytes 262176 | tf_op jit(solution)/shard_map/ppermute | solution.py:162
  36.6 0.0 collective-permute-start.12
  36.6 0.0 collective-permute-done.9.refs_3_
  36.6 0.0 collective-permute-done.10.refs_5_
  36.6 1.5 %collective-permute-done.12.refs_7_ = bf16[64,2048]{1,0:T(8,128)(2,1)S(1)} collective-permute-done((bf16[64,2048]{1,0:T(8,128)(2,1)S(1)}, bf16[64,2048]{1,0:T(8,128)(2,1)S(1)}, u32[]{:S(2)}, u32[]{:S(2)}) %collective-permute-start.12) | collective-permute-done | bytes 262176 | tf_op jit(solution)/shard_map/ppermute | solution.py:27
  38.1 7.4 %project_first.1 = (bf16[512,2048]{1,0:T(8,128)(2,1)}, bf16[128,2048]{1,0:T(8,128)(2,1)S(1)}, bf16[128,2048]{1,0:T(8,128)(2,1)S(1)}, bf16[256,2048]{1,0:T(8,128)(2,1)S(1)}) custom-call(bf16[64,2048]{1,0:T(8,128)(2,1)S(1)} %pad_maximum_fusion.1.refs_0_, bf16[64,2048]{1,0:T(8,128)(2,1)S(1)} %collective-permute-done.6.refs_1_, ...), custom_call_target="tpu_custom_call" | custom-call | flops 1 | bytes 1 | tf_op jit(solution)/shard_map/project_first/pallas_call | solution.py:221
  45.6 2.3 %collective-permute-start.18 = (bf16[256,2048]{1,0:T(8,128)(2,1)S(1)}, bf16[256,2048]{1,0:T(8,128)(2,1)S(1)}, u32[]{:S(2)}, u32[]{:S(2)}) collective-permute-start(bf16[256,2048]{1,0:T(8,128)(2,1)S(1)} %get-tuple-element.59), channel_id=1, source_target_pairs={{0,1},{3,2},{4,5},{7,6},{8,9},{11,10},{12,13},{15,14},{16,17},{19,... | collective-permute-start | bytes 3145736 | tf_op jit(solution)/shard_map/ppermute | solution.py:440
  47.9 0.7 collective-permute-start.16
  48.6 1.3 %collective-permute-start.17 = (bf16[128,3584]{1,0:T(8,128)(2,1)S(1)}, bf16[128,3584]{1,0:T(8,128)(2,1)S(1)}, u32[]{:S(2)}, u32[]{:S(2)}) collective-permute-start(bf16[128,3584]{1,0:T(8,128)(2,1)S(1)} %collective-permute-done.14.o1), channel_id=1, source_target_pairs={{1,0},{2,3},{5,4},{6,7},{9,8},{10,11},{13,12},{14,15},{17,16},{18,... | collective-permute-start | bytes 2752520 | tf_op jit(solution)/shard_map/ppermute | solution.py:440
  49.9 0.0 copy-start.1
  49.9 1.6 %copy-done.1 = bf16[512,2048]{1,0:T(8,128)(2,1)S(1)} copy-done((bf16[512,2048]{1,0:T(8,128)(2,1)S(1)}, bf16[512,2048]{1,0:T(8,128)(2,1)}, u32[]{:S(2)}) %copy-start.1) | copy-done | bytes 2097176
  51.5 5.8 %project.1 = (bf16[128,1536]{1,0:T(8,128)(2,1)S(1)}, bf16[128,1536]{1,0:T(8,128)(2,1)S(1)}, bf16[128,1536]{1,0:T(8,128)(2,1)S(1)}, bf16[128,1536]{1,0:T(8,128)(2,1)S(1)}) custom-call(bf16[512,2048]{1,0:T(8,128)(2,1)S(1)} %copy-done.1, bf16[2048,3584]{1,0:T(8,128)(2,1)} %w_ref.1), custom_call_target="tpu_custom_call" | custom-call | flops 32212254720 | bytes 9961472 | tf_op jit(solution)/shard_map/project/pallas_call | solution.py:243
  57.3 5.1 %collective-permute-start.15 = (bf16[128,1536]{1,0:T(8,128)(2,1)S(1)}, bf16[128,1536]{1,0:T(8,128)(2,1)S(1)}, u32[]{:S(2)}, u32[]{:S(2)}) collective-permute-start(bf16[128,1536]{1,0:T(8,128)(2,1)S(1)} %get-tuple-element.56), channel_id=1, source_target_pairs={{0,1},{3,2},{4,5},{7,6},{8,9},{11,10},{12,13},{15,14},{16,17},{19,... | collective-permute-start | bytes 1179656 | tf_op jit(solution)/shard_map/ppermute | solution.py:440
  62.3 9.0 %collective-permute-done.18 = bf16[256,2048]{1,0:T(8,128)(2,1)S(1)} collective-permute-done((bf16[256,2048]{1,0:T(8,128)(2,1)S(1)}, bf16[256,2048]{1,0:T(8,128)(2,1)S(1)}, u32[]{:S(2)}, u32[]{:S(2)}) %collective-permute-start.18) | collective-permute-done | bytes 1048608 | tf_op jit(solution)/shard_map/ppermute | solution.py:440
  71.3 0.4 add_convert_fusion
  71.7 0.7 collective-permute-start.21
  72.4 0.0 copy-start
  72.4 7.2 %collective-permute-start.20 = (bf16[128,1536]{1,0:T(8,128)(2,1)S(1)}, bf16[128,1536]{1,0:T(8,128)(2,1)S(1)}, u32[]{:S(2)}, u32[]{:S(2)}) collective-permute-start(bf16[128,1536]{1,0:T(8,128)(2,1)S(1)} %get-tuple-element.66), channel_id=1, source_target_pairs={{0,1},{3,2},{4,5},{7,6},{8,9},{11,10},{12,13},{15,14},{16,17},{19,... | collective-permute-start | bytes 1179656 | tf_op jit(solution)/shard_map/ppermute | solution.py:440
  79.7 1.3 %collective-permute-start.22 = (bf16[128,3584]{1,0:T(8,128)(2,1)S(1)}, bf16[128,3584]{1,0:T(8,128)(2,1)S(1)}, u32[]{:S(2)}, u32[]{:S(2)}) collective-permute-start(bf16[128,3584]{1,0:T(8,128)(2,1)S(1)} %collective-permute-done.16.o2), channel_id=1, source_target_pairs={{1,0},{2,3},{5,4},{6,7},{9,8},{10,11},{13,12},{14,15},{17,16},{18,... | collective-permute-start | bytes 2752520 | tf_op jit(solution)/shard_map/ppermute | solution.py:440
  81.0 0.6 transposed.1.q_t
  81.6 0.1 add_convert_fusion.6
  81.7 0.7 collective-permute-start.19
  82.4 3.8 %gradient_early.1.early = f32[2048,1536]{1,0:T(8,128)S(1)} custom-call(bf16[2048,512]{1,0:T(8,128)(2,1)S(1)} %transposed.1.q_t, bf16[128,3584]{1,0:T(8,128)(2,1)S(1)} %copy-done, bf16[128,3584]{1,0:T(8,128)(2,1)S(1)} %collective-permute-done.13.e1, bf16[128,3584]{1,0:T(8,128)(2,1)S(1)} %collective-permute-done.14.o1, ...), custom_call_target="tpu_custom_call" | custom-call | flops 1 | bytes 1 | tf_op jit(solution)/shard_map/gradient_early/pallas_call | solution.py:375
  86.3 1.1 collective-permute-done.20
  87.3 0.1 add_convert_fusion.4
  87.4 0.7 collective-permute-start.25
  88.1 13.8 %collective-permute-done.22.e3 = bf16[128,3584]{1,0:T(8,128)(2,1)S(1)} collective-permute-done((bf16[128,3584]{1,0:T(8,128)(2,1)S(1)}, bf16[128,3584]{1,0:T(8,128)(2,1)S(1)}, u32[]{:S(2)}, u32[]{:S(2)}) %collective-permute-start.22) | collective-permute-done | bytes 917536 | tf_op jit(solution)/shard_map/ppermute | solution.py:440
  101.9 0.1 add_convert_fusion.2
  102.0 0.3 collective-permute-start.23
  102.3 5.4 %gradient_late.1.refs_0_ = f32[2048,3584]{1,0:T(8,128)} custom-call(f32[2048,1536]{1,0:T(8,128)S(1)} %gradient_early.1.early, bf16[2048,512]{1,0:T(8,128)(2,1)S(1)} %transposed.1.q_t, bf16[128,3584]{1,0:T(8,128)(2,1)S(1)} %collective-permute-done.16.o2, bf16[128,3584]{1,0:T(8,128)(2,1)S(1)} %collective-permute-done.22.e3), custom_call_target="tpu_custom_call" | custom-call | flops 9663676416 | bytes 12582912 | tf_op jit(solution)/shard_map/gradient_late/pallas_call | solution.py:418
  107.8 6.2 %collective-permute-done.23 = bf16[128,2048]{1,0:T(8,128)(2,1)S(1)} collective-permute-done((bf16[128,2048]{1,0:T(8,128)(2,1)S(1)}, bf16[128,2048]{1,0:T(8,128)(2,1)S(1)}, u32[]{:S(2)}, u32[]{:S(2)}) %collective-permute-start.23) | collective-permute-done | bytes 524320 | tf_op jit(solution)/shard_map/ppermute | solution.py:27
  114.0 0.1 add_convert_fusion.5
  114.1 0.1 collective-permute-start.24
  114.2 8.2 %weight_gradient.1 = f32[2048,3584]{1,0:T(8,128)} custom-call(bf16[2048,512]{1,0:T(8,128)(2,1)S(1)} %transposed.1.q_t, bf16[128,3584]{1,0:T(8,128)(2,1)S(1)} %copy-done, bf16[128,3584]{1,0:T(8,128)(2,1)S(1)} %collective-permute-done.13.e1, bf16[128,3584]{1,0:T(8,128)(2,1)S(1)} %collective-permute-done.14.o1, ...), custom_call_target="tpu_custom_call", output_to_operand_aliasing={{}: (7, {})} | custom-call | flops 10737418240 | bytes 20971520 | tf_op jit(solution)/shard_map/weight_gradient/pallas_call | solution.py:320
  122.4 0.2 add_convert_fusion.1
  122.6 0.1 add_convert_fusion.3
  122.8 1.0 pad_maximum_fusion
  (16 shorter events, 0.1 us)
Async XLA Ops:
  0.6 1.0 copy-start.2
  1.6 0.7 copy-start.3
  2.3 6.0 %collective-permute-start = (bf16[16,2048]{1,0:T(8,128)(2,1)S(1)}, bf16[16,2048]{1,0:T(8,128)(2,1)S(1)}, u32[]{:S(2)}, u32[]{:S(2)}) collective-permute-start(bf16[16,2048]{1,0:T(8,128)(2,1)S(1)} %get-tuple-element.43), channel_id=1, source_target_pairs={{0,1},{1,0},{2,3},{3,2},{4,5},{5,4},{6,7},{7,6},{8,9},{9,8},{10,11... | collective-permute-start | bytes 196616 | tf_op jit(solution)/shard_map/ppermute | solution.py:27
  5.4 7.3 %collective-permute-start.1 = (bf16[16,2048]{1,0:T(8,128)(2,1)S(1)}, bf16[16,2048]{1,0:T(8,128)(2,1)S(1)}, u32[]{:S(2)}, u32[]{:S(2)}) collective-permute-start(bf16[16,2048]{1,0:T(8,128)(2,1)S(1)} %get-tuple-element.44), channel_id=1, source_target_pairs={{0,2},{1,3},{2,0},{3,1},{4,6},{5,7},{6,4},{7,5},{8,10},{9,11},{10,... | collective-permute-start | bytes 196616 | tf_op jit(solution)/shard_map/ppermute | solution.py:27
  8.0 6.1 %collective-permute-start.2 = (bf16[16,2048]{1,0:T(8,128)(2,1)S(1)}, bf16[16,2048]{1,0:T(8,128)(2,1)S(1)}, u32[]{:S(2)}, u32[]{:S(2)}) collective-permute-start(bf16[16,2048]{1,0:T(8,128)(2,1)S(1)} %get-tuple-element.45), channel_id=1, source_target_pairs={{0,3},{1,2},{2,1},{3,0},{4,7},{5,6},{6,5},{7,4},{8,11},{9,10},{10,... | collective-permute-start | bytes 196616 | tf_op jit(solution)/shard_map/ppermute | solution.py:27
  14.4 6.0 %collective-permute-start.4 = (bf16[16,2048]{1,0:T(8,128)(2,1)S(1)}, bf16[16,2048]{1,0:T(8,128)(2,1)S(1)}, u32[]{:S(2)}, u32[]{:S(2)}) collective-permute-start(bf16[16,2048]{1,0:T(8,128)(2,1)S(1)} %get-tuple-element.48), channel_id=1, source_target_pairs={{0,2},{1,3},{2,0},{3,1},{4,6},{5,7},{6,4},{7,5},{8,10},{9,11},{10,... | collective-permute-start | bytes 196616 | tf_op jit(solution)/shard_map/ppermute | solution.py:27
  16.1 6.1 %collective-permute-start.5 = (bf16[16,2048]{1,0:T(8,128)(2,1)S(1)}, bf16[16,2048]{1,0:T(8,128)(2,1)S(1)}, u32[]{:S(2)}, u32[]{:S(2)}) collective-permute-start(bf16[16,2048]{1,0:T(8,128)(2,1)S(1)} %get-tuple-element.49), channel_id=1, source_target_pairs={{0,3},{1,2},{2,1},{3,0},{4,7},{5,6},{6,5},{7,4},{8,11},{9,10},{10,... | collective-permute-start | bytes 196616 | tf_op jit(solution)/shard_map/ppermute | solution.py:27
  16.7 5.4 %collective-permute-start.3 = (bf16[16,2048]{1,0:T(8,128)(2,1)S(1)}, bf16[16,2048]{1,0:T(8,128)(2,1)S(1)}, u32[]{:S(2)}, u32[]{:S(2)}) collective-permute-start(bf16[16,2048]{1,0:T(8,128)(2,1)S(1)} %get-tuple-element.47), channel_id=1, source_target_pairs={{0,1},{1,0},{2,3},{3,2},{4,5},{5,4},{6,7},{7,6},{8,9},{9,8},{10,11... | collective-permute-start | bytes 196616 | tf_op jit(solution)/shard_map/ppermute | solution.py:27
  22.2 6.4 %collective-permute-start.7 = (bf16[64,2048]{1,0:T(8,128)(2,1)S(1)}, bf16[64,2048]{1,0:T(8,128)(2,1)S(1)}, u32[]{:S(2)}, u32[]{:S(2)}) collective-permute-start(bf16[64,2048]{1,0:T(8,128)(2,1)S(1)} %pad_maximum_fusion.1.refs_0_), channel_id=1, source_target_pairs={{0,8},{4,12},{8,0},{12,4},{16,24},{20,28},{24,16},{28,20},{1,9},{5... | collective-permute-start | bytes 786440 | tf_op jit(solution)/shard_map/ppermute | solution.py:27
  23.7 6.4 %collective-permute-start.8 = (bf16[64,2048]{1,0:T(8,128)(2,1)S(1)}, bf16[64,2048]{1,0:T(8,128)(2,1)S(1)}, u32[]{:S(2)}, u32[]{:S(2)}) collective-permute-start(bf16[64,2048]{1,0:T(8,128)(2,1)S(1)} %pad_maximum_fusion.1.refs_0_), channel_id=1, source_target_pairs={{0,16},{4,20},{8,24},{12,28},{16,0},{20,4},{24,8},{28,12},{1,17},{... | collective-permute-start | bytes 786440 | tf_op jit(solution)/shard_map/ppermute | solution.py:27
  25.3 22.6 %collective-permute-start.13 = (bf16[128,3584]{1,0:T(8,128)(2,1)}, bf16[128,3584]{1,0:T(8,128)(2,1)S(1)}, u32[]{:S(2)}, u32[]{:S(2)}) collective-permute-start(bf16[128,3584]{1,0:T(8,128)(2,1)} %own_ref.3), channel_id=1, source_target_pairs={{0,1},{1,0},{2,3},{3,2},{4,5},{5,4},{6,7},{7,6},{8,9},{9,8},{10,11... | collective-permute-start | bytes 2752520 | tf_op jit(solution)/shard_map/ppermute | solution.py:27
  25.4 22.5 %collective-permute-start.14 = (bf16[128,3584]{1,0:T(8,128)(2,1)}, bf16[128,3584]{1,0:T(8,128)(2,1)S(1)}, u32[]{:S(2)}, u32[]{:S(2)}) collective-permute-start(bf16[128,3584]{1,0:T(8,128)(2,1)} %own_ref.3), channel_id=1, source_target_pairs={{1,2},{2,1},{5,6},{6,5},{9,10},{10,9},{13,14},{14,13},{17,18},{18,... | collective-permute-start | bytes 2752520 | tf_op jit(solution)/shard_map/ppermute | solution.py:440
  26.1 5.6 %collective-permute-start.6 = (bf16[64,2048]{1,0:T(8,128)(2,1)S(1)}, bf16[64,2048]{1,0:T(8,128)(2,1)S(1)}, u32[]{:S(2)}, u32[]{:S(2)}) collective-permute-start(bf16[64,2048]{1,0:T(8,128)(2,1)S(1)} %pad_maximum_fusion.1.refs_0_), channel_id=1, source_target_pairs={{0,4},{4,0},{8,12},{12,8},{16,20},{20,16},{24,28},{28,24},{1,5},{5... | collective-permute-start | bytes 786440 | tf_op jit(solution)/shard_map/ppermute | solution.py:27
  30.1 6.4 %collective-permute-start.11 = (bf16[64,2048]{1,0:T(8,128)(2,1)S(1)}, bf16[64,2048]{1,0:T(8,128)(2,1)S(1)}, u32[]{:S(2)}, u32[]{:S(2)}) collective-permute-start(bf16[64,2048]{1,0:T(8,128)(2,1)S(1)} %broadcast_select_fusion), channel_id=1, source_target_pairs={{0,16},{4,12},{8,24},{12,4},{16,0},{20,28},{24,8},{28,20},{1,17},{... | collective-permute-start | bytes 786440 | tf_op jit(solution)/shard_map/ppermute | solution.py:162
  31.7 4.9 %collective-permute-start.9 = (bf16[64,2048]{1,0:T(8,128)(2,1)S(1)}, bf16[64,2048]{1,0:T(8,128)(2,1)S(1)}, u32[]{:S(2)}, u32[]{:S(2)}) collective-permute-start(bf16[64,2048]{1,0:T(8,128)(2,1)S(1)} %collective-permute-done.7.refs_2_), channel_id=1, source_target_pairs={{0,4},{4,0},{8,12},{12,8},{16,20},{20,16},{24,28},{28,24},{1,5},{5... | collective-permute-start | bytes 786440 | tf_op jit(solution)/shard_map/ppermute | solution.py:27
  31.7 4.9 %collective-permute-start.10 = (bf16[64,2048]{1,0:T(8,128)(2,1)S(1)}, bf16[64,2048]{1,0:T(8,128)(2,1)S(1)}, u32[]{:S(2)}, u32[]{:S(2)}) collective-permute-start(bf16[64,2048]{1,0:T(8,128)(2,1)S(1)} %collective-permute-done.8.refs_4_), channel_id=1, source_target_pairs={{0,4},{4,0},{8,12},{12,8},{16,20},{20,16},{24,28},{28,24},{1,5},{5... | collective-permute-start | bytes 786440 | tf_op jit(solution)/shard_map/ppermute | solution.py:27
  36.6 1.5 %collective-permute-start.12 = (bf16[64,2048]{1,0:T(8,128)(2,1)S(1)}, bf16[64,2048]{1,0:T(8,128)(2,1)S(1)}, u32[]{:S(2)}, u32[]{:S(2)}) collective-permute-start(bf16[64,2048]{1,0:T(8,128)(2,1)S(1)} %collective-permute-done.11.refs_6_), channel_id=1, source_target_pairs={{0,4},{4,0},{8,12},{12,8},{16,20},{20,16},{24,28},{28,24},{1,5},{5... | collective-permute-start | bytes 786440 | tf_op jit(solution)/shard_map/ppermute | solution.py:27
  45.6 25.7 %collective-permute-start.18 = (bf16[256,2048]{1,0:T(8,128)(2,1)S(1)}, bf16[256,2048]{1,0:T(8,128)(2,1)S(1)}, u32[]{:S(2)}, u32[]{:S(2)}) collective-permute-start(bf16[256,2048]{1,0:T(8,128)(2,1)S(1)} %get-tuple-element.59), channel_id=1, source_target_pairs={{0,1},{3,2},{4,5},{7,6},{8,9},{11,10},{12,13},{15,14},{16,17},{19,... | collective-permute-start | bytes 3145736 | tf_op jit(solution)/shard_map/ppermute | solution.py:440
  47.9 31.8 %collective-permute-start.16 = (bf16[128,3584]{1,0:T(8,128)(2,1)S(1)}, bf16[128,3584]{1,0:T(8,128)(2,1)S(1)}, u32[]{:S(2)}, u32[]{:S(2)}) collective-permute-start(bf16[128,3584]{1,0:T(8,128)(2,1)S(1)} %collective-permute-done.13.e1), channel_id=1, source_target_pairs={{1,2},{2,1},{5,6},{6,5},{9,10},{10,9},{13,14},{14,13},{17,18},{18,... | collective-permute-start | bytes 2752520 | tf_op jit(solution)/shard_map/ppermute | solution.py:440
  48.6 31.1 %collective-permute-start.17 = (bf16[128,3584]{1,0:T(8,128)(2,1)S(1)}, bf16[128,3584]{1,0:T(8,128)(2,1)S(1)}, u32[]{:S(2)}, u32[]{:S(2)}) collective-permute-start(bf16[128,3584]{1,0:T(8,128)(2,1)S(1)} %collective-permute-done.14.o1), channel_id=1, source_target_pairs={{1,0},{2,3},{5,4},{6,7},{9,8},{10,11},{13,12},{14,15},{17,16},{18,... | collective-permute-start | bytes 2752520 | tf_op jit(solution)/shard_map/ppermute | solution.py:440
  49.9 1.6 %copy-start.1 = (bf16[512,2048]{1,0:T(8,128)(2,1)S(1)}, bf16[512,2048]{1,0:T(8,128)(2,1)}, u32[]{:S(2)}) copy-start(bf16[512,2048]{1,0:T(8,128)(2,1)} %get-tuple-element.67.q_ref) | copy-start | bytes 6291460
  57.3 23.7 %collective-permute-start.15 = (bf16[128,1536]{1,0:T(8,128)(2,1)S(1)}, bf16[128,1536]{1,0:T(8,128)(2,1)S(1)}, u32[]{:S(2)}, u32[]{:S(2)}) collective-permute-start(bf16[128,1536]{1,0:T(8,128)(2,1)S(1)} %get-tuple-element.56), channel_id=1, source_target_pairs={{0,1},{3,2},{4,5},{7,6},{8,9},{11,10},{12,13},{15,14},{16,17},{19,... | collective-permute-start | bytes 1179656 | tf_op jit(solution)/shard_map/ppermute | solution.py:440
  71.7 30.2 %collective-permute-start.21 = (bf16[256,2048]{1,0:T(8,128)(2,1)S(1)}, bf16[256,2048]{1,0:T(8,128)(2,1)S(1)}, u32[]{:S(2)}, u32[]{:S(2)}) collective-permute-start(bf16[256,2048]{1,0:T(8,128)(2,1)S(1)} %add_convert_fusion), channel_id=1, source_target_pairs={{1,2},{2,1},{5,6},{6,5},{9,10},{10,9},{13,14},{14,13},{17,18},{18,... | collective-permute-start | bytes 3145736 | tf_op jit(solution)/shard_map/ppermute | solution.py:440
  72.4 10.0 %copy-start = (bf16[128,3584]{1,0:T(8,128)(2,1)S(1)}, bf16[128,3584]{1,0:T(8,128)(2,1)}, u32[]{:S(2)}) copy-start(bf16[128,3584]{1,0:T(8,128)(2,1)} %own_ref.3) | copy-start | bytes 2752516
  72.4 14.9 %collective-permute-start.20 = (bf16[128,1536]{1,0:T(8,128)(2,1)S(1)}, bf16[128,1536]{1,0:T(8,128)(2,1)S(1)}, u32[]{:S(2)}, u32[]{:S(2)}) collective-permute-start(bf16[128,1536]{1,0:T(8,128)(2,1)S(1)} %get-tuple-element.66), channel_id=1, source_target_pairs={{0,1},{3,2},{4,5},{7,6},{8,9},{11,10},{12,13},{15,14},{16,17},{19,... | collective-permute-start | bytes 1179656 | tf_op jit(solution)/shard_map/ppermute | solution.py:440
  79.7 22.2 %collective-permute-start.22 = (bf16[128,3584]{1,0:T(8,128)(2,1)S(1)}, bf16[128,3584]{1,0:T(8,128)(2,1)S(1)}, u32[]{:S(2)}, u32[]{:S(2)}) collective-permute-start(bf16[128,3584]{1,0:T(8,128)(2,1)S(1)} %collective-permute-done.16.o2), channel_id=1, source_target_pairs={{1,0},{2,3},{5,4},{6,7},{9,8},{10,11},{13,12},{14,15},{17,16},{18,... | collective-permute-start | bytes 2752520 | tf_op jit(solution)/shard_map/ppermute | solution.py:440
  81.7 26.1 %collective-permute-start.19 = (bf16[128,1536]{1,0:T(8,128)(2,1)S(1)}, bf16[128,1536]{1,0:T(8,128)(2,1)S(1)}, u32[]{:S(2)}, u32[]{:S(2)}) collective-permute-start(bf16[128,1536]{1,0:T(8,128)(2,1)S(1)} %add_convert_fusion.6), channel_id=1, source_target_pairs={{1,2},{2,1},{5,6},{6,5},{9,10},{10,9},{13,14},{14,13},{17,18},{18,... | collective-permute-start | bytes 1179656 | tf_op jit(solution)/shard_map/ppermute | solution.py:440
  87.4 35.2 %collective-permute-start.25 = (bf16[128,1536]{1,0:T(8,128)(2,1)S(1)}, bf16[128,1536]{1,0:T(8,128)(2,1)S(1)}, u32[]{:S(2)}, u32[]{:S(2)}) collective-permute-start(bf16[128,1536]{1,0:T(8,128)(2,1)S(1)} %add_convert_fusion.4), channel_id=1, source_target_pairs={{1,2},{2,1},{5,6},{6,5},{9,10},{10,9},{13,14},{14,13},{17,18},{18,... | collective-permute-start | bytes 1179656 | tf_op jit(solution)/shard_map/ppermute | solution.py:440
  102.0 12.0 %collective-permute-start.23 = (bf16[128,2048]{1,0:T(8,128)(2,1)S(1)}, bf16[128,2048]{1,0:T(8,128)(2,1)S(1)}, u32[]{:S(2)}, u32[]{:S(2)}) collective-permute-start(bf16[128,2048]{1,0:T(8,128)(2,1)S(1)} %add_convert_fusion.2), channel_id=1, source_target_pairs={{0,1},{1,0},{2,3},{3,2},{4,5},{5,4},{6,7},{7,6},{8,9},{9,8},{10,11... | collective-permute-start | bytes 1572872 | tf_op jit(solution)/shard_map/ppermute | solution.py:27
  114.1 8.5 %collective-permute-start.24 = (bf16[128,1536]{1,0:T(8,128)(2,1)S(1)}, bf16[128,1536]{1,0:T(8,128)(2,1)S(1)}, u32[]{:S(2)}, u32[]{:S(2)}) collective-permute-start(bf16[128,1536]{1,0:T(8,128)(2,1)S(1)} %add_convert_fusion.5), channel_id=1, source_target_pairs={{0,1},{1,0},{2,3},{3,2},{4,5},{5,4},{6,7},{7,6},{8,9},{9,8},{10,11... | collective-permute-start | bytes 1179656 | tf_op jit(solution)/shard_map/ppermute | solution.py:27

commit v3 on v1

--- a/solution.py
+++ b/solution.py
@@ -467,7 +467,7 @@
     o1 = move(up, *MIDDLE)
 
     gathered = gather_rows(own, d)
-    cut = 3 * hidden // 7 // 512 * 512
+    cut = 2 * hidden // 7 // 512 * 512
     block = rows * len(gathered) // groups
     q, *first = project_first(gathered, weight, cut, (block, block, 2 * block))
     own_a, pair_a, beyond_a = first[0]

time: 114 us -> 114 us (level)
  starting transfers between devices: 35.5 us -> 39.4 us
  waiting for transfers between devices: 41.2 us -> 37.9 us
    ppermute x15, starting transfers between devices: 14.5 us -> 20.2 us  [swap(): lax.ppermute(block, axis, [(i, i ^ mask) for i in range(count) if i ^ mas...]
    ppermute x15, waiting for transfers between devices: 19.2 us -> 17.3 us  [swap(): lax.ppermute(block, axis, [(i, i ^ mask) for i in range(count) if i ^ mas...]
    ppermute x10, starting transfers between devices: 19.4 us -> 17.6 us  [move(): return lax.ppermute(block, 'tensor', pairs)]
    pallas_call x1, Pallas kernels: 6.03 us -> 4.45 us  [project_first(): pl.pallas_call(first_kernel, out_shape=[jax.ShapeDtypeStruct((tokens, dep...]
    pallas_call x1, Pallas kernels: 7.14 us -> 8.67 us  [project(): pl.pallas_call(project_kernel, out_shape=[jax.ShapeDtypeStruct((block, wi...]
    ppermute x10, waiting for transfers between devices: 17.6 us -> 16.2 us  [move(): return lax.ppermute(block, 'tensor', pairs)]
  transfers between devices with their start and end apart: 26 -> 26, of which waited for: 15 -> 14; matrix products, arithmetic and copies ran while one was open for 1% -> 1% of each run, Pallas kernels for 28% -> 27%
where the time goes in v3:
time: 114 us
  starting transfers between devices  39.4 us (35%)
  waiting for transfers between devices  37.9 us (33%)
  Pallas kernels  31.5 us (28%)
  other arithmetic  2.47 us (2%)
  local copies, waits for them, and re-layouts  1.72 us (2%)
    ppermute x15, starting transfers between devices, swap(): lax.ppermute(block, axis, [(i, i ^ mask) for i in range(count) if i ^ mas...  20.2 us
    ppermute x10, starting transfers between devices, move(): return lax.ppermute(block, 'tensor', pairs)  17.6 us
    ppermute x15, waiting for transfers between devices, swap(): lax.ppermute(block, axis, [(i, i ^ mask) for i in range(count) if i ^ mas...  17.3 us
    ppermute x10, waiting for transfers between devices, move(): return lax.ppermute(block, 'tensor', pairs)  16.2 us
    pallas_call x1, Pallas kernels, project(): pl.pallas_call(project_kernel, out_shape=[jax.ShapeDtypeStruct((block, wi...  8.67 us
    pallas_call x1, Pallas kernels, weight_gradient(): pl.pallas_call(functools.partial(grad_kernel, tile, start), out_shape=jax...  8.14 us
    pallas_call x1, Pallas kernels, gradient_late(): pl.pallas_call(functools.partial(late_kernel, tile), out_shape=jax.ShapeD...  5.45 us
    pallas_call x1, Pallas kernels, project_first(): pl.pallas_call(first_kernel, out_shape=[jax.ShapeDtypeStruct((tokens, dep...  4.45 us
  transfers between devices with their start and end apart: 26, of which 14 were waited for; matrix products, arithmetic and copies ran while one was open for 1% of the time, Pallas kernels for 27%

profile of v3, /device:TPU:0, one launch (start us, length us, event | category | flops | bytes accessed | tf_op | source)
XLA Modules:
  0.0 113.9 jit_solution(4009630489323560409)
XLA Ops:
  0.6 1.0 copy-done.1
  1.7 0.7 copy-done.2
  2.4 0.1 signed_pieces.1
  2.4 3.1 %collective-permute-start = (bf16[16,2048]{1,0:T(8,128)(2,1)S(1)}, bf16[16,2048]{1,0:T(8,128)(2,1)S(1)}, u32[]{:S(2)}, u32[]{:S(2)}) collective-permute-start(bf16[16,2048]{1,0:T(8,128)(2,1)S(1)} %get-tuple-element.41), channel_id=1, source_target_pairs={{0,1},{1,0},{2,3},{3,2},{4,5},{5,4},{6,7},{7,6},{8,9},{9,8},{10,11... | collective-permute-start | bytes 196616 | tf_op jit(solution)/shard_map/ppermute | solution.py:27
  5.5 2.6 %collective-permute-start.1 = (bf16[16,2048]{1,0:T(8,128)(2,1)S(1)}, bf16[16,2048]{1,0:T(8,128)(2,1)S(1)}, u32[]{:S(2)}, u32[]{:S(2)}) collective-permute-start(bf16[16,2048]{1,0:T(8,128)(2,1)S(1)} %get-tuple-element.42), channel_id=1, source_target_pairs={{0,2},{1,3},{2,0},{3,1},{4,6},{5,7},{6,4},{7,5},{8,10},{9,11},{10,... | collective-permute-start | bytes 196616 | tf_op jit(solution)/shard_map/ppermute | solution.py:27
  8.1 0.0 collective-permute-start.2
  8.1 0.3 fusion.3.h_ref
  8.5 4.3 %collective-permute-done.1.refs_2_ = bf16[16,2048]{1,0:T(8,128)(2,1)S(1)} collective-permute-done((bf16[16,2048]{1,0:T(8,128)(2,1)S(1)}, bf16[16,2048]{1,0:T(8,128)(2,1)S(1)}, u32[]{:S(2)}, u32[]{:S(2)}) %collective-permute-start.1) | collective-permute-done | bytes 65568 | tf_op jit(solution)/shard_map/ppermute | solution.py:27
  12.8 1.4 %collective-permute-done.2.refs_3_ = bf16[16,2048]{1,0:T(8,128)(2,1)S(1)} collective-permute-done((bf16[16,2048]{1,0:T(8,128)(2,1)S(1)}, bf16[16,2048]{1,0:T(8,128)(2,1)S(1)}, u32[]{:S(2)}, u32[]{:S(2)}) %collective-permute-start.2) | collective-permute-done | bytes 65568 | tf_op jit(solution)/shard_map/ppermute | solution.py:27
  14.2 0.3 rotate.1
  14.5 1.6 %collective-permute-start.4 = (bf16[16,2048]{1,0:T(8,128)(2,1)S(1)}, bf16[16,2048]{1,0:T(8,128)(2,1)S(1)}, u32[]{:S(2)}, u32[]{:S(2)}) collective-permute-start(bf16[16,2048]{1,0:T(8,128)(2,1)S(1)} %get-tuple-element.46), channel_id=1, source_target_pairs={{0,2},{1,3},{2,0},{3,1},{4,6},{5,7},{6,4},{7,5},{8,10},{9,11},{10,... | collective-permute-start | bytes 196616 | tf_op jit(solution)/shard_map/ppermute | solution.py:27
  16.1 0.7 collective-permute-start.5
  16.8 1.2 %collective-permute-start.3 = (bf16[16,2048]{1,0:T(8,128)(2,1)S(1)}, bf16[16,2048]{1,0:T(8,128)(2,1)S(1)}, u32[]{:S(2)}, u32[]{:S(2)}) collective-permute-start(bf16[16,2048]{1,0:T(8,128)(2,1)S(1)} %get-tuple-element.45), channel_id=1, source_target_pairs={{0,1},{1,0},{2,3},{3,2},{4,5},{5,4},{6,7},{7,6},{8,9},{9,8},{10,11... | collective-permute-start | bytes 196616 | tf_op jit(solution)/shard_map/ppermute | solution.py:27
  18.0 2.4 %collective-permute-done.4 = bf16[16,2048]{1,0:T(8,128)(2,1)S(1)} collective-permute-done((bf16[16,2048]{1,0:T(8,128)(2,1)S(1)}, bf16[16,2048]{1,0:T(8,128)(2,1)S(1)}, u32[]{:S(2)}, u32[]{:S(2)}) %collective-permute-start.4) | collective-permute-done | bytes 65568 | tf_op jit(solution)/shard_map/ppermute | solution.py:27
  20.5 1.7 %collective-permute-done.5 = bf16[16,2048]{1,0:T(8,128)(2,1)S(1)} collective-permute-done((bf16[16,2048]{1,0:T(8,128)(2,1)S(1)}, bf16[16,2048]{1,0:T(8,128)(2,1)S(1)}, u32[]{:S(2)}, u32[]{:S(2)}) %collective-permute-start.5) | collective-permute-done | bytes 65568 | tf_op jit(solution)/shard_map/ppermute | solution.py:27
  22.3 1.6 %collective-permute-start.7 = (bf16[64,2048]{1,0:T(8,128)(2,1)S(1)}, bf16[64,2048]{1,0:T(8,128)(2,1)S(1)}, u32[]{:S(2)}, u32[]{:S(2)}) collective-permute-start(bf16[64,2048]{1,0:T(8,128)(2,1)S(1)} %pad_maximum_fusion.1.refs_0_), channel_id=1, source_target_pairs={{0,8},{4,12},{8,0},{12,4},{16,24},{20,28},{24,16},{28,20},{1,9},{5... | collective-permute-start | bytes 786440 | tf_op jit(solution)/shard_map/ppermute | solution.py:27
  23.8 1.5 %collective-permute-start.8 = (bf16[64,2048]{1,0:T(8,128)(2,1)S(1)}, bf16[64,2048]{1,0:T(8,128)(2,1)S(1)}, u32[]{:S(2)}, u32[]{:S(2)}) collective-permute-start(bf16[64,2048]{1,0:T(8,128)(2,1)S(1)} %pad_maximum_fusion.1.refs_0_), channel_id=1, source_target_pairs={{0,16},{4,20},{8,24},{12,28},{16,0},{20,4},{24,8},{28,12},{1,17},{... | collective-permute-start | bytes 786440 | tf_op jit(solution)/shard_map/ppermute | solution.py:27
  25.4 0.1 collective-permute-start.13
  25.5 0.7 collective-permute-start.14
  26.2 0.1 collective-permute-start.6
  26.3 2.5 %collective-permute-done.7.refs_2_ = bf16[64,2048]{1,0:T(8,128)(2,1)S(1)} collective-permute-done((bf16[64,2048]{1,0:T(8,128)(2,1)S(1)}, bf16[64,2048]{1,0:T(8,128)(2,1)S(1)}, u32[]{:S(2)}, u32[]{:S(2)}) %collective-permute-start.7) | collective-permute-done | bytes 262176 | tf_op jit(solution)/shard_map/ppermute | solution.py:27
  28.7 1.5 %collective-permute-done.8.refs_4_ = bf16[64,2048]{1,0:T(8,128)(2,1)S(1)} collective-permute-done((bf16[64,2048]{1,0:T(8,128)(2,1)S(1)}, bf16[64,2048]{1,0:T(8,128)(2,1)S(1)}, u32[]{:S(2)}, u32[]{:S(2)}) %collective-permute-start.8) | collective-permute-done | bytes 262176 | tf_op jit(solution)/shard_map/ppermute | solution.py:27
  30.2 1.6 %collective-permute-start.11 = (bf16[64,2048]{1,0:T(8,128)(2,1)S(1)}, bf16[64,2048]{1,0:T(8,128)(2,1)S(1)}, u32[]{:S(2)}, u32[]{:S(2)}) collective-permute-start(bf16[64,2048]{1,0:T(8,128)(2,1)S(1)} %broadcast_select_fusion), channel_id=1, source_target_pairs={{0,16},{4,12},{8,24},{12,4},{16,0},{20,28},{24,8},{28,20},{1,17},{... | collective-permute-start | bytes 786440 | tf_op jit(solution)/shard_map/ppermute | solution.py:162
  31.8 0.0 collective-permute-start.9
  31.8 0.0 collective-permute-done.6.refs_1_
  31.8 0.5 collective-permute-start.10
  32.3 4.3 %collective-permute-done.11.refs_6_ = bf16[64,2048]{1,0:T(8,128)(2,1)S(1)} collective-permute-done((bf16[64,2048]{1,0:T(8,128)(2,1)S(1)}, bf16[64,2048]{1,0:T(8,128)(2,1)S(1)}, u32[]{:S(2)}, u32[]{:S(2)}) %collective-permute-start.11) | collective-permute-done | bytes 262176 | tf_op jit(solution)/shard_map/ppermute | solution.py:162
  36.7 0.0 collective-permute-start.12
  36.7 1.5 %collective-permute-done.12.refs_7_ = bf16[64,2048]{1,0:T(8,128)(2,1)S(1)} collective-permute-done((bf16[64,2048]{1,0:T(8,128)(2,1)S(1)}, bf16[64,2048]{1,0:T(8,128)(2,1)S(1)}, u32[]{:S(2)}, u32[]{:S(2)}) %collective-permute-start.12) | collective-permute-done | bytes 262176 | tf_op jit(solution)/shard_map/ppermute | solution.py:27
  38.2 4.4 %project_first.1 = (bf16[512,2048]{1,0:T(8,128)(2,1)S(1)}, bf16[128,1024]{1,0:T(8,128)(2,1)S(1)}, bf16[128,1024]{1,0:T(8,128)(2,1)S(1)}, bf16[256,1024]{1,0:T(8,128)(2,1)S(1)}) custom-call(bf16[64,2048]{1,0:T(8,128)(2,1)S(1)} %pad_maximum_fusion.1.refs_0_, bf16[64,2048]{1,0:T(8,128)(2,1)S(1)} %collective-permute-done.6.refs_1_, ...), custom_call_target="tpu_custom_call" | custom-call | flops 1 | bytes 1 | tf_op jit(solution)/shard_map/project_first/pallas_call | solution.py:221
  42.7 2.2 %collective-permute-start.18 = (bf16[256,1024]{1,0:T(8,128)(2,1)S(1)}, bf16[256,1024]{1,0:T(8,128)(2,1)S(1)}, u32[]{:S(2)}, u32[]{:S(2)}) collective-permute-start(bf16[256,1024]{1,0:T(8,128)(2,1)S(1)} %get-tuple-element.57), channel_id=1, source_target_pairs={{0,1},{3,2},{4,5},{7,6},{8,9},{11,10},{12,13},{15,14},{16,17},{19,... | collective-permute-start | bytes 1572872 | tf_op jit(solution)/shard_map/ppermute | solution.py:440
  44.9 0.0 collective-permute-done.13.e1
  44.9 0.0 collective-permute-done.14.o1
  44.9 0.7 collective-permute-start.16
  45.7 1.3 %collective-permute-start.17 = (bf16[128,3584]{1,0:T(8,128)(2,1)S(1)}, bf16[128,3584]{1,0:T(8,128)(2,1)S(1)}, u32[]{:S(2)}, u32[]{:S(2)}) collective-permute-start(bf16[128,3584]{1,0:T(8,128)(2,1)S(1)} %collective-permute-done.14.o1), channel_id=1, source_target_pairs={{1,0},{2,3},{5,4},{6,7},{9,8},{10,11},{13,12},{14,15},{17,16},{18,... | collective-permute-start | bytes 2752520 | tf_op jit(solution)/shard_map/ppermute | solution.py:440
  47.0 8.7 %project.1 = (bf16[128,2560]{1,0:T(8,128)(2,1)S(1)}, bf16[128,2560]{1,0:T(8,128)(2,1)S(1)}, bf16[128,2560]{1,0:T(8,128)(2,1)S(1)}, bf16[128,2560]{1,0:T(8,128)(2,1)S(1)}) custom-call(bf16[512,2048]{1,0:T(8,128)(2,1)S(1)} %get-tuple-element.63.q_ref, bf16[2048,3584]{1,0:T(8,128)(2,1)} %w_ref.1), custom_call_target="tpu_custom_call" | custom-call | flops 5368709120 | bytes 15204352 | tf_op jit(solution)/shard_map/project/pallas_call | solution.py:243
  55.7 7.9 %collective-permute-start.15 = (bf16[128,2560]{1,0:T(8,128)(2,1)S(1)}, bf16[128,2560]{1,0:T(8,128)(2,1)S(1)}, u32[]{:S(2)}, u32[]{:S(2)}) collective-permute-start(bf16[128,2560]{1,0:T(8,128)(2,1)S(1)} %get-tuple-element.54), channel_id=1, source_target_pairs={{0,1},{3,2},{4,5},{7,6},{8,9},{11,10},{12,13},{15,14},{16,17},{19,... | collective-permute-start | bytes 1966088 | tf_op jit(solution)/shard_map/ppermute | solution.py:440
  63.6 1.3 %collective-permute-start.20 = (bf16[128,2560]{1,0:T(8,128)(2,1)S(1)}, bf16[128,2560]{1,0:T(8,128)(2,1)S(1)}, u32[]{:S(2)}, u32[]{:S(2)}) collective-permute-start(bf16[128,2560]{1,0:T(8,128)(2,1)S(1)} %get-tuple-element.62), channel_id=1, source_target_pairs={{0,1},{3,2},{4,5},{7,6},{8,9},{11,10},{12,13},{15,14},{16,17},{19,... | collective-permute-start | bytes 1966088 | tf_op jit(solution)/shard_map/ppermute | solution.py:440
  64.9 0.2 add_convert_fusion.4
  65.1 0.7 collective-permute-start.21
  65.8 0.0 collective-permute-done.16.o2
  65.8 3.9 %collective-permute-done.17.e2 = bf16[128,3584]{1,0:T(8,128)(2,1)S(1)} collective-permute-done((bf16[128,3584]{1,0:T(8,128)(2,1)S(1)}, bf16[128,3584]{1,0:T(8,128)(2,1)S(1)}, u32[]{:S(2)}, u32[]{:S(2)}) %collective-permute-start.17) | collective-permute-done | bytes 917536 | tf_op jit(solution)/shard_map/ppermute | solution.py:440
  69.7 1.3 %collective-permute-start.22 = (bf16[128,3584]{1,0:T(8,128)(2,1)S(1)}, bf16[128,3584]{1,0:T(8,128)(2,1)S(1)}, u32[]{:S(2)}, u32[]{:S(2)}) collective-permute-start(bf16[128,3584]{1,0:T(8,128)(2,1)S(1)} %collective-permute-done.16.o2), channel_id=1, source_target_pairs={{1,0},{2,3},{5,4},{6,7},{9,8},{10,11},{13,12},{14,15},{17,16},{18,... | collective-permute-start | bytes 2752520 | tf_op jit(solution)/shard_map/ppermute | solution.py:440
  71.0 7.7 %collective-permute-done.15 = bf16[128,2560]{1,0:T(8,128)(2,1)S(1)} collective-permute-done((bf16[128,2560]{1,0:T(8,128)(2,1)S(1)}, bf16[128,2560]{1,0:T(8,128)(2,1)S(1)}, u32[]{:S(2)}, u32[]{:S(2)}) %collective-permute-start.15) | collective-permute-done | bytes 655392 | tf_op jit(solution)/shard_map/ppermute | solution.py:440
  78.7 0.2 add_convert_fusion.3
  78.8 0.6 transposed.1.q_t
  79.4 0.7 collective-permute-start.19
  80.1 3.9 %gradient_early.1.early = f32[2048,1536]{1,0:T(8,128)S(1)} custom-call(bf16[2048,512]{1,0:T(8,128)(2,1)S(1)} %transposed.1.q_t, bf16[128,3584]{1,0:T(8,128)(2,1)S(1)} %copy-done, bf16[128,3584]{1,0:T(8,128)(2,1)S(1)} %collective-permute-done.13.e1, bf16[128,3584]{1,0:T(8,128)(2,1)S(1)} %collective-permute-done.14.o1, ...), custom_call_target="tpu_custom_call" | custom-call | flops 1 | bytes 1 | tf_op jit(solution)/shard_map/gradient_early/pallas_call | solution.py:375
  84.0 4.0 %collective-permute-done.20 = bf16[128,2560]{1,0:T(8,128)(2,1)S(1)} collective-permute-done((bf16[128,2560]{1,0:T(8,128)(2,1)S(1)}, bf16[128,2560]{1,0:T(8,128)(2,1)S(1)}, u32[]{:S(2)}, u32[]{:S(2)}) %collective-permute-start.20) | collective-permute-done | bytes 655392 | tf_op jit(solution)/shard_map/ppermute | solution.py:440
  88.0 0.2 add_convert_fusion.1
  88.2 0.7 collective-permute-start.25
  88.9 0.0 collective-permute-done.21
  88.9 0.6 collective-permute-done.22.e3
  89.5 0.1 add_convert_fusion.6
  89.6 4.7 %collective-permute-start.23 = (bf16[128,1024]{1,0:T(8,128)(2,1)S(1)}, bf16[128,1024]{1,0:T(8,128)(2,1)S(1)}, u32[]{:S(2)}, u32[]{:S(2)}) collective-permute-start(bf16[128,1024]{1,0:T(8,128)(2,1)S(1)} %add_convert_fusion.6), channel_id=1, source_target_pairs={{0,1},{1,0},{2,3},{3,2},{4,5},{5,4},{6,7},{7,6},{8,9},{9,8},{10,11... | collective-permute-start | bytes 786440 | tf_op jit(solution)/shard_map/ppermute | solution.py:27
  94.3 5.4 %gradient_late.1.refs_0_ = f32[2048,3584]{1,0:T(8,128)} custom-call(f32[2048,1536]{1,0:T(8,128)S(1)} %gradient_early.1.early, bf16[2048,512]{1,0:T(8,128)(2,1)S(1)} %transposed.1.q_t, bf16[128,3584]{1,0:T(8,128)(2,1)S(1)} %collective-permute-done.16.o2, bf16[128,3584]{1,0:T(8,128)(2,1)S(1)} %collective-permute-done.22.e3), custom_call_target="tpu_custom_call" | custom-call | flops 4831838208 | bytes 12582912 | tf_op jit(solution)/shard_map/gradient_late/pallas_call | solution.py:418
  99.7 0.3 collective-permute-done.23
  100.0 0.2 add_convert_fusion.2
  100.2 2.5 %collective-permute-start.24 = (bf16[128,2560]{1,0:T(8,128)(2,1)S(1)}, bf16[128,2560]{1,0:T(8,128)(2,1)S(1)}, u32[]{:S(2)}, u32[]{:S(2)}) collective-permute-start(bf16[128,2560]{1,0:T(8,128)(2,1)S(1)} %add_convert_fusion.2), channel_id=1, source_target_pairs={{0,1},{1,0},{2,3},{3,2},{4,5},{5,4},{6,7},{7,6},{8,9},{9,8},{10,11... | collective-permute-start | bytes 1966088 | tf_op jit(solution)/shard_map/ppermute | solution.py:27
  102.7 0.1 add_convert_fusion.5
  102.9 8.1 %weight_gradient.1 = f32[2048,3584]{1,0:T(8,128)} custom-call(bf16[2048,512]{1,0:T(8,128)(2,1)S(1)} %transposed.1.q_t, bf16[128,3584]{1,0:T(8,128)(2,1)S(1)} %copy-done, bf16[128,3584]{1,0:T(8,128)(2,1)S(1)} %collective-permute-done.13.e1, bf16[128,3584]{1,0:T(8,128)(2,1)S(1)} %collective-permute-done.14.o1, ...), custom_call_target="tpu_custom_call", output_to_operand_aliasing={{}: (7, {})} | custom-call | flops 10737418240 | bytes 20971520 | tf_op jit(solution)/shard_map/weight_gradient/pallas_call | solution.py:320
  111.0 1.6 %collective-permute-done.24 = bf16[128,2560]{1,0:T(8,128)(2,1)S(1)} collective-permute-done((bf16[128,2560]{1,0:T(8,128)(2,1)S(1)}, bf16[128,2560]{1,0:T(8,128)(2,1)S(1)}, u32[]{:S(2)}, u32[]{:S(2)}) %collective-permute-start.24) | collective-permute-done | bytes 655392 | tf_op jit(solution)/shard_map/ppermute | solution.py:27
  112.6 0.2 add_convert_fusion
  112.9 1.0 pad_maximum_fusion
  (14 shorter events, 0.1 us)
Async XLA Ops:
  0.6 24.7 %copy-start = (bf16[128,3584]{1,0:T(8,128)(2,1)S(1)}, bf16[128,3584]{1,0:T(8,128)(2,1)}, u32[]{:S(2)}) copy-start(bf16[128,3584]{1,0:T(8,128)(2,1)} %own_ref.3) | copy-start | bytes 2752516
  0.6 1.0 copy-start.1
  1.7 0.7 copy-start.2
  2.4 6.0 %collective-permute-start = (bf16[16,2048]{1,0:T(8,128)(2,1)S(1)}, bf16[16,2048]{1,0:T(8,128)(2,1)S(1)}, u32[]{:S(2)}, u32[]{:S(2)}) collective-permute-start(bf16[16,2048]{1,0:T(8,128)(2,1)S(1)} %get-tuple-element.41), channel_id=1, source_target_pairs={{0,1},{1,0},{2,3},{3,2},{4,5},{5,4},{6,7},{7,6},{8,9},{9,8},{10,11... | collective-permute-start | bytes 196616 | tf_op jit(solution)/shard_map/ppermute | solution.py:27
  5.5 7.3 %collective-permute-start.1 = (bf16[16,2048]{1,0:T(8,128)(2,1)S(1)}, bf16[16,2048]{1,0:T(8,128)(2,1)S(1)}, u32[]{:S(2)}, u32[]{:S(2)}) collective-permute-start(bf16[16,2048]{1,0:T(8,128)(2,1)S(1)} %get-tuple-element.42), channel_id=1, source_target_pairs={{0,2},{1,3},{2,0},{3,1},{4,6},{5,7},{6,4},{7,5},{8,10},{9,11},{10,... | collective-permute-start | bytes 196616 | tf_op jit(solution)/shard_map/ppermute | solution.py:27
  8.1 6.1 %collective-permute-start.2 = (bf16[16,2048]{1,0:T(8,128)(2,1)S(1)}, bf16[16,2048]{1,0:T(8,128)(2,1)S(1)}, u32[]{:S(2)}, u32[]{:S(2)}) collective-permute-start(bf16[16,2048]{1,0:T(8,128)(2,1)S(1)} %get-tuple-element.43), channel_id=1, source_target_pairs={{0,3},{1,2},{2,1},{3,0},{4,7},{5,6},{6,5},{7,4},{8,11},{9,10},{10,... | collective-permute-start | bytes 196616 | tf_op jit(solution)/shard_map/ppermute | solution.py:27
  14.5 6.0 %collective-permute-start.4 = (bf16[16,2048]{1,0:T(8,128)(2,1)S(1)}, bf16[16,2048]{1,0:T(8,128)(2,1)S(1)}, u32[]{:S(2)}, u32[]{:S(2)}) collective-permute-start(bf16[16,2048]{1,0:T(8,128)(2,1)S(1)} %get-tuple-element.46), channel_id=1, source_target_pairs={{0,2},{1,3},{2,0},{3,1},{4,6},{5,7},{6,4},{7,5},{8,10},{9,11},{10,... | collective-permute-start | bytes 196616 | tf_op jit(solution)/shard_map/ppermute | solution.py:27
  16.1 6.1 %collective-permute-start.5 = (bf16[16,2048]{1,0:T(8,128)(2,1)S(1)}, bf16[16,2048]{1,0:T(8,128)(2,1)S(1)}, u32[]{:S(2)}, u32[]{:S(2)}) collective-permute-start(bf16[16,2048]{1,0:T(8,128)(2,1)S(1)} %get-tuple-element.47), channel_id=1, source_target_pairs={{0,3},{1,2},{2,1},{3,0},{4,7},{5,6},{6,5},{7,4},{8,11},{9,10},{10,... | collective-permute-start | bytes 196616 | tf_op jit(solution)/shard_map/ppermute | solution.py:27
  16.8 5.4 %collective-permute-start.3 = (bf16[16,2048]{1,0:T(8,128)(2,1)S(1)}, bf16[16,2048]{1,0:T(8,128)(2,1)S(1)}, u32[]{:S(2)}, u32[]{:S(2)}) collective-permute-start(bf16[16,2048]{1,0:T(8,128)(2,1)S(1)} %get-tuple-element.45), channel_id=1, source_target_pairs={{0,1},{1,0},{2,3},{3,2},{4,5},{5,4},{6,7},{7,6},{8,9},{9,8},{10,11... | collective-permute-start | bytes 196616 | tf_op jit(solution)/shard_map/ppermute | solution.py:27
  22.3 6.4 %collective-permute-start.7 = (bf16[64,2048]{1,0:T(8,128)(2,1)S(1)}, bf16[64,2048]{1,0:T(8,128)(2,1)S(1)}, u32[]{:S(2)}, u32[]{:S(2)}) collective-permute-start(bf16[64,2048]{1,0:T(8,128)(2,1)S(1)} %pad_maximum_fusion.1.refs_0_), channel_id=1, source_target_pairs={{0,8},{4,12},{8,0},{12,4},{16,24},{20,28},{24,16},{28,20},{1,9},{5... | collective-permute-start | bytes 786440 | tf_op jit(solution)/shard_map/ppermute | solution.py:27
  23.8 6.4 %collective-permute-start.8 = (bf16[64,2048]{1,0:T(8,128)(2,1)S(1)}, bf16[64,2048]{1,0:T(8,128)(2,1)S(1)}, u32[]{:S(2)}, u32[]{:S(2)}) collective-permute-start(bf16[64,2048]{1,0:T(8,128)(2,1)S(1)} %pad_maximum_fusion.1.refs_0_), channel_id=1, source_target_pairs={{0,16},{4,20},{8,24},{12,28},{16,0},{20,4},{24,8},{28,12},{1,17},{... | collective-permute-start | bytes 786440 | tf_op jit(solution)/shard_map/ppermute | solution.py:27
  25.4 19.6 %collective-permute-start.13 = (bf16[128,3584]{1,0:T(8,128)(2,1)S(1)}, bf16[128,3584]{1,0:T(8,128)(2,1)S(1)}, u32[]{:S(2)}, u32[]{:S(2)}) collective-permute-start(bf16[128,3584]{1,0:T(8,128)(2,1)S(1)} %copy-done), channel_id=1, source_target_pairs={{0,1},{1,0},{2,3},{3,2},{4,5},{5,4},{6,7},{7,6},{8,9},{9,8},{10,11... | collective-permute-start | bytes 2752520 | tf_op jit(solution)/shard_map/ppermute | solution.py:27
  25.5 19.5 %collective-permute-start.14 = (bf16[128,3584]{1,0:T(8,128)(2,1)S(1)}, bf16[128,3584]{1,0:T(8,128)(2,1)S(1)}, u32[]{:S(2)}, u32[]{:S(2)}) collective-permute-start(bf16[128,3584]{1,0:T(8,128)(2,1)S(1)} %copy-done), channel_id=1, source_target_pairs={{1,2},{2,1},{5,6},{6,5},{9,10},{10,9},{13,14},{14,13},{17,18},{18,... | collective-permute-start | bytes 2752520 | tf_op jit(solution)/shard_map/ppermute | solution.py:440
  26.2 5.7 %collective-permute-start.6 = (bf16[64,2048]{1,0:T(8,128)(2,1)S(1)}, bf16[64,2048]{1,0:T(8,128)(2,1)S(1)}, u32[]{:S(2)}, u32[]{:S(2)}) collective-permute-start(bf16[64,2048]{1,0:T(8,128)(2,1)S(1)} %pad_maximum_fusion.1.refs_0_), channel_id=1, source_target_pairs={{0,4},{4,0},{8,12},{12,8},{16,20},{20,16},{24,28},{28,24},{1,5},{5... | collective-permute-start | bytes 786440 | tf_op jit(solution)/shard_map/ppermute | solution.py:27
  30.2 6.4 %collective-permute-start.11 = (bf16[64,2048]{1,0:T(8,128)(2,1)S(1)}, bf16[64,2048]{1,0:T(8,128)(2,1)S(1)}, u32[]{:S(2)}, u32[]{:S(2)}) collective-permute-start(bf16[64,2048]{1,0:T(8,128)(2,1)S(1)} %broadcast_select_fusion), channel_id=1, source_target_pairs={{0,16},{4,12},{8,24},{12,4},{16,0},{20,28},{24,8},{28,20},{1,17},{... | collective-permute-start | bytes 786440 | tf_op jit(solution)/shard_map/ppermute | solution.py:162
  31.8 4.9 %collective-permute-start.9 = (bf16[64,2048]{1,0:T(8,128)(2,1)S(1)}, bf16[64,2048]{1,0:T(8,128)(2,1)S(1)}, u32[]{:S(2)}, u32[]{:S(2)}) collective-permute-start(bf16[64,2048]{1,0:T(8,128)(2,1)S(1)} %collective-permute-done.7.refs_2_), channel_id=1, source_target_pairs={{0,4},{4,0},{8,12},{12,8},{16,20},{20,16},{24,28},{28,24},{1,5},{5... | collective-permute-start | bytes 786440 | tf_op jit(solution)/shard_map/ppermute | solution.py:27
  31.8 4.9 %collective-permute-start.10 = (bf16[64,2048]{1,0:T(8,128)(2,1)S(1)}, bf16[64,2048]{1,0:T(8,128)(2,1)S(1)}, u32[]{:S(2)}, u32[]{:S(2)}) collective-permute-start(bf16[64,2048]{1,0:T(8,128)(2,1)S(1)} %collective-permute-done.8.refs_4_), channel_id=1, source_target_pairs={{0,4},{4,0},{8,12},{12,8},{16,20},{20,16},{24,28},{28,24},{1,5},{5... | collective-permute-start | bytes 786440 | tf_op jit(solution)/shard_map/ppermute | solution.py:27
  36.7 1.5 %collective-permute-start.12 = (bf16[64,2048]{1,0:T(8,128)(2,1)S(1)}, bf16[64,2048]{1,0:T(8,128)(2,1)S(1)}, u32[]{:S(2)}, u32[]{:S(2)}) collective-permute-start(bf16[64,2048]{1,0:T(8,128)(2,1)S(1)} %collective-permute-done.11.refs_6_), channel_id=1, source_target_pairs={{0,4},{4,0},{8,12},{12,8},{16,20},{20,16},{24,28},{28,24},{1,5},{5... | collective-permute-start | bytes 786440 | tf_op jit(solution)/shard_map/ppermute | solution.py:27
  42.7 20.9 %collective-permute-start.18 = (bf16[256,1024]{1,0:T(8,128)(2,1)S(1)}, bf16[256,1024]{1,0:T(8,128)(2,1)S(1)}, u32[]{:S(2)}, u32[]{:S(2)}) collective-permute-start(bf16[256,1024]{1,0:T(8,128)(2,1)S(1)} %get-tuple-element.57), channel_id=1, source_target_pairs={{0,1},{3,2},{4,5},{7,6},{8,9},{11,10},{12,13},{15,14},{16,17},{19,... | collective-permute-start | bytes 1572872 | tf_op jit(solution)/shard_map/ppermute | solution.py:440
  44.9 20.9 %collective-permute-start.16 = (bf16[128,3584]{1,0:T(8,128)(2,1)S(1)}, bf16[128,3584]{1,0:T(8,128)(2,1)S(1)}, u32[]{:S(2)}, u32[]{:S(2)}) collective-permute-start(bf16[128,3584]{1,0:T(8,128)(2,1)S(1)} %collective-permute-done.13.e1), channel_id=1, source_target_pairs={{1,2},{2,1},{5,6},{6,5},{9,10},{10,9},{13,14},{14,13},{17,18},{18,... | collective-permute-start | bytes 2752520 | tf_op jit(solution)/shard_map/ppermute | solution.py:440
  45.7 24.0 %collective-permute-start.17 = (bf16[128,3584]{1,0:T(8,128)(2,1)S(1)}, bf16[128,3584]{1,0:T(8,128)(2,1)S(1)}, u32[]{:S(2)}, u32[]{:S(2)}) collective-permute-start(bf16[128,3584]{1,0:T(8,128)(2,1)S(1)} %collective-permute-done.14.o1), channel_id=1, source_target_pairs={{1,0},{2,3},{5,4},{6,7},{9,8},{10,11},{13,12},{14,15},{17,16},{18,... | collective-permute-start | bytes 2752520 | tf_op jit(solution)/shard_map/ppermute | solution.py:440
  55.7 23.0 %collective-permute-start.15 = (bf16[128,2560]{1,0:T(8,128)(2,1)S(1)}, bf16[128,2560]{1,0:T(8,128)(2,1)S(1)}, u32[]{:S(2)}, u32[]{:S(2)}) collective-permute-start(bf16[128,2560]{1,0:T(8,128)(2,1)S(1)} %get-tuple-element.54), channel_id=1, source_target_pairs={{0,1},{3,2},{4,5},{7,6},{8,9},{11,10},{12,13},{15,14},{16,17},{19,... | collective-permute-start | bytes 1966088 | tf_op jit(solution)/shard_map/ppermute | solution.py:440
  63.6 24.5 %collective-permute-start.20 = (bf16[128,2560]{1,0:T(8,128)(2,1)S(1)}, bf16[128,2560]{1,0:T(8,128)(2,1)S(1)}, u32[]{:S(2)}, u32[]{:S(2)}) collective-permute-start(bf16[128,2560]{1,0:T(8,128)(2,1)S(1)} %get-tuple-element.62), channel_id=1, source_target_pairs={{0,1},{3,2},{4,5},{7,6},{8,9},{11,10},{12,13},{15,14},{16,17},{19,... | collective-permute-start | bytes 1966088 | tf_op jit(solution)/shard_map/ppermute | solution.py:440
  65.1 23.8 %collective-permute-start.21 = (bf16[256,1024]{1,0:T(8,128)(2,1)S(1)}, bf16[256,1024]{1,0:T(8,128)(2,1)S(1)}, u32[]{:S(2)}, u32[]{:S(2)}) collective-permute-start(bf16[256,1024]{1,0:T(8,128)(2,1)S(1)} %add_convert_fusion.4), channel_id=1, source_target_pairs={{1,2},{2,1},{5,6},{6,5},{9,10},{10,9},{13,14},{14,13},{17,18},{18,... | collective-permute-start | bytes 1572872 | tf_op jit(solution)/shard_map/ppermute | solution.py:440
  69.7 19.8 %collective-permute-start.22 = (bf16[128,3584]{1,0:T(8,128)(2,1)S(1)}, bf16[128,3584]{1,0:T(8,128)(2,1)S(1)}, u32[]{:S(2)}, u32[]{:S(2)}) collective-permute-start(bf16[128,3584]{1,0:T(8,128)(2,1)S(1)} %collective-permute-done.16.o2), channel_id=1, source_target_pairs={{1,0},{2,3},{5,4},{6,7},{9,8},{10,11},{13,12},{14,15},{17,16},{18,... | collective-permute-start | bytes 2752520 | tf_op jit(solution)/shard_map/ppermute | solution.py:440
  79.4 20.3 %collective-permute-start.19 = (bf16[128,2560]{1,0:T(8,128)(2,1)S(1)}, bf16[128,2560]{1,0:T(8,128)(2,1)S(1)}, u32[]{:S(2)}, u32[]{:S(2)}) collective-permute-start(bf16[128,2560]{1,0:T(8,128)(2,1)S(1)} %add_convert_fusion.3), channel_id=1, source_target_pairs={{1,2},{2,1},{5,6},{6,5},{9,10},{10,9},{13,14},{14,13},{17,18},{18,... | collective-permute-start | bytes 1966088 | tf_op jit(solution)/shard_map/ppermute | solution.py:440
  88.2 22.8 %collective-permute-start.25 = (bf16[128,2560]{1,0:T(8,128)(2,1)S(1)}, bf16[128,2560]{1,0:T(8,128)(2,1)S(1)}, u32[]{:S(2)}, u32[]{:S(2)}) collective-permute-start(bf16[128,2560]{1,0:T(8,128)(2,1)S(1)} %add_convert_fusion.1), channel_id=1, source_target_pairs={{1,2},{2,1},{5,6},{6,5},{9,10},{10,9},{13,14},{14,13},{17,18},{18,... | collective-permute-start | bytes 1966088 | tf_op jit(solution)/shard_map/ppermute | solution.py:440
  89.6 10.5 %collective-permute-start.23 = (bf16[128,1024]{1,0:T(8,128)(2,1)S(1)}, bf16[128,1024]{1,0:T(8,128)(2,1)S(1)}, u32[]{:S(2)}, u32[]{:S(2)}) collective-permute-start(bf16[128,1024]{1,0:T(8,128)(2,1)S(1)} %add_convert_fusion.6), channel_id=1, source_target_pairs={{0,1},{1,0},{2,3},{3,2},{4,5},{5,4},{6,7},{7,6},{8,9},{9,8},{10,11... | collective-permute-start | bytes 786440 | tf_op jit(solution)/shard_map/ppermute | solution.py:27
  100.2 12.5 %collective-permute-start.24 = (bf16[128,2560]{1,0:T(8,128)(2,1)S(1)}, bf16[128,2560]{1,0:T(8,128)(2,1)S(1)}, u32[]{:S(2)}, u32[]{:S(2)}) collective-permute-start(bf16[128,2560]{1,0:T(8,128)(2,1)S(1)} %add_convert_fusion.2), channel_id=1, source_target_pairs={{0,1},{1,0},{2,3},{3,2},{4,5},{5,4},{6,7},{7,6},{8,9},{9,8},{10,11... | collective-permute-start | bytes 1966088 | tf_op jit(solution)/shard_map/ppermute | solution.py:27

commit v4 on v3

--- a/solution.py
+++ b/solution.py
@@ -330,8 +330,8 @@
         ],
         compiler_params=pltpu.CompilerParams(vmem_limit_bytes=28 * MIB),
         cost_estimate=pl.CostEstimate(
-            flops=5 * tokens * depth * width,
-            bytes_accessed=2 * tokens * (depth + width) + 4 * depth * width,
+            flops=1,
+            bytes_accessed=1,
             transcendentals=0,
         ),
         name="weight_gradient",
@@ -498,9 +498,9 @@
     grad = gradient_late(early, late, o2, e3)
 
     across_near = move(total(near_b, inward_near), *MIDDLE)
-    across_far, grad, out_a = after([across_far, grad, out_a])
+    across_far, out_a = after([across_far, out_a])
     out_b = swap(total(pair_b, across_far), "tensor", 1)
-    (late,) = after([q_t], across_far)
+    late, grad = after([q_t, grad], across_far)
     weight_grad = weight_gradient(late, upstream, moved, some, hidden - some, grad)
     projected = jnp.concatenate(
         [total(own_a, out_a, across_a[block:]), total(own_b, out_b, across_near)], axis=1

time: 114 us -> 118 us (1.035)
  starting transfers between devices: 39.4 us -> 42.4 us
    ppermute x10, waiting for transfers between devices: 16.2 us -> 11.7 us  [move(): return lax.ppermute(block, 'tensor', pairs)]
    ppermute x15, waiting for transfers between devices: 17.3 us -> 21 us  [swap(): lax.ppermute(block, axis, [(i, i ^ mask) for i in range(count) if i ^ mas...]
    ppermute x10, starting transfers between devices: 17.6 us -> 20 us  [move(): return lax.ppermute(block, 'tensor', pairs)]
    ppermute x15, starting transfers between devices: 20.2 us -> 21.9 us  [swap(): lax.ppermute(block, axis, [(i, i ^ mask) for i in range(count) if i ^ mas...]
  transfers between devices with their start and end apart: 26 -> 26, of which waited for: 14 -> 13; matrix products, arithmetic and copies ran while one was open for 1% -> 1% of each run, Pallas kernels for 27% -> 27%
where the time goes in v4:
time: 118 us; the launch traced here: 117 us
  starting transfers between devices  42.4 us (36%)
  waiting for transfers between devices  38.1 us (32%)
  Pallas kernels  31.5 us (27%)
  other arithmetic  2.48 us (2%)
  local copies, waits for them, and re-layouts  1.72 us (1%)
    ppermute x15, starting transfers between devices, swap(): lax.ppermute(block, axis, [(i, i ^ mask) for i in range(count) if i ^ mas...  21.9 us
    ppermute x15, waiting for transfers between devices, swap(): lax.ppermute(block, axis, [(i, i ^ mask) for i in range(count) if i ^ mas...  21 us
    ppermute x10, starting transfers between devices, move(): return lax.ppermute(block, 'tensor', pairs)  20 us
    ppermute x10, waiting for transfers between devices, move(): return lax.ppermute(block, 'tensor', pairs)  11.7 us
    pallas_call x1, Pallas kernels, project(): pl.pallas_call(project_kernel, out_shape=[jax.ShapeDtypeStruct((block, wi...  8.67 us
    pallas_call x1, Pallas kernels, weight_gradient(): pl.pallas_call(functools.partial(grad_kernel, tile, start), out_shape=jax...  8.13 us
    pallas_call x1, Pallas kernels, gradient_late(): pl.pallas_call(functools.partial(late_kernel, tile), out_shape=jax.ShapeD...  5.44 us
    ppermute x1, waiting for transfers between devices, gather_rows(): lax.ppermute(through, 'dp', [(i, i ^ (4 if i & 1 == 0 else 2)) for i in r...  5.35 us
  transfers between devices with their start and end apart: 26, of which 13 were waited for; matrix products, arithmetic and copies ran while one was open for 1% of the time, Pallas kernels for 27%

profile of v4, /device:TPU:0, one launch (start us, length us, event | category | flops | bytes accessed | tf_op | source)
XLA Modules:
  0.0 117.1 jit_solution(8534925005227959958)
XLA Ops:
  0.6 1.0 copy-done.1
  1.7 0.7 copy-done.2
  2.4 0.1 signed_pieces.1
  2.4 3.1 %collective-permute-start = (bf16[16,2048]{1,0:T(8,128)(2,1)S(1)}, bf16[16,2048]{1,0:T(8,128)(2,1)S(1)}, u32[]{:S(2)}, u32[]{:S(2)}) collective-permute-start(bf16[16,2048]{1,0:T(8,128)(2,1)S(1)} %get-tuple-element.41), channel_id=1, source_target_pairs={{0,1},{1,0},{2,3},{3,2},{4,5},{5,4},{6,7},{7,6},{8,9},{9,8},{10,11... | collective-permute-start | bytes 196616 | tf_op jit(solution)/shard_map/ppermute | solution.py:27
  5.5 2.6 %collective-permute-start.1 = (bf16[16,2048]{1,0:T(8,128)(2,1)S(1)}, bf16[16,2048]{1,0:T(8,128)(2,1)S(1)}, u32[]{:S(2)}, u32[]{:S(2)}) collective-permute-start(bf16[16,2048]{1,0:T(8,128)(2,1)S(1)} %get-tuple-element.42), channel_id=1, source_target_pairs={{0,2},{1,3},{2,0},{3,1},{4,6},{5,7},{6,4},{7,5},{8,10},{9,11},{10,... | collective-permute-start | bytes 196616 | tf_op jit(solution)/shard_map/ppermute | solution.py:27
  8.1 0.3 fusion.3.h_ref
  8.4 0.0 collective-permute-done.refs_1_
  8.5 4.3 %collective-permute-done.1.refs_2_ = bf16[16,2048]{1,0:T(8,128)(2,1)S(1)} collective-permute-done((bf16[16,2048]{1,0:T(8,128)(2,1)S(1)}, bf16[16,2048]{1,0:T(8,128)(2,1)S(1)}, u32[]{:S(2)}, u32[]{:S(2)}) %collective-permute-start.1) | collective-permute-done | bytes 65568 | tf_op jit(solution)/shard_map/ppermute | solution.py:27
  12.8 1.4 %collective-permute-done.2.refs_3_ = bf16[16,2048]{1,0:T(8,128)(2,1)S(1)} collective-permute-done((bf16[16,2048]{1,0:T(8,128)(2,1)S(1)}, bf16[16,2048]{1,0:T(8,128)(2,1)S(1)}, u32[]{:S(2)}, u32[]{:S(2)}) %collective-permute-start.2) | collective-permute-done | bytes 65568 | tf_op jit(solution)/shard_map/ppermute | solution.py:27
  14.2 0.3 rotate.1
  14.5 0.1 collective-permute-start.3
  14.6 2.3 %collective-permute-start.4 = (bf16[16,2048]{1,0:T(8,128)(2,1)S(1)}, bf16[16,2048]{1,0:T(8,128)(2,1)S(1)}, u32[]{:S(2)}, u32[]{:S(2)}) collective-permute-start(bf16[16,2048]{1,0:T(8,128)(2,1)S(1)} %get-tuple-element.46), channel_id=1, source_target_pairs={{0,2},{1,3},{2,0},{3,1},{4,6},{5,7},{6,4},{7,5},{8,10},{9,11},{10,... | collective-permute-start | bytes 196616 | tf_op jit(solution)/shard_map/ppermute | solution.py:27
  16.9 2.0 %collective-permute-start.5 = (bf16[16,2048]{1,0:T(8,128)(2,1)S(1)}, bf16[16,2048]{1,0:T(8,128)(2,1)S(1)}, u32[]{:S(2)}, u32[]{:S(2)}) collective-permute-start(bf16[16,2048]{1,0:T(8,128)(2,1)S(1)} %get-tuple-element.47), channel_id=1, source_target_pairs={{0,3},{1,2},{2,1},{3,0},{4,7},{5,6},{6,5},{7,4},{8,11},{9,10},{10,... | collective-permute-start | bytes 196616 | tf_op jit(solution)/shard_map/ppermute | solution.py:27
  18.9 1.4 %collective-permute-done.4 = bf16[16,2048]{1,0:T(8,128)(2,1)S(1)} collective-permute-done((bf16[16,2048]{1,0:T(8,128)(2,1)S(1)}, bf16[16,2048]{1,0:T(8,128)(2,1)S(1)}, u32[]{:S(2)}, u32[]{:S(2)}) %collective-permute-start.4) | collective-permute-done | bytes 65568 | tf_op jit(solution)/shard_map/ppermute | solution.py:27
  20.4 2.6 %collective-permute-done.5 = bf16[16,2048]{1,0:T(8,128)(2,1)S(1)} collective-permute-done((bf16[16,2048]{1,0:T(8,128)(2,1)S(1)}, bf16[16,2048]{1,0:T(8,128)(2,1)S(1)}, u32[]{:S(2)}, u32[]{:S(2)}) %collective-permute-start.5) | collective-permute-done | bytes 65568 | tf_op jit(solution)/shard_map/ppermute | solution.py:27
  23.0 1.6 %collective-permute-start.8 = (bf16[64,2048]{1,0:T(8,128)(2,1)S(1)}, bf16[64,2048]{1,0:T(8,128)(2,1)S(1)}, u32[]{:S(2)}, u32[]{:S(2)}) collective-permute-start(bf16[64,2048]{1,0:T(8,128)(2,1)S(1)} %pad_maximum_fusion.1.refs_0_), channel_id=1, source_target_pairs={{0,16},{4,20},{8,24},{12,28},{16,0},{20,4},{24,8},{28,12},{1,17},{... | collective-permute-start | bytes 786440 | tf_op jit(solution)/shard_map/ppermute | solution.py:27
  24.6 1.5 %collective-permute-start.7 = (bf16[64,2048]{1,0:T(8,128)(2,1)S(1)}, bf16[64,2048]{1,0:T(8,128)(2,1)S(1)}, u32[]{:S(2)}, u32[]{:S(2)}) collective-permute-start(bf16[64,2048]{1,0:T(8,128)(2,1)S(1)} %pad_maximum_fusion.1.refs_0_), channel_id=1, source_target_pairs={{0,8},{4,12},{8,0},{12,4},{16,24},{20,28},{24,16},{28,20},{1,9},{5... | collective-permute-start | bytes 786440 | tf_op jit(solution)/shard_map/ppermute | solution.py:27
  26.1 0.7 collective-permute-start.14
  26.8 2.1 %collective-permute-start.13 = (bf16[128,3584]{1,0:T(8,128)(2,1)S(1)}, bf16[128,3584]{1,0:T(8,128)(2,1)S(1)}, u32[]{:S(2)}, u32[]{:S(2)}) collective-permute-start(bf16[128,3584]{1,0:T(8,128)(2,1)S(1)} %copy-done), channel_id=1, source_target_pairs={{0,1},{1,0},{2,3},{3,2},{4,5},{5,4},{6,7},{7,6},{8,9},{9,8},{10,11... | collective-permute-start | bytes 2752520 | tf_op jit(solution)/shard_map/ppermute | solution.py:27
  29.0 0.0 collective-permute-start.6
  29.0 0.5 collective-permute-done.8.refs_4_
  29.5 1.5 %collective-permute-done.7.refs_2_ = bf16[64,2048]{1,0:T(8,128)(2,1)S(1)} collective-permute-done((bf16[64,2048]{1,0:T(8,128)(2,1)S(1)}, bf16[64,2048]{1,0:T(8,128)(2,1)S(1)}, u32[]{:S(2)}, u32[]{:S(2)}) %collective-permute-start.7) | collective-permute-done | bytes 262176 | tf_op jit(solution)/shard_map/ppermute | solution.py:27
  31.0 0.6 collective-permute-start.11
  31.6 0.0 collective-permute-start.9
  31.6 0.0 collective-permute-done.6.refs_1_
  31.6 0.5 collective-permute-start.10
  32.1 5.3 %collective-permute-done.11.refs_6_ = bf16[64,2048]{1,0:T(8,128)(2,1)S(1)} collective-permute-done((bf16[64,2048]{1,0:T(8,128)(2,1)S(1)}, bf16[64,2048]{1,0:T(8,128)(2,1)S(1)}, u32[]{:S(2)}, u32[]{:S(2)}) %collective-permute-start.11) | collective-permute-done | bytes 262176 | tf_op jit(solution)/shard_map/ppermute | solution.py:162
  37.5 0.0 collective-permute-start.12
  37.5 0.0 collective-permute-done.9.refs_3_
  37.5 0.0 collective-permute-done.10.refs_5_
  37.5 1.5 %collective-permute-done.12.refs_7_ = bf16[64,2048]{1,0:T(8,128)(2,1)S(1)} collective-permute-done((bf16[64,2048]{1,0:T(8,128)(2,1)S(1)}, bf16[64,2048]{1,0:T(8,128)(2,1)S(1)}, u32[]{:S(2)}, u32[]{:S(2)}) %collective-permute-start.12) | collective-permute-done | bytes 262176 | tf_op jit(solution)/shard_map/ppermute | solution.py:27
  39.0 4.4 %project_first.1 = (bf16[512,2048]{1,0:T(8,128)(2,1)S(1)}, bf16[128,1024]{1,0:T(8,128)(2,1)S(1)}, bf16[128,1024]{1,0:T(8,128)(2,1)S(1)}, bf16[256,1024]{1,0:T(8,128)(2,1)S(1)}) custom-call(bf16[64,2048]{1,0:T(8,128)(2,1)S(1)} %pad_maximum_fusion.1.refs_0_, bf16[64,2048]{1,0:T(8,128)(2,1)S(1)} %collective-permute-done.6.refs_1_, ...), custom_call_target="tpu_custom_call" | custom-call | flops 1 | bytes 1 | tf_op jit(solution)/shard_map/project_first/pallas_call | solution.py:221
  43.5 0.0 collective-permute-done.14.o1
  43.5 3.0 %collective-permute-done.13.e1 = bf16[128,3584]{1,0:T(8,128)(2,1)S(1)} collective-permute-done((bf16[128,3584]{1,0:T(8,128)(2,1)S(1)}, bf16[128,3584]{1,0:T(8,128)(2,1)S(1)}, u32[]{:S(2)}, u32[]{:S(2)}) %collective-permute-start.13) | collective-permute-done | bytes 917536 | tf_op jit(solution)/shard_map/ppermute | solution.py:27
  46.4 0.7 collective-permute-start.16
  47.1 1.3 %collective-permute-start.17 = (bf16[128,3584]{1,0:T(8,128)(2,1)S(1)}, bf16[128,3584]{1,0:T(8,128)(2,1)S(1)}, u32[]{:S(2)}, u32[]{:S(2)}) collective-permute-start(bf16[128,3584]{1,0:T(8,128)(2,1)S(1)} %collective-permute-done.14.o1), channel_id=1, source_target_pairs={{1,0},{2,3},{5,4},{6,7},{9,8},{10,11},{13,12},{14,15},{17,16},{18,... | collective-permute-start | bytes 2752520 | tf_op jit(solution)/shard_map/ppermute | solution.py:440
  48.4 5.2 %collective-permute-start.18 = (bf16[256,1024]{1,0:T(8,128)(2,1)S(1)}, bf16[256,1024]{1,0:T(8,128)(2,1)S(1)}, u32[]{:S(2)}, u32[]{:S(2)}) collective-permute-start(bf16[256,1024]{1,0:T(8,128)(2,1)S(1)} %get-tuple-element.57), channel_id=1, source_target_pairs={{0,1},{3,2},{4,5},{7,6},{8,9},{11,10},{12,13},{15,14},{16,17},{19,... | collective-permute-start | bytes 1572872 | tf_op jit(solution)/shard_map/ppermute | solution.py:440
  53.7 8.7 %project.1 = (bf16[128,2560]{1,0:T(8,128)(2,1)S(1)}, bf16[128,2560]{1,0:T(8,128)(2,1)S(1)}, bf16[128,2560]{1,0:T(8,128)(2,1)S(1)}, bf16[128,2560]{1,0:T(8,128)(2,1)S(1)}) custom-call(bf16[512,2048]{1,0:T(8,128)(2,1)S(1)} %get-tuple-element.69.q_ref, bf16[2048,3584]{1,0:T(8,128)(2,1)} %w_ref.1), custom_call_target="tpu_custom_call" | custom-call | flops 5368709120 | bytes 15204352 | tf_op jit(solution)/shard_map/project/pallas_call | solution.py:243
  62.3 1.3 %collective-permute-start.15 = (bf16[128,2560]{1,0:T(8,128)(2,1)S(1)}, bf16[128,2560]{1,0:T(8,128)(2,1)S(1)}, u32[]{:S(2)}, u32[]{:S(2)}) collective-permute-start(bf16[128,2560]{1,0:T(8,128)(2,1)S(1)} %get-tuple-element.54), channel_id=1, source_target_pairs={{0,1},{3,2},{4,5},{7,6},{8,9},{11,10},{12,13},{15,14},{16,17},{19,... | collective-permute-start | bytes 1966088 | tf_op jit(solution)/shard_map/ppermute | solution.py:440
  63.7 0.0 collective-permute-done.18
  63.7 4.8 %collective-permute-done.17.e2 = bf16[128,3584]{1,0:T(8,128)(2,1)S(1)} collective-permute-done((bf16[128,3584]{1,0:T(8,128)(2,1)S(1)}, bf16[128,3584]{1,0:T(8,128)(2,1)S(1)}, u32[]{:S(2)}, u32[]{:S(2)}) %collective-permute-start.17) | collective-permute-done | bytes 917536 | tf_op jit(solution)/shard_map/ppermute | solution.py:440
  68.5 1.3 %collective-permute-start.21 = (bf16[128,3584]{1,0:T(8,128)(2,1)S(1)}, bf16[128,3584]{1,0:T(8,128)(2,1)S(1)}, u32[]{:S(2)}, u32[]{:S(2)}) collective-permute-start(bf16[128,3584]{1,0:T(8,128)(2,1)S(1)} %collective-permute-done.16.o2), channel_id=1, source_target_pairs={{1,0},{2,3},{5,4},{6,7},{9,8},{10,11},{13,12},{14,15},{17,16},{18,... | collective-permute-start | bytes 2752520 | tf_op jit(solution)/shard_map/ppermute | solution.py:440
  69.8 0.2 add_convert_fusion.4
  70.0 0.7 collective-permute-start.20
  70.7 7.3 %collective-permute-start.24 = (bf16[128,2560]{1,0:T(8,128)(2,1)S(1)}, bf16[128,2560]{1,0:T(8,128)(2,1)S(1)}, u32[]{:S(2)}, u32[]{:S(2)}) collective-permute-start(bf16[128,2560]{1,0:T(8,128)(2,1)S(1)} %get-tuple-element.68), channel_id=1, source_target_pairs={{0,1},{3,2},{4,5},{7,6},{8,9},{11,10},{12,13},{15,14},{16,17},{19,... | collective-permute-start | bytes 1966088 | tf_op jit(solution)/shard_map/ppermute | solution.py:440
  78.0 0.3 collective-permute-done.15
  78.3 0.6 transposed.1.q_t
  78.9 0.2 add_convert_fusion.3
  79.1 0.7 collective-permute-start.19
  79.8 3.9 %gradient_early.1.early = f32[2048,1536]{1,0:T(8,128)S(1)} custom-call(bf16[2048,512]{1,0:T(8,128)(2,1)S(1)} %transposed.1.q_t, bf16[128,3584]{1,0:T(8,128)(2,1)S(1)} %copy-done, bf16[128,3584]{1,0:T(8,128)(2,1)S(1)} %collective-permute-done.13.e1, bf16[128,3584]{1,0:T(8,128)(2,1)S(1)} %collective-permute-done.14.o1, ...), custom_call_target="tpu_custom_call" | custom-call | flops 1 | bytes 1 | tf_op jit(solution)/shard_map/gradient_early/pallas_call | solution.py:375
  83.6 6.6 %collective-permute-done.24 = bf16[128,2560]{1,0:T(8,128)(2,1)S(1)} collective-permute-done((bf16[128,2560]{1,0:T(8,128)(2,1)S(1)}, bf16[128,2560]{1,0:T(8,128)(2,1)S(1)}, u32[]{:S(2)}, u32[]{:S(2)}) %collective-permute-start.24) | collective-permute-done | bytes 655392 | tf_op jit(solution)/shard_map/ppermute | solution.py:440
  90.2 0.1 add_convert_fusion.6
  90.3 2.5 %collective-permute-start.22 = (bf16[128,1024]{1,0:T(8,128)(2,1)S(1)}, bf16[128,1024]{1,0:T(8,128)(2,1)S(1)}, u32[]{:S(2)}, u32[]{:S(2)}) collective-permute-start(bf16[128,1024]{1,0:T(8,128)(2,1)S(1)} %add_convert_fusion.6), channel_id=1, source_target_pairs={{0,1},{1,0},{2,3},{3,2},{4,5},{5,4},{6,7},{7,6},{8,9},{9,8},{10,11... | collective-permute-start | bytes 786440 | tf_op jit(solution)/shard_map/ppermute | solution.py:27
  92.9 0.2 add_convert_fusion.1
  93.0 0.7 collective-permute-start.25
  93.7 0.0 collective-permute-done.19
  93.7 4.8 %collective-permute-done.22 = bf16[128,1024]{1,0:T(8,128)(2,1)S(1)} collective-permute-done((bf16[128,1024]{1,0:T(8,128)(2,1)S(1)}, bf16[128,1024]{1,0:T(8,128)(2,1)S(1)}, u32[]{:S(2)}, u32[]{:S(2)}) %collective-permute-start.22) | collective-permute-done | bytes 262176 | tf_op jit(solution)/shard_map/ppermute | solution.py:27
  98.5 0.2 add_convert_fusion.2
  98.7 3.5 %collective-permute-start.23 = (bf16[128,2560]{1,0:T(8,128)(2,1)S(1)}, bf16[128,2560]{1,0:T(8,128)(2,1)S(1)}, u32[]{:S(2)}, u32[]{:S(2)}) collective-permute-start(bf16[128,2560]{1,0:T(8,128)(2,1)S(1)} %add_convert_fusion.2), channel_id=1, source_target_pairs={{0,1},{1,0},{2,3},{3,2},{4,5},{5,4},{6,7},{7,6},{8,9},{9,8},{10,11... | collective-permute-start | bytes 1966088 | tf_op jit(solution)/shard_map/ppermute | solution.py:27
  102.1 5.4 %gradient_late.1.refs_0_ = f32[2048,3584]{1,0:T(8,128)} custom-call(f32[2048,1536]{1,0:T(8,128)S(1)} %gradient_early.1.early, bf16[2048,512]{1,0:T(8,128)(2,1)S(1)} %transposed.1.q_t, bf16[128,3584]{1,0:T(8,128)(2,1)S(1)} %collective-permute-done.16.o2, bf16[128,3584]{1,0:T(8,128)(2,1)S(1)} %collective-permute-done.21.e3), custom_call_target="tpu_custom_call" | custom-call | flops 4831838208 | bytes 12582912 | tf_op jit(solution)/shard_map/gradient_late/pallas_call | solution.py:418
  107.6 8.1 %weight_gradient.1 = f32[2048,3584]{1,0:T(8,128)} custom-call(bf16[2048,512]{1,0:T(8,128)(2,1)S(1)} %transposed.1.q_t, bf16[128,3584]{1,0:T(8,128)(2,1)S(1)} %copy-done, bf16[128,3584]{1,0:T(8,128)(2,1)S(1)} %collective-permute-done.13.e1, bf16[128,3584]{1,0:T(8,128)(2,1)S(1)} %collective-permute-done.14.o1, ...), custom_call_target="tpu_custom_call", output_to_operand_aliasing={{}: (7, {})} | custom-call | flops 1 | bytes 1 | tf_op jit(solution)/shard_map/weight_gradient/pallas_call | solution.py:320
  115.7 0.1 add_convert_fusion.5
  115.9 0.2 add_convert_fusion
  116.1 1.0 pad_maximum_fusion
  (14 shorter events, 0.1 us)
Async XLA Ops:
  0.6 25.5 %copy-start = (bf16[128,3584]{1,0:T(8,128)(2,1)S(1)}, bf16[128,3584]{1,0:T(8,128)(2,1)}, u32[]{:S(2)}) copy-start(bf16[128,3584]{1,0:T(8,128)(2,1)} %own_ref.3) | copy-start | bytes 2752516
  0.6 1.0 copy-start.1
  1.7 0.7 copy-start.2
  2.4 6.0 %collective-permute-start = (bf16[16,2048]{1,0:T(8,128)(2,1)S(1)}, bf16[16,2048]{1,0:T(8,128)(2,1)S(1)}, u32[]{:S(2)}, u32[]{:S(2)}) collective-permute-start(bf16[16,2048]{1,0:T(8,128)(2,1)S(1)} %get-tuple-element.41), channel_id=1, source_target_pairs={{0,1},{1,0},{2,3},{3,2},{4,5},{5,4},{6,7},{7,6},{8,9},{9,8},{10,11... | collective-permute-start | bytes 196616 | tf_op jit(solution)/shard_map/ppermute | solution.py:27
  5.5 7.3 %collective-permute-start.1 = (bf16[16,2048]{1,0:T(8,128)(2,1)S(1)}, bf16[16,2048]{1,0:T(8,128)(2,1)S(1)}, u32[]{:S(2)}, u32[]{:S(2)}) collective-permute-start(bf16[16,2048]{1,0:T(8,128)(2,1)S(1)} %get-tuple-element.42), channel_id=1, source_target_pairs={{0,2},{1,3},{2,0},{3,1},{4,6},{5,7},{6,4},{7,5},{8,10},{9,11},{10,... | collective-permute-start | bytes 196616 | tf_op jit(solution)/shard_map/ppermute | solution.py:27
  8.1 6.1 %collective-permute-start.2 = (bf16[16,2048]{1,0:T(8,128)(2,1)S(1)}, bf16[16,2048]{1,0:T(8,128)(2,1)S(1)}, u32[]{:S(2)}, u32[]{:S(2)}) collective-permute-start(bf16[16,2048]{1,0:T(8,128)(2,1)S(1)} %get-tuple-element.43), channel_id=1, source_target_pairs={{0,3},{1,2},{2,1},{3,0},{4,7},{5,6},{6,5},{7,4},{8,11},{9,10},{10,... | collective-permute-start | bytes 196616 | tf_op jit(solution)/shard_map/ppermute | solution.py:27
  14.5 4.5 %collective-permute-start.3 = (bf16[16,2048]{1,0:T(8,128)(2,1)S(1)}, bf16[16,2048]{1,0:T(8,128)(2,1)S(1)}, u32[]{:S(2)}, u32[]{:S(2)}) collective-permute-start(bf16[16,2048]{1,0:T(8,128)(2,1)S(1)} %get-tuple-element.45), channel_id=1, source_target_pairs={{0,1},{1,0},{2,3},{3,2},{4,5},{5,4},{6,7},{7,6},{8,9},{9,8},{10,11... | collective-permute-start | bytes 196616 | tf_op jit(solution)/shard_map/ppermute | solution.py:27
  14.6 5.8 %collective-permute-start.4 = (bf16[16,2048]{1,0:T(8,128)(2,1)S(1)}, bf16[16,2048]{1,0:T(8,128)(2,1)S(1)}, u32[]{:S(2)}, u32[]{:S(2)}) collective-permute-start(bf16[16,2048]{1,0:T(8,128)(2,1)S(1)} %get-tuple-element.46), channel_id=1, source_target_pairs={{0,2},{1,3},{2,0},{3,1},{4,6},{5,7},{6,4},{7,5},{8,10},{9,11},{10,... | collective-permute-start | bytes 196616 | tf_op jit(solution)/shard_map/ppermute | solution.py:27
  16.9 6.1 %collective-permute-start.5 = (bf16[16,2048]{1,0:T(8,128)(2,1)S(1)}, bf16[16,2048]{1,0:T(8,128)(2,1)S(1)}, u32[]{:S(2)}, u32[]{:S(2)}) collective-permute-start(bf16[16,2048]{1,0:T(8,128)(2,1)S(1)} %get-tuple-element.47), channel_id=1, source_target_pairs={{0,3},{1,2},{2,1},{3,0},{4,7},{5,6},{6,5},{7,4},{8,11},{9,10},{10,... | collective-permute-start | bytes 196616 | tf_op jit(solution)/shard_map/ppermute | solution.py:27
  23.0 6.4 %collective-permute-start.8 = (bf16[64,2048]{1,0:T(8,128)(2,1)S(1)}, bf16[64,2048]{1,0:T(8,128)(2,1)S(1)}, u32[]{:S(2)}, u32[]{:S(2)}) collective-permute-start(bf16[64,2048]{1,0:T(8,128)(2,1)S(1)} %pad_maximum_fusion.1.refs_0_), channel_id=1, source_target_pairs={{0,16},{4,20},{8,24},{12,28},{16,0},{20,4},{24,8},{28,12},{1,17},{... | collective-permute-start | bytes 786440 | tf_op jit(solution)/shard_map/ppermute | solution.py:27
  24.6 6.4 %collective-permute-start.7 = (bf16[64,2048]{1,0:T(8,128)(2,1)S(1)}, bf16[64,2048]{1,0:T(8,128)(2,1)S(1)}, u32[]{:S(2)}, u32[]{:S(2)}) collective-permute-start(bf16[64,2048]{1,0:T(8,128)(2,1)S(1)} %pad_maximum_fusion.1.refs_0_), channel_id=1, source_target_pairs={{0,8},{4,12},{8,0},{12,4},{16,24},{20,28},{24,16},{28,20},{1,9},{5... | collective-permute-start | bytes 786440 | tf_op jit(solution)/shard_map/ppermute | solution.py:27
  26.1 17.3 %collective-permute-start.14 = (bf16[128,3584]{1,0:T(8,128)(2,1)S(1)}, bf16[128,3584]{1,0:T(8,128)(2,1)S(1)}, u32[]{:S(2)}, u32[]{:S(2)}) collective-permute-start(bf16[128,3584]{1,0:T(8,128)(2,1)S(1)} %copy-done), channel_id=1, source_target_pairs={{1,2},{2,1},{5,6},{6,5},{9,10},{10,9},{13,14},{14,13},{17,18},{18,... | collective-permute-start | bytes 2752520 | tf_op jit(solution)/shard_map/ppermute | solution.py:440
  26.8 19.6 %collective-permute-start.13 = (bf16[128,3584]{1,0:T(8,128)(2,1)S(1)}, bf16[128,3584]{1,0:T(8,128)(2,1)S(1)}, u32[]{:S(2)}, u32[]{:S(2)}) collective-permute-start(bf16[128,3584]{1,0:T(8,128)(2,1)S(1)} %copy-done), channel_id=1, source_target_pairs={{0,1},{1,0},{2,3},{3,2},{4,5},{5,4},{6,7},{7,6},{8,9},{9,8},{10,11... | collective-permute-start | bytes 2752520 | tf_op jit(solution)/shard_map/ppermute | solution.py:27
  29.0 2.6 %collective-permute-start.6 = (bf16[64,2048]{1,0:T(8,128)(2,1)S(1)}, bf16[64,2048]{1,0:T(8,128)(2,1)S(1)}, u32[]{:S(2)}, u32[]{:S(2)}) collective-permute-start(bf16[64,2048]{1,0:T(8,128)(2,1)S(1)} %pad_maximum_fusion.1.refs_0_), channel_id=1, source_target_pairs={{0,4},{4,0},{8,12},{12,8},{16,20},{20,16},{24,28},{28,24},{1,5},{5... | collective-permute-start | bytes 786440 | tf_op jit(solution)/shard_map/ppermute | solution.py:27
  31.0 6.4 %collective-permute-start.11 = (bf16[64,2048]{1,0:T(8,128)(2,1)S(1)}, bf16[64,2048]{1,0:T(8,128)(2,1)S(1)}, u32[]{:S(2)}, u32[]{:S(2)}) collective-permute-start(bf16[64,2048]{1,0:T(8,128)(2,1)S(1)} %broadcast_select_fusion), channel_id=1, source_target_pairs={{0,16},{4,12},{8,24},{12,4},{16,0},{20,28},{24,8},{28,20},{1,17},{... | collective-permute-start | bytes 786440 | tf_op jit(solution)/shard_map/ppermute | solution.py:162
  31.6 5.9 %collective-permute-start.9 = (bf16[64,2048]{1,0:T(8,128)(2,1)S(1)}, bf16[64,2048]{1,0:T(8,128)(2,1)S(1)}, u32[]{:S(2)}, u32[]{:S(2)}) collective-permute-start(bf16[64,2048]{1,0:T(8,128)(2,1)S(1)} %collective-permute-done.7.refs_2_), channel_id=1, source_target_pairs={{0,4},{4,0},{8,12},{12,8},{16,20},{20,16},{24,28},{28,24},{1,5},{5... | collective-permute-start | bytes 786440 | tf_op jit(solution)/shard_map/ppermute | solution.py:27
  31.6 5.9 %collective-permute-start.10 = (bf16[64,2048]{1,0:T(8,128)(2,1)S(1)}, bf16[64,2048]{1,0:T(8,128)(2,1)S(1)}, u32[]{:S(2)}, u32[]{:S(2)}) collective-permute-start(bf16[64,2048]{1,0:T(8,128)(2,1)S(1)} %collective-permute-done.8.refs_4_), channel_id=1, source_target_pairs={{0,4},{4,0},{8,12},{12,8},{16,20},{20,16},{24,28},{28,24},{1,5},{5... | collective-permute-start | bytes 786440 | tf_op jit(solution)/shard_map/ppermute | solution.py:27
  37.5 1.5 %collective-permute-start.12 = (bf16[64,2048]{1,0:T(8,128)(2,1)S(1)}, bf16[64,2048]{1,0:T(8,128)(2,1)S(1)}, u32[]{:S(2)}, u32[]{:S(2)}) collective-permute-start(bf16[64,2048]{1,0:T(8,128)(2,1)S(1)} %collective-permute-done.11.refs_6_), channel_id=1, source_target_pairs={{0,4},{4,0},{8,12},{12,8},{16,20},{20,16},{24,28},{28,24},{1,5},{5... | collective-permute-start | bytes 786440 | tf_op jit(solution)/shard_map/ppermute | solution.py:27
  46.4 17.3 %collective-permute-start.16 = (bf16[128,3584]{1,0:T(8,128)(2,1)S(1)}, bf16[128,3584]{1,0:T(8,128)(2,1)S(1)}, u32[]{:S(2)}, u32[]{:S(2)}) collective-permute-start(bf16[128,3584]{1,0:T(8,128)(2,1)S(1)} %collective-permute-done.13.e1), channel_id=1, source_target_pairs={{1,2},{2,1},{5,6},{6,5},{9,10},{10,9},{13,14},{14,13},{17,18},{18,... | collective-permute-start | bytes 2752520 | tf_op jit(solution)/shard_map/ppermute | solution.py:440
  47.1 21.4 %collective-permute-start.17 = (bf16[128,3584]{1,0:T(8,128)(2,1)S(1)}, bf16[128,3584]{1,0:T(8,128)(2,1)S(1)}, u32[]{:S(2)}, u32[]{:S(2)}) collective-permute-start(bf16[128,3584]{1,0:T(8,128)(2,1)S(1)} %collective-permute-done.14.o1), channel_id=1, source_target_pairs={{1,0},{2,3},{5,4},{6,7},{9,8},{10,11},{13,12},{14,15},{17,16},{18,... | collective-permute-start | bytes 2752520 | tf_op jit(solution)/shard_map/ppermute | solution.py:440
  48.4 15.2 %collective-permute-start.18 = (bf16[256,1024]{1,0:T(8,128)(2,1)S(1)}, bf16[256,1024]{1,0:T(8,128)(2,1)S(1)}, u32[]{:S(2)}, u32[]{:S(2)}) collective-permute-start(bf16[256,1024]{1,0:T(8,128)(2,1)S(1)} %get-tuple-element.57), channel_id=1, source_target_pairs={{0,1},{3,2},{4,5},{7,6},{8,9},{11,10},{12,13},{15,14},{16,17},{19,... | collective-permute-start | bytes 1572872 | tf_op jit(solution)/shard_map/ppermute | solution.py:440
  62.3 16.0 %collective-permute-start.15 = (bf16[128,2560]{1,0:T(8,128)(2,1)S(1)}, bf16[128,2560]{1,0:T(8,128)(2,1)S(1)}, u32[]{:S(2)}, u32[]{:S(2)}) collective-permute-start(bf16[128,2560]{1,0:T(8,128)(2,1)S(1)} %get-tuple-element.54), channel_id=1, source_target_pairs={{0,1},{3,2},{4,5},{7,6},{8,9},{11,10},{12,13},{15,14},{16,17},{19,... | collective-permute-start | bytes 1966088 | tf_op jit(solution)/shard_map/ppermute | solution.py:440
  68.5 21.8 %collective-permute-start.21 = (bf16[128,3584]{1,0:T(8,128)(2,1)S(1)}, bf16[128,3584]{1,0:T(8,128)(2,1)S(1)}, u32[]{:S(2)}, u32[]{:S(2)}) collective-permute-start(bf16[128,3584]{1,0:T(8,128)(2,1)S(1)} %collective-permute-done.16.o2), channel_id=1, source_target_pairs={{1,0},{2,3},{5,4},{6,7},{9,8},{10,11},{13,12},{14,15},{17,16},{18,... | collective-permute-start | bytes 2752520 | tf_op jit(solution)/shard_map/ppermute | solution.py:440
  70.0 20.3 %collective-permute-start.20 = (bf16[256,1024]{1,0:T(8,128)(2,1)S(1)}, bf16[256,1024]{1,0:T(8,128)(2,1)S(1)}, u32[]{:S(2)}, u32[]{:S(2)}) collective-permute-start(bf16[256,1024]{1,0:T(8,128)(2,1)S(1)} %add_convert_fusion.4), channel_id=1, source_target_pairs={{1,2},{2,1},{5,6},{6,5},{9,10},{10,9},{13,14},{14,13},{17,18},{18,... | collective-permute-start | bytes 1572872 | tf_op jit(solution)/shard_map/ppermute | solution.py:440
  70.7 19.6 %collective-permute-start.24 = (bf16[128,2560]{1,0:T(8,128)(2,1)S(1)}, bf16[128,2560]{1,0:T(8,128)(2,1)S(1)}, u32[]{:S(2)}, u32[]{:S(2)}) collective-permute-start(bf16[128,2560]{1,0:T(8,128)(2,1)S(1)} %get-tuple-element.68), channel_id=1, source_target_pairs={{0,1},{3,2},{4,5},{7,6},{8,9},{11,10},{12,13},{15,14},{16,17},{19,... | collective-permute-start | bytes 1966088 | tf_op jit(solution)/shard_map/ppermute | solution.py:440
  79.1 14.7 %collective-permute-start.19 = (bf16[128,2560]{1,0:T(8,128)(2,1)S(1)}, bf16[128,2560]{1,0:T(8,128)(2,1)S(1)}, u32[]{:S(2)}, u32[]{:S(2)}) collective-permute-start(bf16[128,2560]{1,0:T(8,128)(2,1)S(1)} %add_convert_fusion.3), channel_id=1, source_target_pairs={{1,2},{2,1},{5,6},{6,5},{9,10},{10,9},{13,14},{14,13},{17,18},{18,... | collective-permute-start | bytes 1966088 | tf_op jit(solution)/shard_map/ppermute | solution.py:440
  90.3 8.2 %collective-permute-start.22 = (bf16[128,1024]{1,0:T(8,128)(2,1)S(1)}, bf16[128,1024]{1,0:T(8,128)(2,1)S(1)}, u32[]{:S(2)}, u32[]{:S(2)}) collective-permute-start(bf16[128,1024]{1,0:T(8,128)(2,1)S(1)} %add_convert_fusion.6), channel_id=1, source_target_pairs={{0,1},{1,0},{2,3},{3,2},{4,5},{5,4},{6,7},{7,6},{8,9},{9,8},{10,11... | collective-permute-start | bytes 786440 | tf_op jit(solution)/shard_map/ppermute | solution.py:27
  93.0 22.8 %collective-permute-start.25 = (bf16[128,2560]{1,0:T(8,128)(2,1)S(1)}, bf16[128,2560]{1,0:T(8,128)(2,1)S(1)}, u32[]{:S(2)}, u32[]{:S(2)}) collective-permute-start(bf16[128,2560]{1,0:T(8,128)(2,1)S(1)} %add_convert_fusion.1), channel_id=1, source_target_pairs={{1,2},{2,1},{5,6},{6,5},{9,10},{10,9},{13,14},{14,13},{17,18},{18,... | collective-permute-start | bytes 1966088 | tf_op jit(solution)/shard_map/ppermute | solution.py:440
  98.7 17.2 %collective-permute-start.23 = (bf16[128,2560]{1,0:T(8,128)(2,1)S(1)}, bf16[128,2560]{1,0:T(8,128)(2,1)S(1)}, u32[]{:S(2)}, u32[]{:S(2)}) collective-permute-start(bf16[128,2560]{1,0:T(8,128)(2,1)S(1)} %add_convert_fusion.2), channel_id=1, source_target_pairs={{0,1},{1,0},{2,3},{3,2},{4,5},{5,4},{6,7},{7,6},{8,9},{9,8},{10,11... | collective-permute-start | bytes 1966088 | tf_op jit(solution)/shard_map/ppermute | solution.py:27
